TPU v7x, 512 devices: a whole 4x4x16 slice. The times are simulated.
512 devices in a mesh: normal: 4 (over z_lo), strike: 16 (over z_hi, y), depth: 8 (over x, core).
Axes of the slice: x: 4, y: 4, z: 16 (z_hi: 4, z_lo: 4; z = z_hi * 4 + z_lo), core: 2. Of those that a mesh axis runs over, the one named last changes fastest.
Arguments:
- field_now: float32 [3, 32, 256, 1024], P(None, 'normal', 'strike', 'depth'), may hold values from -6 to 6
- field_prev: float32 [3, 32, 256, 1024], P(None, 'normal', 'strike', 'depth'), may hold values from -6 to 6
- rigidity: bfloat16 [32, 256, 1024], P('normal', 'strike', 'depth'), may hold values from 1 to 2
- density: bfloat16 [32, 256, 1024], P('normal', 'strike', 'depth'), may hold values from 1 to 2
- fault_nodes: int32 [16, 8, 256], P('strike', 'depth'), may hold values from 0 to 2047, as said below
- patch_ids: int32 [16, 8, 256], P('strike', 'depth'), may hold values from 0 to 255, as said below
Outputs:
- field_next: float32 [3, 32, 256, 1024], P(None, 'normal', 'strike', 'depth')
- field_mid: float32 [3, 32, 256, 1024], P(None, 'normal', 'strike', 'depth')
- slip_gradient: float32 [256, 3], P(('strike', 'depth'))
Inputs may be any that keep to these rules, and one draw needn't show every extreme that they name: `fault_nodes`: within one block the 256 entries are distinct. `patch_ids`: every patch holds exactly 128 pairs over all blocks.
All inputs are finite; a program needn't handle non-finite values.
Results may differ from a plain program's by a relative error of at most 0.0003.
Values may be sent and summed in bfloat16 or wider, within the bound.
No kernel may reach another device: no remote copies, remote signals or barrier semaphores. Data moves between devices by JAX's collectives and lax.ppermute only.
A program may use at most 64 MiB of HBM per device.

v0:
```python
import math

import jax
import jax.numpy as jnp
import numpy as np
from jax import lax
from jax.sharding import PartitionSpec as P

PATCH_DEV = 2


DT = 0.03
HIGHEST_PRECISION = lax.Precision.HIGHEST
SPLIT_FORMS = ("ceayz,ba->cebyz", "cxeaz,ba->cxebz", "cxyea,ba->cxyeb")
BACK_FORMS = ("cebyz,ba->ceayz", "cxebz,ba->cxeaz", "cxyeb,ba->cxyea")


def extended(cells, sides, width):
    for axis, dim in sides:
        count = lax.axis_size(axis)
        ends = count - 1
        head = lax.slice_in_dim(cells, 0, width, axis=dim)
        tail = lax.slice_in_dim(cells, cells.shape[dim] - width, cells.shape[dim], axis=dim)
        cells = jnp.concatenate(
            [
                lax.ppermute(tail, axis, [(i, (i + 1) % count) for i in range(ends)]),
                cells,
                lax.ppermute(head, axis, [((i + 1) % count, i) for i in range(ends)]),
            ],
            axis=dim,
        )
    return cells


def from_root(value, axis, source):
    kept = jnp.where(lax.axis_index(axis) == source, value, 0).astype(value.dtype)
    return lax.psum(kept, axis)


def gll_tables():
    spread_point = math.sqrt(3.0 / 7.0)
    points = np.array([-1.0, -spread_point, 0.0, spread_point, 1.0])
    weights = np.array([0.1, 49.0 / 90.0, 32.0 / 45.0, 49.0 / 90.0, 0.1]) * 0.5
    derivative = np.zeros((5, 5))
    for row_index in range(5):
        for col_index in range(5):
            if row_index == col_index:
                derivative[row_index, col_index] = sum(
                    (
                        1.0 / (points[row_index] - points[other_index])
                        for other_index in range(5)
                        if other_index != row_index
                    )
                )
            else:
                row_product = np.prod(
                    [
                        points[row_index] - points[other_index]
                        for other_index in range(5)
                        if other_index != row_index
                    ]
                )
                col_product = np.prod(
                    [
                        points[col_index] - points[other_index]
                        for other_index in range(5)
                        if other_index != col_index
                    ]
                )
                derivative[row_index, col_index] = row_product / (
                    col_product * (points[row_index] - points[col_index])
                )
    return (weights, 2.0 * derivative)


def axis_weights(start, count, weights):
    positions = start + jnp.arange(count, dtype=jnp.int32)
    phase = positions % 4
    chosen = jnp.zeros((count,), jnp.float32)
    for slot_index in range(4):
        chosen = jnp.where(phase == slot_index, weights[slot_index], chosen)
    chosen = jnp.where(phase == 0, 2.0 * weights[0], chosen)
    return jnp.where(positions == 0, weights[0], chosen)


def along(vector, direction):
    shape_list = [1, 1, 1]
    shape_list[direction] = -1
    return vector.reshape(shape_list)


def element_split(values, axis):
    count_elems = (values.shape[axis] - 1) // 4
    head = lax.slice_in_dim(values, 0, 4 * count_elems, axis=axis)
    blocks = head.reshape(values.shape[:axis] + (count_elems, 4) + values.shape[axis + 1 :])
    closing = lax.slice_in_dim(values, 4, 4 * count_elems + 1, 4, axis=axis)
    return jnp.concatenate([blocks, jnp.expand_dims(closing, axis + 1)], axis=axis + 1)


def line_terms(values, rigid_part, direction, weights, derivative, first_node=None):
    elements = element_split(values, direction + 1)
    rigid_elems = element_split(rigid_part, direction)
    weight_shape = [1, 1, 1, 1]
    weight_shape[direction + 1] = 5
    point_scale = rigid_elems * weights.reshape(weight_shape)
    count_elems = rigid_elems.shape[direction]
    inside = first_node + 4 * jnp.arange(count_elems, dtype=jnp.int32) >= 0
    live_shape = [1, 1, 1, 1]
    live_shape[direction] = count_elems
    point_scale = point_scale * inside.astype(jnp.float32).reshape(live_shape)
    grads = jnp.einsum(SPLIT_FORMS[direction], elements, derivative, precision=HIGHEST_PRECISION)
    fluxes = grads * point_scale[None]
    return jnp.einsum(BACK_FORMS[direction], fluxes, derivative, precision=HIGHEST_PRECISION)


def assemble_line(terms, axis):
    count_elems = terms.shape[axis]
    heads = lax.slice_in_dim(terms, 0, 4, axis=axis + 1)
    closing = lax.slice_in_dim(terms, 4, 5, axis=axis + 1)
    filler_shape = list(closing.shape)
    filler_shape[axis + 1] = 3
    closing = jnp.concatenate([jnp.zeros(filler_shape, terms.dtype), closing], axis=axis + 1)
    merged_shape = terms.shape[:axis] + (4 * count_elems,) + terms.shape[axis + 2 :]
    head_pads = [(0, 0)] * len(merged_shape)
    close_pads = [(0, 0)] * len(merged_shape)
    head_pads[axis] = (0, 1)
    close_pads[axis] = (1, 0)
    return jnp.pad(heads.reshape(merged_shape), head_pads) + jnp.pad(
        closing.reshape(merged_shape), close_pads
    )


def box_force(values, rigid_box, offset, inner, box_start, weights, derivative):
    node_weight = [
        axis_weights(box_start[direction] + offset, inner[direction], weights)
        for direction in range(3)
    ]
    total = jnp.zeros((3,) + tuple(inner), jnp.float32)
    normal_terms = None
    for direction in range(3):
        cuts = [slice(offset, offset + inner[other]) for other in range(3)]
        cuts[direction] = slice(None)
        terms = line_terms(
            values[(slice(None),) + tuple(cuts)],
            rigid_box[tuple(cuts)],
            direction,
            weights,
            derivative,
            box_start[direction],
        )
        if direction == 0:
            normal_terms = terms
        nodes = lax.slice_in_dim(
            assemble_line(terms, direction + 1),
            offset,
            offset + inner[direction],
            axis=direction + 1,
        )
        first_other = (direction + 1) % 3
        second_other = (direction + 2) % 3
        scale = along(node_weight[first_other], first_other) * along(
            node_weight[second_other], second_other
        )
        total = total + nodes * scale[None]
    return (total, normal_terms)


def local(field_now, field_prev, rigidity, density, fault_nodes, patch_ids):
    weights_np, derivative_np = gll_tables()
    weights = jnp.asarray(weights_np, jnp.float32)
    derivative = jnp.asarray(derivative_np, jnp.float32)
    size_x, size_y, size_z = rigidity.shape
    base_x = lax.axis_index("normal") * size_x
    base_y = lax.axis_index("strike") * size_y
    base_z = lax.axis_index("depth") * size_z
    reach = 4
    material = extended(
        jnp.stack([rigidity, density]), (("normal", 1), ("strike", 2), ("depth", 3)), reach
    )
    rigid_wide = material[0].astype(jnp.float32)
    owned_x = axis_weights(base_x, size_x, weights)
    owned_y = axis_weights(base_y, size_y, weights)
    owned_z = axis_weights(base_z, size_z, weights)
    mass = density.astype(jnp.float32) * along(owned_x, 0) * along(owned_y, 1) * along(owned_z, 2)
    face_weight = owned_y[:, None] * owned_z[None, :]
    current, previous = (field_now, field_prev)
    traction_sum = jnp.zeros((3, size_y, size_z), jnp.float32)
    rigid_box = rigid_wide[: size_x + 5, : size_y + 5, : size_z + 5]
    starts = (base_x - 4, base_y - 4, base_z - 4)
    states = []
    for step_index in range(2):
        padded = extended(current, (("normal", 1), ("strike", 2), ("depth", 3)), 4)
        box_values = padded[:, : size_x + 5, : size_y + 5, : size_z + 5]
        force, normal_terms = box_force(
            box_values, rigid_box, 4, (size_x, size_y, size_z), starts, weights, derivative
        )
        traction_sum = (
            traction_sum + 0.5 * (normal_terms[:, 0, 4] - normal_terms[:, 1, 0]) * face_weight[None]
        )
        following = 2.0 * current - previous - DT * DT * force / mass
        previous, current = (current, following)
        states.append(current)
    field_mid = states[0]
    field_next = states[1]
    fault_side = lax.axis_index("normal") == lax.axis_size("normal") // 2
    picked = jnp.take(traction_sum.reshape(3, size_y * size_z), fault_nodes.reshape(-1), axis=1)
    picked = jnp.where(fault_side, picked, 0.0)
    node_patch = patch_ids.reshape(-1)
    hits = (
        node_patch[:, None]
        == jnp.arange(PATCH_DEV * lax.axis_size(("strike", "depth")), dtype=jnp.int32)[None, :]
    ).astype(jnp.float32)
    patch_share = lax.psum_scatter(
        jnp.einsum("fp,cf->pc", hits, picked, precision=HIGHEST_PRECISION),
        ("strike", "depth"),
        scatter_dimension=0,
        tiled=True,
    )
    patch_share = from_root(patch_share, "normal", lax.axis_size("normal") // 2)
    return (field_next, field_mid, patch_share)


def solution(mesh):
    placed = (
        P(None, "normal", "strike", "depth"),
        P(None, "normal", "strike", "depth"),
        P("normal", "strike", "depth"),
        P("normal", "strike", "depth"),
        P("strike", "depth", None),
        P("strike", "depth", None),
    )
    return jax.shard_map(
        local,
        mesh=mesh,
        in_specs=placed,
        out_specs=(
            P(None, "normal", "strike", "depth"),
            P(None, "normal", "strike", "depth"),
            P(("strike", "depth"), None),
        ),
        check_vma=False,
    )
```

profile of v0, /device:TPU:1, one launch (start us, length us, event | category | flops | bytes accessed | tf_op | source)
XLA Modules:
  0.0 967.7 jit_solution(6714639400137630692)
XLA Ops:
  1.6 4.4 collective-permute-start
  6.0 1.3 collective-permute-start.1
  9.4 4.8 collective-permute-start.2
  21.1 1.3 collective-permute-start.5
  22.4 4.0 collective-permute-start.4
  28.4 7.2 collective-permute-start.7
  35.6 1.9 collective-permute-start.6
  44.5 4.6 collective-permute-start.8
  53.7 2.1 collective-permute-start.11
  56.8 4.7 collective-permute-start.10
  67.5 2.6 slice.346
  71.3 1.7 copy.240
  73.0 2.7 fusion
  75.7 1.5 fusion.10
  79.9 1.6 copy.250
  81.5 2.1 copy.247
  84.7 1.4 fusion.51
  87.4 4.3 collective-permute-start.12
  91.8 1.6 collective-permute-done.12
  95.3 4.5 collective-permute-start.14
  102.7 1.4 copy.276
  104.0 1.9 gather_fusion
  106.5 808.4 %all-reduce.18 = f32[256,3]{1,0:T(8,128)S(1)} all-reduce(f32[256,3]{1,0:T(8,128)S(1)} %fusion.31), channel_id=2, replica_groups=mesh['normal'=4,'strike'=16,'depth'=8] {'strike','depth'}, use_global_device_ids=true, to_apply=%region_0.1.clone | all-reduce | flops 768 | bytes 6144
  914.9 11.1 %psum.7 = f32[2,3]{1,0:T(2,128)} all-reduce(f32[2,3]{1,0:T(2,128)S(1)} %dynamic-slice_select_fusion), channel_id=1, replica_groups=mesh['normal'=4,'strike'=16,'depth'=8] {'normal'}, use_global_device_ids=true, to_apply=%region_1.2 | all-reduce | flops 6 | bytes 48 | tf_op jit(solution)/shard_map/psum | solution.py:37
  928.4 14.4 %collective-permute-start.17 = (f32[3,16,24,4]{2,1,3,0:T(8,128)S(1)}, f32[3,16,24,4]{2,1,3,0:T(8,128)}, u32[]{:S(2)}, u32[]{:S(2)}) collective-permute-start(f32[3,16,24,4]{2,1,3,0:T(8,128)S(1)} %copy.266), channel_id=1, source_target_pairs={{1,0},{2,1},{3,2},{4,3},{5,4},{6,5},{7,6},{9,8},{10,9},{11,10},{12... | collective-permute-start | bytes 55304 | tf_op jit(solution)/shard_map/ppermute | solution.py:28
  943.8 1.9 collective-permute-start.16
  951.8 2.0 slice.372
  955.0 1.7 copy.269
  956.6 1.8 fusion.4
  958.5 1.5 fusion.8
  962.6 2.1 copy.272
  965.8 1.9 fusion.43
  (197 shorter events, 54.8 us)
Async XLA Ops:
  0.6 39.5 %copy-start.13 = (bf16[8,16,128]{2,1,0:T(8,128)(2,1)S(1)}, bf16[8,16,128]{2,1,0:T(8,128)(2,1)}, u32[]{:S(2)}) copy-start(bf16[8,16,128]{2,1,0:T(8,128)(2,1)} %param.10) | copy-start | bytes 98308
  0.6 39.5 %copy-start.7 = (bf16[8,16,128]{2,1,0:T(8,128)(2,1)S(1)}, bf16[8,16,128]{2,1,0:T(8,128)(2,1)}, u32[]{:S(2)}) copy-start(bf16[8,16,128]{2,1,0:T(8,128)(2,1)} %param.11) | copy-start | bytes 98308
  1.6 41.2 %collective-permute-start = (f32[3,4,16,128]{3,2,1,0:T(8,128)S(1)}, f32[3,4,16,128]{3,2,1,0:T(8,128)S(1)}, u32[]{:S(2)}, u32[]{:S(2)}) collective-permute-start(f32[3,4,16,128]{3,2,1,0:T(8,128)S(1)} %get-tuple-element.16), channel_id=1, source_target_pairs={{0,128},{128,256},{256,384},{1,129},{129,257},{257,385},{2,130},{1... | collective-permute-start | bytes 294920 | tf_op jit(solution)/shard_map/ppermute | solution.py:26
  6.0 37.1 %collective-permute-start.1 = (f32[3,4,16,128]{3,2,1,0:T(8,128)S(1)}, f32[3,4,16,128]{3,2,1,0:T(8,128)S(1)}, u32[]{:S(2)}, u32[]{:S(2)}) collective-permute-start(f32[3,4,16,128]{3,2,1,0:T(8,128)S(1)} %get-tuple-element.15), channel_id=1, source_target_pairs={{128,0},{256,128},{384,256},{129,1},{257,129},{385,257},{130,2},{2... | collective-permute-start | bytes 294920 | tf_op jit(solution)/shard_map/ppermute | solution.py:28
  8.1 12.1 %collective-permute-start.3 = (bf16[2,4,16,128]{3,2,1,0:T(8,128)(2,1)S(1)}, bf16[2,4,16,128]{3,2,1,0:T(8,128)(2,1)S(1)}, u32[]{:S(2)}, u32[]{:S(2)}) collective-permute-start(bf16[2,4,16,128]{3,2,1,0:T(8,128)(2,1)S(1)} %get-tuple-element.20), channel_id=1, source_target_pairs={{128,0},{256,128},{384,256},{129,1},{257,129},{385,257},{130,2},{2... | collective-permute-start | bytes 98312 | tf_op jit(solution)/shard_map/ppermute | solution.py:28
  9.4 10.9 %collective-permute-start.2 = (bf16[2,4,16,128]{3,2,1,0:T(8,128)(2,1)S(1)}, bf16[2,4,16,128]{3,2,1,0:T(8,128)(2,1)S(1)}, u32[]{:S(2)}, u32[]{:S(2)}) collective-permute-start(bf16[2,4,16,128]{3,2,1,0:T(8,128)(2,1)S(1)} %get-tuple-element.19), channel_id=1, source_target_pairs={{0,128},{128,256},{256,384},{1,129},{129,257},{257,385},{2,130},{1... | collective-permute-start | bytes 98312 | tf_op jit(solution)/shard_map/ppermute | solution.py:26
  15.8 68.8 %copy-start.8 = (f32[8,16,128]{2,1,0:T(8,128)}, f32[8,16,128]{2,1,0:T(8,128)S(1)}, u32[]{:S(2)}) copy-start(f32[8,16,128]{2,1,0:T(8,128)S(1)} %multiply_multiply_fusion) | copy-start | bytes 196612
  21.1 5.3 collective-permute-start.5
  22.4 5.0 collective-permute-start.4
  28.4 11.1 %collective-permute-start.7 = (bf16[2,16,24,4]{3,2,1,0:T(8,128)(2,1)S(1)}, bf16[2,16,24,4]{3,2,1,0:T(8,128)(2,1)S(1)}, u32[]{:S(2)}, u32[]{:S(2)}) collective-permute-start(bf16[2,16,24,4]{3,2,1,0:T(8,128)(2,1)S(1)} %get-tuple-element.14), channel_id=1, source_target_pairs={{1,0},{2,1},{3,2},{4,3},{5,4},{6,5},{7,6},{9,8},{10,9},{11,10},{12... | collective-permute-start | bytes 18440 | tf_op jit(solution)/shard_map/ppermute | solution.py:28
  35.6 4.5 collective-permute-start.6
  40.3 1.9 copy-start.18
  42.8 6.5 copy-start.10
  43.2 9.1 collective-permute-start.9
  44.5 7.8 collective-permute-start.8
  50.7 1.7 copy-start.3
  53.7 11.1 %collective-permute-start.11 = (f32[3,16,24,4]{2,1,3,0:T(8,128)}, f32[3,16,24,4]{2,1,3,0:T(8,128)}, u32[]{:S(2)}, u32[]{:S(2)}) collective-permute-start(f32[3,16,24,4]{2,1,3,0:T(8,128)} %copy.237), channel_id=1, source_target_pairs={{1,0},{2,1},{3,2},{4,3},{5,4},{6,5},{7,6},{9,8},{10,9},{11,10},{12... | collective-permute-start | bytes 55304 | tf_op jit(solution)/shard_map/ppermute | solution.py:28
  56.8 9.2 collective-permute-start.10
  73.0 2.8 copy-start.11
  84.5 7.2 copy-start.19
  86.1 879.5 %copy-start = (f32[3,8,16,128]{3,2,1,0:T(8,128)}, f32[3,8,16,128]{3,2,1,0:T(8,128)S(1)}, u32[]{:S(2)}) copy-start(f32[3,8,16,128]{3,2,1,0:T(8,128)S(1)} %fusion.51) | copy-start | bytes 589828
  86.1 5.6 collective-permute-start.13
  87.4 5.9 collective-permute-start.12
  91.7 8.3 copy-start.12
  94.0 833.6 %collective-permute-start.15 = (f32[3,16,4,128]{3,2,1,0:T(4,128)}, f32[3,16,4,128]{3,2,1,0:T(4,128)S(1)}, u32[]{:S(2)}, u32[]{:S(2)}) collective-permute-start(f32[3,16,4,128]{3,2,1,0:T(4,128)} %get-tuple-element.8), channel_id=1, source_target_pairs={{8,0},{16,8},{24,16},{32,24},{40,32},{48,40},{56,48},{64,56},{72,6... | collective-permute-start | bytes 294920 | tf_op jit(solution)/shard_map/ppermute | solution.py:28
  95.3 832.3 %collective-permute-start.14 = (f32[3,16,4,128]{3,2,1,0:T(4,128)}, f32[3,16,4,128]{3,2,1,0:T(4,128)S(1)}, u32[]{:S(2)}, u32[]{:S(2)}) collective-permute-start(f32[3,16,4,128]{3,2,1,0:T(4,128)} %get-tuple-element.7), channel_id=1, source_target_pairs={{0,8},{8,16},{16,24},{24,32},{32,40},{40,48},{48,56},{56,64},{64,7... | collective-permute-start | bytes 294920 | tf_op jit(solution)/shard_map/ppermute | solution.py:26
  99.9 2.7 copy-start.17
  100.1 5.9 copy-start.20
  100.1 5.9 copy-start.21
  928.4 20.7 %collective-permute-start.17 = (f32[3,16,24,4]{2,1,3,0:T(8,128)S(1)}, f32[3,16,24,4]{2,1,3,0:T(8,128)}, u32[]{:S(2)}, u32[]{:S(2)}) collective-permute-start(f32[3,16,24,4]{2,1,3,0:T(8,128)S(1)} %copy.266), channel_id=1, source_target_pairs={{1,0},{2,1},{3,2},{4,3},{5,4},{6,5},{7,6},{9,8},{10,9},{11,10},{12... | collective-permute-start | bytes 55304 | tf_op jit(solution)/shard_map/ppermute | solution.py:28
  943.8 6.5 collective-permute-start.16
  960.0 1.2 copy-start.2
  (9 other events, 9.2 us)
where the time goes:
time: 973 us; the launch traced here: 968 us
  blocking collectives  819 us (84%)
  starting transfers between devices  66.5 us (7%)
  local copies, waits for them, and re-layouts  47.4 us (5%)
  other arithmetic  15.4 us (2%)
  matrix products  13.3 us (1%)
    unnamed x1, blocking collectives  808 us
    ppermute x9, starting transfers between devices, extended(): lax.ppermute(tail, axis, [(i, (i + 1) % count) for i in range(ends)])  35 us
    ppermute x9, starting transfers between devices, extended(): lax.ppermute(head, axis, [((i + 1) % count, i) for i in range(ends)])  31.5 us
  transfers between devices with their start and end apart: 18, of which 3 were waited for; matrix products, arithmetic and copies ran while one was open for 4% of the time, Pallas kernels for 0%

commit v1 on v0

v1 whole, which is shorter than its diff:
```python
import functools
import math

import jax
import jax.numpy as jnp
import numpy as np
from jax import lax
from jax.experimental import pallas as pl
from jax.experimental.pallas import tpu as pltpu
from jax.sharding import PartitionSpec as P

DT = 0.03
NXL, NYL, NZL = 8, 16, 128
ROWS = NXL * NYL
F32 = jnp.float32
HIGHEST = lax.Precision.HIGHEST


def gll_tables():
    spread = math.sqrt(3.0 / 7.0)
    points = np.array([-1.0, -spread, 0.0, spread, 1.0])
    weights = np.array([0.1, 49.0 / 90.0, 32.0 / 45.0, 49.0 / 90.0, 0.1]) * 0.5
    derivative = np.zeros((5, 5))
    for b in range(5):
        for a in range(5):
            if a == b:
                derivative[b, a] = sum(1.0 / (points[b] - points[o]) for o in range(5) if o != b)
            else:
                row = np.prod([points[b] - points[o] for o in range(5) if o != b and o != a])
                col = np.prod([points[a] - points[o] for o in range(5) if o != a and o != b])
                derivative[b, a] = row / (col * (points[a] - points[b]))
    return weights, 2.0 * derivative


WQ, D = gll_tables()
W0 = float(WQ[0])
NODE_W = np.array([2 * WQ[0], WQ[1], WQ[2], WQ[3], 2 * WQ[0]])
E = (WQ[:, None] * D).T / NODE_W[:, None]
KAPPA = float(E[4, 4])


def total(pairs):
    acc = None
    for const, arr in pairs:
        if abs(const) < 1e-12:
            continue
        term = arr * np.float32(const)
        acc = term if acc is None else acc + term
    return acc


def element(v, r):
    twice = v[2] + v[2]
    s0, s1 = v[0] + v[4] - twice, v[1] + v[3] - twice
    d0, d1 = v[0] - v[4], v[1] - v[3]
    ev = [total([((D[b, 0] + D[b, 4]) / 2, s0), ((D[b, 1] + D[b, 3]) / 2, s1)]) for b in (0, 1)]
    od = [total([((D[b, 0] - D[b, 4]) / 2, d0), ((D[b, 1] - D[b, 3]) / 2, d1)]) for b in (0, 1)]
    g2 = total([(D[2, 0], d0), (D[2, 1], d1)])
    q = [r[0] * (od[0] + ev[0]), r[1] * (od[1] + ev[1]), r[2] * g2, r[3] * (od[1] - ev[1]), r[4] * (od[0] - ev[0])]
    p0, m0, p1, m1 = q[0] + q[4], q[0] - q[4], q[1] + q[3], q[1] - q[3]
    ec = [total([((E[a, 0] + E[a, 4]) / 2, p0), ((E[a, 1] + E[a, 3]) / 2, p1), (E[a, 2], q[2])]) for a in (0, 1)]
    oc = [total([((E[a, 0] - E[a, 4]) / 2, m0), ((E[a, 1] - E[a, 3]) / 2, m1)]) for a in (0, 1)]
    c2 = total([(E[2, 0], m0), (E[2, 1], m1)])
    return [oc[0] + ec[0], oc[1] + ec[1], c2, oc[1] - ec[1], oc[0] - ec[0]]


def first_term(v, r):
    twice = v[2] + v[2]
    s0, s1 = v[0] + v[4] - twice, v[1] + v[3] - twice
    d0, d1 = v[0] - v[4], v[1] - v[3]
    ev = [total([((D[b, 0] + D[b, 4]) / 2, s0), ((D[b, 1] + D[b, 3]) / 2, s1)]) for b in (0, 1)]
    od = [total([((D[b, 0] - D[b, 4]) / 2, d0), ((D[b, 1] - D[b, 3]) / 2, d1)]) for b in (0, 1)]
    g2 = total([(D[2, 0], d0), (D[2, 1], d1)])
    q = [r[0] * (od[0] + ev[0]), r[1] * (od[1] + ev[1]), r[2] * g2, r[3] * (od[1] - ev[1]), r[4] * (od[0] - ev[0])]
    return total([(E[0, b], q[b]) for b in range(5)])


def open_terms(v, r):
    flux = [r[b] * total([(D[b, a], v[a]) for a in range(4)]) for b in range(4)]
    part = total([(E[4, b], flux[b]) for b in range(4)])
    grad = total([(D[4, a], v[a]) for a in range(4)])
    return part, grad


def open_scale(r):
    return total([(E[4, b] * D[b, 4], r[b]) for b in range(4)])


def rolled(x, shift):
    shift = shift % NZL
    return x if shift == 0 else pltpu.roll(x, shift, 1)


def lane_of():
    return lax.broadcasted_iota(jnp.int32, (8, NZL), 1)


def lane_table(phase, values):
    out = jnp.full((8, NZL), np.float32(values[0]), F32)
    for b in range(1, 4):
        out = jnp.where(phase == b, np.float32(values[b]), out)
    return out


def x_rows(x, half):
    return pl.ds(x * NYL + half * 8, 8)


def y_rows(y):
    return pl.ds(y, 8, stride=NYL)


def first_lanes(read, read_r, lane):
    out = jnp.zeros((8, NZL), F32)
    for k in range(16):
        rows = pl.ds(8 * k, 8)
        for c in range(3 if read_r is None else 4):
            src = read_r(rows) if c == 3 else read(c, rows)
            out = jnp.where(lane == 4 * k + c, rolled(src, 4 * k + c), out)
    return out


def last_lanes(read, lane):
    out = jnp.zeros((8, NZL), F32)
    for k in range(16):
        out = jnp.where((lane >> 2) == k, rolled(read(pl.ds(8 * k, 8)), 4 * k + 4), out)
    return out


def interleaved(parts, lane, base):
    out = jnp.zeros((8, NZL), F32)
    for j, part in enumerate(parts):
        if part is None:
            continue
        out = jnp.where((lane >= base) & (lane < base + 64) & ((lane & 3) == j), rolled(part, base + j - 3), out)
    return out


def widen(src, dst):
    for x in range(NXL):
        dst[pl.ds(x * NYL, NYL), :] = src[pl.ds(x * NYL, NYL), :].astype(F32)


def pack_kernel(now, rig, xu, xd, yu, yd, zu, zd, rw):
    widen(rig, rw)
    lane = lane_of()
    for half in range(2):
        r = [rw[x_rows(4 + a, half), :] for a in range(4)]
        xu[pl.ds(96 + 8 * half, 8), :] = open_scale(r)
        xd[pl.ds(48 + 8 * half, 8), :] = rw[x_rows(0, half), :]
        for c in range(3):
            part, grad = open_terms([now[c, x_rows(4 + a, half), :] for a in range(4)], r)
            xu[pl.ds(16 * c + 8 * half, 8), :] = part
            xu[pl.ds(48 + 16 * c + 8 * half, 8), :] = grad
            xd[pl.ds(16 * c + 8 * half, 8), :] = now[c, x_rows(0, half), :]
    r = [rw[y_rows(12 + a), :] for a in range(4)]
    yu[pl.ds(48, 8), :] = open_scale(r)
    yd[pl.ds(24, 8), :] = rw[y_rows(0), :]
    for c in range(3):
        part, grad = open_terms([now[c, y_rows(12 + a), :] for a in range(4)], r)
        yu[pl.ds(8 * c, 8), :] = part
        yu[pl.ds(24 + 8 * c, 8), :] = grad
        yd[pl.ds(8 * c, 8), :] = now[c, y_rows(0), :]
    back = lambda t: [rolled(t, 3 - a) for a in range(4)]
    r = back(last_lanes(lambda rows: rw[rows, :], lane))
    parts, grads = [], []
    for c in range(3):
        part, grad = open_terms(back(last_lanes(lambda rows: now[c, rows, :], lane)), r)
        parts.append(part)
        grads.append(grad)
    zu[...] = jnp.where(
        lane < 64, interleaved(parts + [open_scale(r)], lane, 0), interleaved(grads + [None], lane, 64)
    )
    zd[...] = first_lanes(lambda c, rows: now[c, rows, :], lambda rows: rw[rows, :], lane)


def from_fourth(tile, lane):
    phase = lane & 3
    out = tile
    for j in range(3):
        out = jnp.where(phase == j, rolled(tile, j - 3), out)
    return out


def advance(now, prev, rw, low, high_v, high_r, scale, ghost_z, ghost_rz, closing_z, index, store, acc, on_first):
    index_x, index_y, index_z = index
    at_x = jnp.where(index_x == 0, 2.0, 1.0).astype(F32)
    at_y = jnp.where(index_y == 0, 2.0, 1.0).astype(F32)
    at_z = jnp.where(index_z == 0, 2.0, 1.0).astype(F32)

    def along_y(c, carry):
        v = [now[c, y_rows(y), :] for y in range(NYL)] + [high_v[1][pl.ds(8 * c, 8), :]]
        r = [rw[y_rows(y), :] for y in range(NYL)] + [high_r[1][...]]
        carried = low[1](c, v[0])
        for e in range(4):
            terms = element(v[4 * e : 4 * e + 5], r[4 * e : 4 * e + 5])
            head = terms[0] * at_y if e == 0 else terms[0]
            acc[c, y_rows(4 * e), :] = head + carried
            for a in range(1, 4):
                acc[c, y_rows(4 * e + a), :] = terms[a]
            carried = terms[4]
        return carry

    lax.fori_loop(0, 3, along_y, 0)

    lane = lane_of()
    phase = lane & 3
    gm = [lane_table(phase, [D[b, b - k] if b >= k else 0 for b in range(4)]) for k in range(4)]
    gp = [None] + [lane_table(phase, [D[b, b + k] if b + k <= 4 else 0 for b in range(4)]) for k in range(1, 5)]
    cm = [lane_table(phase, [E[a, a - k] if a >= k else 0 for a in range(4)]) for k in range(4)]
    cp = [None] + [lane_table(phase, [E[a, a + k] if a + k <= 3 else 0 for a in range(4)]) for k in range(1, 4)]
    c_close = lane_table(phase, [E[a, 4] for a in range(4)])
    last = [lane_table(phase, [0, 0, 0, E[4, b]]) for b in range(5)]
    first = lane == 0
    edge = jnp.where(first, at_z, jnp.float32(1.0))

    def along_xz(n, carry):
        c, half = n >> 1, n & 1
        offset = half * 8
        rows = [pl.ds(pl.multiple_of(x * NYL + offset, 8), 8) for x in range(NXL)]
        plane = pl.ds(pl.multiple_of(16 * c + offset, 8), 8)
        v = [now[c, rows[x], :] for x in range(NXL)] + [high_v[0][plane, :]]
        r = [rw[rows[x], :] for x in range(NXL)] + [high_r[0][pl.ds(pl.multiple_of(offset, 8), 8), :]]
        carried = low[0](c, offset, plane, v[0])
        back = NZL - (4 * half + c)
        ghost_v = pltpu.roll(ghost_z, back, 1)
        ghost_r = pltpu.roll(ghost_rz, NZL - 4 * half, 1)
        closing = pltpu.roll(closing_z, back, 1)
        for e in range(2):
            terms = element(v[4 * e : 4 * e + 5], r[4 * e : 4 * e + 5])
            if e == 0:
                on_first(c, plane, carried, terms[0])
            for a in range(4):
                x = 4 * e + a
                force = terms[a] + acc[c, rows[x], :]
                if a == 0:
                    force = (terms[0] * at_x if e == 0 else terms[0]) + carried + acc[c, rows[x], :]
                vx = jnp.where(first, rolled(ghost_v, -8 * x), v[x])
                rx = jnp.where(first, rolled(ghost_r, -8 * x), r[x])
                vm = [v[x]] + [rolled(v[x], k) for k in range(1, 4)]
                vp = [None] + [rolled(vx, -k) for k in range(1, 5)]
                g = gm[0] * v[x]
                for k in range(1, 4):
                    g = g + gm[k] * vm[k]
                for k in range(1, 5):
                    g = g + gp[k] * vp[k]
                g4 = total([(D[4, 0], vm[3]), (D[4, 1], vm[2]), (D[4, 2], vm[1]), (D[4, 3], vm[0]), (D[4, 4], vp[1])])
                q = r[x] * g
                q4 = jnp.where(phase == 3, rolled(rx, -1) * g4, 0.0)
                qm = [q] + [rolled(q, k) for k in range(1, 4)]
                own = cm[0] * q
                for k in range(1, 4):
                    own = own + cm[k] * qm[k]
                for k in range(1, 4):
                    own = own + cp[k] * rolled(q, -k)
                pair = q4 + rolled(q4, -1)
                own = own + c_close * (pair + rolled(pair, -2))
                tail = last[3] * q + last[4] * q4
                for b in range(3):
                    tail = tail + last[b] * qm[3 - b]
                tail = jnp.where(first, rolled(closing, -8 * x), rolled(tail, 1))
                force = force + own * edge + tail
                after = (v[x] + v[x]) - prev[c, rows[x], :] - scale[rows[x], :] * force
                store(c, x, rows[x], plane, after)
            carried = terms[4]
        return carry

    lax.fori_loop(0, 6, along_xz, 0)


def step_scale(rho, scale):
    for x in range(NXL):
        rows = pl.ds(x * NYL, NYL)
        scale[rows, :] = np.float32(DT * DT) / rho[rows, :].astype(F32)


def axis_weight(pos, is_first):
    phase = pos & 3
    out = jnp.full(pos.shape, np.float32(2 * W0), F32)
    for b in range(1, 4):
        out = jnp.where(phase == b, np.float32(WQ[b]), out)
    return jnp.where((pos == 0) & is_first, np.float32(W0), out)


def first_kernel(
    middle, now, prev, rig, rho, xu, xd, yu, yd, zu, zd, zd_own,
    out, xu2, xd2, yu2, yd2, zu2, zd2, mx, my, mz, slip,
    rw, scale, acc, early,
):
    index = (lax.axis_index("normal"), lax.axis_index("strike"), lax.axis_index("depth"))
    widen(rig, rw)
    step_scale(rho, scale)
    lane = lane_of()
    has = [(i > 0).astype(F32) for i in index]
    for half in range(2):
        rows = pl.ds(8 * half, 8)
        mx[rows, :] = (xu[pl.ds(96 + 8 * half, 8), :] + np.float32(KAPPA * D[4, 4]) * rw[x_rows(0, half), :]) * has[0]
    my[...] = (yu[pl.ds(48, 8), :] + np.float32(KAPPA * D[4, 4]) * rw[y_rows(0), :]) * has[1]
    own, above = zd_own[...], zu[...]
    r_first = from_fourth(own, lane)
    scale_z = (from_fourth(above, lane) + np.float32(KAPPA * D[4, 4]) * r_first) * has[2]
    mz[...] = scale_z
    closing_z = above + np.float32(KAPPA) * r_first * rolled(above, 64) + scale_z * own
    kappa = np.float32(KAPPA)

    def low_x(c, offset, plane, v0):
        rows = pl.ds(pl.multiple_of(offset, 8), 8)
        grad = xu[pl.ds(pl.multiple_of(48 + 16 * c + offset, 8), 8), :]
        return xu[plane, :] + kappa * rw[rows, :] * grad + mx[rows, :] * v0

    def low_y(c, v0):
        grad = yu[pl.ds(pl.multiple_of(24 + 8 * c, 8), 8), :]
        return yu[pl.ds(pl.multiple_of(8 * c, 8), 8), :] + kappa * rw[y_rows(0), :] * grad + my[...] * v0

    def store(c, x, rows, plane, after):
        out[c, rows, :] = after
        if x == 0:
            xd2[plane, :] = after

    def on_first(c, plane, carried, term):
        early[plane, :] = carried - term

    below = zd[...]
    advance(
        now, prev, rw, (low_x, low_y), (xd, yd), (xd.at[pl.ds(48, 16)], yd.at[pl.ds(24, 8)]), scale,
        below, rolled(below, -3), closing_z, index, store, acc, on_first,
    )

    on_one, on_two = index[0] == middle - 1, index[0] == middle
    for half in range(2):
        rows = pl.ds(8 * half, 8)
        r = [rw[x_rows(x, half), :] for x in range(8)] + [xd[pl.ds(48 + 8 * half, 8), :]]
        y_pos = lax.broadcasted_iota(jnp.int32, (8, NZL), 0) + 8 * half
        face = axis_weight(y_pos, index[1] == 0) * axis_weight(lane, index[2] == 0) * np.float32(W0)
        for c in range(3):
            plane = pl.ds(16 * c + 8 * half, 8)
            v = [out[c, x_rows(x, half), :] for x in range(8)]
            part, grad = open_terms(v[4:], r[4:8])
            sent = part + kappa * r[8] * grad
            xu2[plane, :] = sent
            here = early[plane, :] + mx[rows, :] * v[0] - first_term(v[:5], r[:5])
            slip[plane, :] = face * jnp.where(on_one, sent, jnp.where(on_two, here, 0.0))
    r = [rw[y_rows(12 + a), :] for a in range(4)]
    for c in range(3):
        part, grad = open_terms([out[c, y_rows(12 + a), :] for a in range(4)], r)
        yu2[pl.ds(8 * c, 8), :] = part + kappa * yd[pl.ds(24, 8), :] * grad
        yd2[pl.ds(8 * c, 8), :] = out[c, y_rows(0), :]
    back = lambda t: [rolled(t, 3 - a) for a in range(4)]
    r = back(last_lanes(lambda rows: rw[rows, :], lane))
    sent = []
    for c in range(3):
        part, grad = open_terms(back(last_lanes(lambda rows: out[c, rows, :], lane)), r)
        sent.append(part + kappa * below * grad)
    zu2[...] = interleaved(sent + [None], lane, 0)
    zd2[...] = first_lanes(lambda c, rows: out[c, rows, :], None, lane)


def second_kernel(
    now, prev, rig, rho, xu2, xd2, yu2, yd2, zu2, zd2, zd2_own, mx, my, mz, xd, yd, zd,
    out, rw, scale, acc,
):
    index = (lax.axis_index("normal"), lax.axis_index("strike"), lax.axis_index("depth"))
    widen(rig, rw)
    step_scale(rho, scale)
    closing_z = zu2[...] + mz[...] * zd2_own[...]

    def low_x(c, offset, plane, v0):
        return xu2[plane, :] + mx[pl.ds(pl.multiple_of(offset, 8), 8), :] * v0

    def low_y(c, v0):
        return yu2[pl.ds(pl.multiple_of(8 * c, 8), 8), :] + my[...] * v0

    def store(c, x, rows, plane, after):
        out[c, rows, :] = after

    advance(
        now, prev, rw, (low_x, low_y), (xd2, yd2), (xd.at[pl.ds(48, 16)], yd.at[pl.ds(24, 8)]), scale,
        zd2[...], rolled(zd[...], -3), closing_z, index, store, acc, lambda *args: None,
    )


def patch_kernel(copies, count_d, count_s, slip, nodes, ids, out):
    pairs = nodes.shape[-1]
    node = nodes[...]
    hot_z = (lax.broadcasted_iota(jnp.int32, (NZL, pairs), 0) == (node & (NZL - 1))).astype(F32)
    at_z = jnp.dot(slip[...], hot_z, precision=HIGHEST, preferred_element_type=F32)
    row_y = lax.broadcasted_iota(jnp.int32, (NYL, pairs), 0) == (node >> 7)
    patch = ids[...]
    owner = patch >> 1
    owner_d = owner & (count_d - 1)
    slot = ((owner >> (count_d.bit_length() - 1)) << 1) + (patch & 1)
    hot_slot = lax.broadcasted_iota(jnp.int32, (32, pairs), 0) == slot
    spread = []
    for c in range(3):
        picked = jnp.sum(jnp.where(row_y, at_z[NYL * c : NYL * (c + 1), :], 0.0), axis=0, keepdims=True)
        spread.append(jnp.where(hot_slot, picked, 0.0))
    spread.append(jnp.zeros((32, pairs), F32))
    hot_d = (lax.broadcasted_iota(jnp.int32, (8, pairs), 0) == owner_d).astype(F32)
    tile = lax.dot_general(
        hot_d, jnp.concatenate(spread, axis=0), (((1,), (1,)), ((), ())), precision=HIGHEST,
        preferred_element_type=F32,
    )
    for n in range(copies):
        out[pl.ds(count_d * n, count_d), :] = tile[:count_d, :]


def final_kernel(tiles, out):
    mine = lax.axis_index("strike") * 2
    summed = jnp.sum(tiles[...], axis=0, keepdims=True)
    lane = lax.broadcasted_iota(jnp.int32, (2, NZL), 1)
    place = lax.broadcasted_iota(jnp.int32, (2, NZL), 0)
    for c in range(3):
        hit = lane == 32 * c + mine + place
        out[:, pl.ds(c, 1)] = jnp.sum(jnp.where(hit, summed, 0.0), axis=1, keepdims=True)


def call(kernel, name, outs, scratch=(), flops=0, moved=0):
    return pl.pallas_call(
        kernel,
        out_shape=[jax.ShapeDtypeStruct(shape, F32) for shape in outs],
        scratch_shapes=[pltpu.VMEM(shape, F32) for shape in scratch],
        compiler_params=pltpu.CompilerParams(vmem_limit_bytes=16 * 2**20),
        cost_estimate=pl.CostEstimate(flops=flops, bytes_accessed=moved, transcendentals=0),
        name=name,
    )


def upward(value, axis):
    count = lax.axis_size(axis)
    return lax.ppermute(value, axis, [(i, i + 1) for i in range(count - 1)])


def downward(value, axis):
    count = lax.axis_size(axis)
    return lax.ppermute(value, axis, [(i + 1, i) for i in range(count - 1)])


def exchange(messages):
    axes = ("normal", "normal", "strike", "strike", "depth", "depth")
    return [
        (upward if i % 2 == 0 else downward)(message, axis) for i, (message, axis) in enumerate(zip(messages, axes))
    ]


def local(field_now, field_prev, rigidity, density, fault_nodes, patch_ids):
    count_n, count_s, count_d = (lax.axis_size(a) for a in ("normal", "strike", "depth"))
    flat = (3, ROWS, NZL)
    now, prev = field_now.reshape(flat), field_prev.reshape(flat)
    rig, rho = rigidity.reshape(ROWS, NZL), density.reshape(ROWS, NZL)
    sent = call(
        pack_kernel, "pack", [(112, NZL), (64, NZL), (56, NZL), (32, NZL), (8, NZL), (8, NZL)], [(ROWS, NZL)],
        flops=2_000_000, moved=400_000,
    )(now, rig)
    got = exchange(sent)
    mid, *rest = call(
        functools.partial(first_kernel, count_n // 2), "first",
        [flat, (48, NZL), (48, NZL), (24, NZL), (24, NZL), (8, NZL), (8, NZL), (16, NZL), (8, NZL), (8, NZL), (48, NZL)],
        [(ROWS, NZL), (ROWS, NZL), flat, (48, NZL)], flops=10_000_000, moved=900_000,
    )(now, prev, rig, rho, *got, sent[5])
    sent2, weights, slip = rest[:6], rest[6:9], rest[9]
    got2 = exchange(sent2)
    nodes, ids = fault_nodes.reshape(1, -1), patch_ids.reshape(1, -1)
    (tiles,) = call(
        functools.partial(patch_kernel, count_n, count_d, count_s), "patch", [(count_n * count_d, NZL)],
        flops=10_000_000, moved=60_000,
    )(slip, nodes, ids)
    tiles = lax.all_to_all(tiles, ("normal", "depth"), 0, 0, tiled=True)
    row = jnp.sum(tiles, axis=0, keepdims=True)
    rows = lax.all_to_all(jnp.broadcast_to(row, (count_s, NZL)), "strike", 0, 0, tiled=True)
    (share,) = call(final_kernel, "final", [(2, 3)], flops=10_000, moved=10_000)(rows)
    (following,) = call(
        second_kernel, "second", [flat], [(ROWS, NZL), (ROWS, NZL), flat], flops=10_000_000, moved=900_000,
    )(mid, now, rig, rho, *got2, sent2[5], *weights, got[1], got[3], got[5])
    return following.reshape(field_now.shape), mid.reshape(field_now.shape), share


def solution(mesh):
    field = P(None, "normal", "strike", "depth")
    cells = P("normal", "strike", "depth")
    pairs = P("strike", "depth", None)
    return jax.shard_map(
        local,
        mesh=mesh,
        in_specs=(field, field, cells, cells, pairs, pairs),
        out_specs=(field, field, P(("strike", "depth"), None)),
        check_vma=False,
    )
```

time: 973 us -> 93.4 us (0.10)
  the two profiles are of different devices: /device:TPU:1 before, /device:TPU:161 now
where the time goes in v1:
time: 93.4 us; the launch traced here: 92.8 us
  starting transfers between devices  56.8 us (61%)
  blocking collectives  14.1 us (15%)
  waiting for transfers between devices  8.57 us (9%)
  Pallas kernels  8.54 us (9%)
  local copies, waits for them, and re-layouts  3.91 us (4%)
    ppermute x6, starting transfers between devices, downward(): return lax.ppermute(value, axis, [(i + 1, i) for i in range(count - 1)])  25.1 us
    ppermute x6, starting transfers between devices, upward(): return lax.ppermute(value, axis, [(i, i + 1) for i in range(count - 1)])  21.1 us
    all_to_all x1, blocking collectives, local(): tiles = lax.all_to_all(tiles, ('normal', 'depth'), 0, 0, tiled=True)  14.1 us
    all_to_all x1, starting transfers between devices, local(): lax.all_to_all(jnp.broadcast_to(row, (count_s, NZL)), 'strike', 0, 0, til...  10.6 us
    ppermute x6, waiting for transfers between devices, downward(): return lax.ppermute(value, axis, [(i + 1, i) for i in range(count - 1)])  7.09 us
    pallas_call x1, Pallas kernels, local(): call(functools.partial(first_kernel, count_n // 2), 'first', [flat, (48,...  3.67 us
    pallas_call x1, Pallas kernels, local(): call(second_kernel, 'second', [flat], [(ROWS, NZL), (ROWS, NZL), flat], f...  3.45 us
    unnamed x18, local copies, waits for them, and re-layouts  3.3 us
  transfers between devices with their start and end apart: 13, of which 4 were waited for; matrix products, arithmetic and copies ran while one was open for 0% of the time, Pallas kernels for 4%

profile of v1, /device:TPU:161, one launch (start us, length us, event | category | flops | bytes accessed | tf_op | source)
XLA Modules:
  0.0 92.8 jit_solution(13034745867454471358)
XLA Ops:
  0.6 0.0 copy-start
  0.6 0.9 copy-done
  1.6 0.8 copy-done.2
  2.3 0.3 pack.1
  2.6 3.5 %collective-permute-start = (f32[112,128]{1,0:T(8,128)S(1)}, f32[112,128]{1,0:T(8,128)S(1)}, u32[]{:S(2)}, u32[]{:S(2)}) collective-permute-start(f32[112,128]{1,0:T(8,128)S(1)} %get-tuple-element.20), channel_id=1, source_target_pairs={{0,128},{128,256},{256,384},{1,129},{129,257},{257,385},{2,130},{1... | collective-permute-start | bytes 172040 | tf_op jit(solution)/shard_map/ppermute | solution.py:430
  6.2 1.9 %collective-permute-start.1 = (f32[64,128]{1,0:T(8,128)S(1)}, f32[64,128]{1,0:T(8,128)S(1)}, u32[]{:S(2)}, u32[]{:S(2)}) collective-permute-start(f32[64,128]{1,0:T(8,128)S(1)} %get-tuple-element.21), channel_id=1, source_target_pairs={{128,0},{256,128},{384,256},{129,1},{257,129},{385,257},{130,2},{2... | collective-permute-start | bytes 98312 | tf_op jit(solution)/shard_map/ppermute | solution.py:435
  8.1 3.2 %collective-permute-start.2 = (f32[56,128]{1,0:T(8,128)S(1)}, f32[56,128]{1,0:T(8,128)S(1)}, u32[]{:S(2)}, u32[]{:S(2)}) collective-permute-start(f32[56,128]{1,0:T(8,128)S(1)} %get-tuple-element.22), channel_id=1, source_target_pairs={{0,8},{8,16},{16,24},{24,32},{32,40},{40,48},{48,56},{56,64},{64,7... | collective-permute-start | bytes 86024 | tf_op jit(solution)/shard_map/ppermute | solution.py:430
  11.3 8.1 %collective-permute-start.3 = (f32[32,128]{1,0:T(8,128)S(1)}, f32[32,128]{1,0:T(8,128)S(1)}, u32[]{:S(2)}, u32[]{:S(2)}) collective-permute-start(f32[32,128]{1,0:T(8,128)S(1)} %get-tuple-element.23), channel_id=1, source_target_pairs={{8,0},{16,8},{24,16},{32,24},{40,32},{48,40},{56,48},{64,56},{72,6... | collective-permute-start | bytes 49160 | tf_op jit(solution)/shard_map/ppermute | solution.py:435
  19.4 4.6 %collective-permute-start.4 = (f32[8,128]{1,0:T(8,128)S(1)}, f32[8,128]{1,0:T(8,128)S(1)}, u32[]{:S(2)}, u32[]{:S(2)}) collective-permute-start(f32[8,128]{1,0:T(8,128)S(1)} %get-tuple-element.24), channel_id=1, source_target_pairs={{0,1},{1,2},{2,3},{3,4},{4,5},{5,6},{6,7},{8,9},{9,10},{10,11},{11... | collective-permute-start | bytes 12296 | tf_op jit(solution)/shard_map/ppermute | solution.py:430
  24.1 0.7 collective-permute-done.4.zu
  24.8 1.9 %collective-permute-start.5 = (f32[8,128]{1,0:T(8,128)S(1)}, f32[8,128]{1,0:T(8,128)S(1)}, u32[]{:S(2)}, u32[]{:S(2)}) collective-permute-start(f32[8,128]{1,0:T(8,128)S(1)} %get-tuple-element.25.zd_own), channel_id=1, source_target_pairs={{1,0},{2,1},{3,2},{4,3},{5,4},{6,5},{7,6},{9,8},{10,9},{11,10},{12... | collective-permute-start | bytes 12296 | tf_op jit(solution)/shard_map/ppermute | solution.py:435
  26.7 3.5 %collective-permute-done.5.zd = f32[8,128]{1,0:T(8,128)S(1)} collective-permute-done((f32[8,128]{1,0:T(8,128)S(1)}, f32[8,128]{1,0:T(8,128)S(1)}, u32[]{:S(2)}, u32[]{:S(2)}) %collective-permute-start.5) | collective-permute-done | bytes 4128 | tf_op jit(solution)/shard_map/ppermute | solution.py:435
  30.3 0.0 copy-start.1
  30.3 3.7 %first.1 = (f32[3,128,128]{2,1,0:T(8,128)}, f32[48,128]{1,0:T(8,128)S(1)}, f32[48,128]{1,0:T(8,128)S(1)}, f32[24,128]{1,0:T(8,128)S(1)}, f32[24,128]{1,0:T(8,128...) custom-call(f32[3,128,128]{2,1,0:T(8,128)S(1)} %bitcast.13, ...), custom_call_target="tpu_custom_call" | custom-call | flops 10000000 | bytes 900000 | tf_op jit(solution)/shard_map/first/pallas_call | solution.py:455
  34.0 0.7 copy-done.7
  34.7 0.4 patch.1
  35.1 14.1 %all_to_all.17 = f32[32,1,128]{2,1,0:T(1,128)S(1)} all-to-all(f32[32,1,128]{2,1,0:T(1,128)S(1)} %bitcast.22), channel_id=1, replica_groups=mesh['normal'=4,'strike'=16,'depth'=8] {'normal','depth'}, dimensions={0} | all-to-all | bytes 32768 | tf_op jit(solution)/shard_map/all_to_all | solution.py:467
  49.3 0.1 reduce_sum.9
  49.3 0.6 broadcast_in_dim.2
  49.9 10.6 %all-to-all-start.1 = ((f32[16,1,128]{2,1,0:T(1,128)}), f32[16,1,128]{2,1,0:T(1,128)S(1)}, u32[]{:S(2)}, u32[]{:S(2)}) async-start(f32[16,1,128]{2,1,0:T(1,128)} %broadcast_in_dim.2), calls=%async_computation.1 | async-start | bytes 16384 | tf_op jit(solution)/shard_map/all_to_all | solution.py:469
  60.5 2.2 %collective-permute-start.6 = (f32[48,128]{1,0:T(8,128)S(1)}, f32[48,128]{1,0:T(8,128)S(1)}, u32[]{:S(2)}, u32[]{:S(2)}) collective-permute-start(f32[48,128]{1,0:T(8,128)S(1)} %get-tuple-element.27), channel_id=1, source_target_pairs={{0,128},{128,256},{256,384},{1,129},{129,257},{257,385},{2,130},{1... | collective-permute-start | bytes 73736 | tf_op jit(solution)/shard_map/ppermute | solution.py:430
  62.7 3.1 %collective-permute-start.7 = (f32[48,128]{1,0:T(8,128)S(1)}, f32[48,128]{1,0:T(8,128)S(1)}, u32[]{:S(2)}, u32[]{:S(2)}) collective-permute-start(f32[48,128]{1,0:T(8,128)S(1)} %get-tuple-element.28), channel_id=1, source_target_pairs={{128,0},{256,128},{384,256},{129,1},{257,129},{385,257},{130,2},{2... | collective-permute-start | bytes 73736 | tf_op jit(solution)/shard_map/ppermute | solution.py:435
  65.8 3.1 %collective-permute-start.8 = (f32[24,128]{1,0:T(8,128)S(1)}, f32[24,128]{1,0:T(8,128)S(1)}, u32[]{:S(2)}, u32[]{:S(2)}) collective-permute-start(f32[24,128]{1,0:T(8,128)S(1)} %get-tuple-element.29), channel_id=1, source_target_pairs={{0,8},{8,16},{16,24},{24,32},{32,40},{40,48},{48,56},{56,64},{64,7... | collective-permute-start | bytes 36872 | tf_op jit(solution)/shard_map/ppermute | solution.py:430
  68.9 8.2 %collective-permute-start.9 = (f32[24,128]{1,0:T(8,128)S(1)}, f32[24,128]{1,0:T(8,128)S(1)}, u32[]{:S(2)}, u32[]{:S(2)}) collective-permute-start(f32[24,128]{1,0:T(8,128)S(1)} %get-tuple-element.30), channel_id=1, source_target_pairs={{8,0},{16,8},{24,16},{32,24},{40,32},{48,40},{56,48},{64,56},{72,6... | collective-permute-start | bytes 36872 | tf_op jit(solution)/shard_map/ppermute | solution.py:435
  77.1 4.4 %collective-permute-start.10 = (f32[8,128]{1,0:T(8,128)S(1)}, f32[8,128]{1,0:T(8,128)S(1)}, u32[]{:S(2)}, u32[]{:S(2)}) collective-permute-start(f32[8,128]{1,0:T(8,128)S(1)} %get-tuple-element.31), channel_id=1, source_target_pairs={{0,1},{1,2},{2,3},{3,4},{4,5},{5,6},{6,7},{8,9},{9,10},{10,11},{11... | collective-permute-start | bytes 12296 | tf_op jit(solution)/shard_map/ppermute | solution.py:430
  81.5 0.7 collective-permute-done.10.zu2
  82.3 1.9 %collective-permute-start.11 = (f32[8,128]{1,0:T(8,128)S(1)}, f32[8,128]{1,0:T(8,128)S(1)}, u32[]{:S(2)}, u32[]{:S(2)}) collective-permute-start(f32[8,128]{1,0:T(8,128)S(1)} %get-tuple-element.32.zd2_own), channel_id=1, source_target_pairs={{1,0},{2,1},{3,2},{4,3},{5,4},{6,5},{7,6},{9,8},{10,9},{11,10},{12... | collective-permute-start | bytes 12296 | tf_op jit(solution)/shard_map/ppermute | solution.py:435
  84.2 3.5 %collective-permute-done.11.zd2 = f32[8,128]{1,0:T(8,128)S(1)} collective-permute-done((f32[8,128]{1,0:T(8,128)S(1)}, f32[8,128]{1,0:T(8,128)S(1)}, u32[]{:S(2)}, u32[]{:S(2)}) %collective-permute-start.11) | collective-permute-done | bytes 4128 | tf_op jit(solution)/shard_map/ppermute | solution.py:435
  87.8 0.0 copy-start.5
  87.8 0.9 copy-done.5
  88.7 3.4 %second.1 = f32[3,128,128]{2,1,0:T(8,128)} custom-call(f32[3,128,128]{2,1,0:T(8,128)S(1)} %copy-done.5, f32[3,128,128]{2,1,0:T(8,128)S(1)} %bitcast.14, bf16[128,128]{1,0:T(8,128)(2,1)S(1)} %bitcast.17, bf16[128,128]{1,0:T(8,128)(2,1)S(1)} %bitcast.21, f32[48,128]{1,0:T(8,128)S(1)} %collective-permute-done.6.xu2, f32[48,128]{1,0:T(8,128)S(1)} %collective-permute-done.7.xd2, ...), custom_call_target="tpu_custom_call" | custom-call | flops 10000000 | bytes 900000 | tf_op jit(solution)/shard_map/second/pallas_call | solution.py:471
  92.1 0.7 final.1
  (20 shorter events, 0.0 us)
Async XLA Ops:
  0.6 0.9 %copy-start = (f32[3,8,16,128]{3,2,1,0:T(8,128)S(1)}, f32[3,8,16,128]{3,2,1,0:T(8,128)}, u32[]{:S(2)}) copy-start(f32[3,8,16,128]{3,2,1,0:T(8,128)} %param.6) | copy-start | bytes 589828
  1.6 0.8 copy-start.2
  2.3 28.0 %copy-start.4 = (f32[3,8,16,128]{3,2,1,0:T(8,128)S(1)}, f32[3,8,16,128]{3,2,1,0:T(8,128)}, u32[]{:S(2)}) copy-start(f32[3,8,16,128]{3,2,1,0:T(8,128)} %param.7) | copy-start | bytes 589828
  2.3 28.0 %copy-start.6 = (bf16[8,16,128]{2,1,0:T(8,128)(2,1)S(1)}, bf16[8,16,128]{2,1,0:T(8,128)(2,1)}, u32[]{:S(2)}) copy-start(bf16[8,16,128]{2,1,0:T(8,128)(2,1)} %param.9) | copy-start | bytes 98308
  2.6 27.6 %collective-permute-start = (f32[112,128]{1,0:T(8,128)S(1)}, f32[112,128]{1,0:T(8,128)S(1)}, u32[]{:S(2)}, u32[]{:S(2)}) collective-permute-start(f32[112,128]{1,0:T(8,128)S(1)} %get-tuple-element.20), channel_id=1, source_target_pairs={{0,128},{128,256},{256,384},{1,129},{129,257},{257,385},{2,130},{1... | collective-permute-start | bytes 172040 | tf_op jit(solution)/shard_map/ppermute | solution.py:430
  6.2 24.1 %collective-permute-start.1 = (f32[64,128]{1,0:T(8,128)S(1)}, f32[64,128]{1,0:T(8,128)S(1)}, u32[]{:S(2)}, u32[]{:S(2)}) collective-permute-start(f32[64,128]{1,0:T(8,128)S(1)} %get-tuple-element.21), channel_id=1, source_target_pairs={{128,0},{256,128},{384,256},{129,1},{257,129},{385,257},{130,2},{2... | collective-permute-start | bytes 98312 | tf_op jit(solution)/shard_map/ppermute | solution.py:435
  8.1 22.1 %collective-permute-start.2 = (f32[56,128]{1,0:T(8,128)S(1)}, f32[56,128]{1,0:T(8,128)S(1)}, u32[]{:S(2)}, u32[]{:S(2)}) collective-permute-start(f32[56,128]{1,0:T(8,128)S(1)} %get-tuple-element.22), channel_id=1, source_target_pairs={{0,8},{8,16},{16,24},{24,32},{32,40},{40,48},{48,56},{56,64},{64,7... | collective-permute-start | bytes 86024 | tf_op jit(solution)/shard_map/ppermute | solution.py:430
  11.3 18.9 %collective-permute-start.3 = (f32[32,128]{1,0:T(8,128)S(1)}, f32[32,128]{1,0:T(8,128)S(1)}, u32[]{:S(2)}, u32[]{:S(2)}) collective-permute-start(f32[32,128]{1,0:T(8,128)S(1)} %get-tuple-element.23), channel_id=1, source_target_pairs={{8,0},{16,8},{24,16},{32,24},{40,32},{48,40},{56,48},{64,56},{72,6... | collective-permute-start | bytes 49160 | tf_op jit(solution)/shard_map/ppermute | solution.py:435
  19.4 5.4 %collective-permute-start.4 = (f32[8,128]{1,0:T(8,128)S(1)}, f32[8,128]{1,0:T(8,128)S(1)}, u32[]{:S(2)}, u32[]{:S(2)}) collective-permute-start(f32[8,128]{1,0:T(8,128)S(1)} %get-tuple-element.24), channel_id=1, source_target_pairs={{0,1},{1,2},{2,3},{3,4},{4,5},{5,6},{6,7},{8,9},{9,10},{10,11},{11... | collective-permute-start | bytes 12296 | tf_op jit(solution)/shard_map/ppermute | solution.py:430
  24.8 5.5 %collective-permute-start.5 = (f32[8,128]{1,0:T(8,128)S(1)}, f32[8,128]{1,0:T(8,128)S(1)}, u32[]{:S(2)}, u32[]{:S(2)}) collective-permute-start(f32[8,128]{1,0:T(8,128)S(1)} %get-tuple-element.25.zd_own), channel_id=1, source_target_pairs={{1,0},{2,1},{3,2},{4,3},{5,4},{6,5},{7,6},{9,8},{10,9},{11,10},{12... | collective-permute-start | bytes 12296 | tf_op jit(solution)/shard_map/ppermute | solution.py:435
  30.3 3.7 %copy-start.8 = (s32[1,1,256]{2,1,0:T(1,128)S(1)}, s32[1,1,256]{2,1,0:T(1,128)}, u32[]{:S(2)}) copy-start(s32[1,1,256]{2,1,0:T(1,128)} %param.11) | copy-start | bytes 3076
  30.3 57.4 %copy-start.1 = (f32[3,8,16,128]{3,2,1,0:T(8,128)S(1)}, f32[3,8,16,128]{3,2,1,0:T(8,128)}, u32[]{:S(2)}) copy-start(f32[3,8,16,128]{3,2,1,0:T(8,128)} %param.6) | copy-start | bytes 589828
  34.0 0.7 copy-start.7
  49.3 38.5 %copy-start.3 = (bf16[8,16,128]{2,1,0:T(8,128)(2,1)S(1)}, bf16[8,16,128]{2,1,0:T(8,128)(2,1)}, u32[]{:S(2)}) copy-start(bf16[8,16,128]{2,1,0:T(8,128)(2,1)} %param.8) | copy-start | bytes 98308
  49.9 42.2 %all-to-all-start.1 = ((f32[16,1,128]{2,1,0:T(1,128)}), f32[16,1,128]{2,1,0:T(1,128)S(1)}, u32[]{:S(2)}, u32[]{:S(2)}) async-start(f32[16,1,128]{2,1,0:T(1,128)} %broadcast_in_dim.2), calls=%async_computation.1 | async-start | bytes 16384 | tf_op jit(solution)/shard_map/all_to_all | solution.py:469
  60.5 27.2 %collective-permute-start.6 = (f32[48,128]{1,0:T(8,128)S(1)}, f32[48,128]{1,0:T(8,128)S(1)}, u32[]{:S(2)}, u32[]{:S(2)}) collective-permute-start(f32[48,128]{1,0:T(8,128)S(1)} %get-tuple-element.27), channel_id=1, source_target_pairs={{0,128},{128,256},{256,384},{1,129},{129,257},{257,385},{2,130},{1... | collective-permute-start | bytes 73736 | tf_op jit(solution)/shard_map/ppermute | solution.py:430
  62.7 25.0 %collective-permute-start.7 = (f32[48,128]{1,0:T(8,128)S(1)}, f32[48,128]{1,0:T(8,128)S(1)}, u32[]{:S(2)}, u32[]{:S(2)}) collective-permute-start(f32[48,128]{1,0:T(8,128)S(1)} %get-tuple-element.28), channel_id=1, source_target_pairs={{128,0},{256,128},{384,256},{129,1},{257,129},{385,257},{130,2},{2... | collective-permute-start | bytes 73736 | tf_op jit(solution)/shard_map/ppermute | solution.py:435
  65.8 21.9 %collective-permute-start.8 = (f32[24,128]{1,0:T(8,128)S(1)}, f32[24,128]{1,0:T(8,128)S(1)}, u32[]{:S(2)}, u32[]{:S(2)}) collective-permute-start(f32[24,128]{1,0:T(8,128)S(1)} %get-tuple-element.29), channel_id=1, source_target_pairs={{0,8},{8,16},{16,24},{24,32},{32,40},{40,48},{48,56},{56,64},{64,7... | collective-permute-start | bytes 36872 | tf_op jit(solution)/shard_map/ppermute | solution.py:430
  68.9 18.8 %collective-permute-start.9 = (f32[24,128]{1,0:T(8,128)S(1)}, f32[24,128]{1,0:T(8,128)S(1)}, u32[]{:S(2)}, u32[]{:S(2)}) collective-permute-start(f32[24,128]{1,0:T(8,128)S(1)} %get-tuple-element.30), channel_id=1, source_target_pairs={{8,0},{16,8},{24,16},{32,24},{40,32},{48,40},{56,48},{64,56},{72,6... | collective-permute-start | bytes 36872 | tf_op jit(solution)/shard_map/ppermute | solution.py:435
  77.1 5.1 %collective-permute-start.10 = (f32[8,128]{1,0:T(8,128)S(1)}, f32[8,128]{1,0:T(8,128)S(1)}, u32[]{:S(2)}, u32[]{:S(2)}) collective-permute-start(f32[8,128]{1,0:T(8,128)S(1)} %get-tuple-element.31), channel_id=1, source_target_pairs={{0,1},{1,2},{2,3},{3,4},{4,5},{5,6},{6,7},{8,9},{9,10},{10,11},{11... | collective-permute-start | bytes 12296 | tf_op jit(solution)/shard_map/ppermute | solution.py:430
  82.3 5.5 %collective-permute-start.11 = (f32[8,128]{1,0:T(8,128)S(1)}, f32[8,128]{1,0:T(8,128)S(1)}, u32[]{:S(2)}, u32[]{:S(2)}) collective-permute-start(f32[8,128]{1,0:T(8,128)S(1)} %get-tuple-element.32.zd2_own), channel_id=1, source_target_pairs={{1,0},{2,1},{3,2},{4,3},{5,4},{6,5},{7,6},{9,8},{10,9},{11,10},{12... | collective-permute-start | bytes 12296 | tf_op jit(solution)/shard_map/ppermute | solution.py:435
  87.8 0.9 %copy-start.5 = (f32[3,128,128]{2,1,0:T(8,128)S(1)}, f32[3,128,128]{2,1,0:T(8,128)}, u32[]{:S(2)}) copy-start(f32[3,128,128]{2,1,0:T(8,128)} %get-tuple-element.26.now) | copy-start | bytes 589828

commit v2 on v1

--- a/solution.py
+++ b/solution.py
@@ -141,7 +141,23 @@
         dst[pl.ds(x * NYL, NYL), :] = src[pl.ds(x * NYL, NYL), :].astype(F32)
 
 
-def pack_kernel(now, rig, xu, xd, yu, yd, zu, zd, rw):
+def sides(ref, up, down):
+    return ref.at[pl.ds(0, up)], ref.at[pl.ds(up, down)]
+
+
+def neighbours(gathered, index, count, up, down, low, high):
+    below = pl.multiple_of(jnp.maximum(index - 1, 0) * (up + down), 8)
+    above = pl.multiple_of(jnp.minimum(index + 1, count - 1) * (up + down) + up, 8)
+    low[...] = jnp.where(index > 0, gathered[pl.ds(below, up), :], 0.0)
+    high[...] = jnp.where(index < count - 1, gathered[pl.ds(above, down), :], 0.0)
+
+
+FIRST_ROWS = ((112, 64), (56, 32), (8, 8))
+SECOND_ROWS = ((48, 48), (24, 24), (8, 8))
+
+
+def pack_kernel(now, rig, hx, hy, hz, rw):
+    (xu, xd), (yu, yd), (zu, zd) = (sides(ref, *n) for ref, n in zip((hx, hy, hz), FIRST_ROWS))
     widen(rig, rw)
     lane = lane_of()
     for half in range(2):
@@ -283,11 +299,16 @@
 
 
 def first_kernel(
-    middle, now, prev, rig, rho, xu, xd, yu, yd, zu, zd, zd_own,
-    out, xu2, xd2, yu2, yd2, zu2, zd2, mx, my, mz, slip,
-    rw, scale, acc, early,
+    counts, now, prev, rig, rho, gx, gy, gz, hz,
+    out, hx2, hy2, hz2, mx, my, mz, slip, xd, yd, zd,
+    rw, scale, acc, early, xu, yu, zu,
 ):
+    middle = counts[0] // 2
     index = (lax.axis_index("normal"), lax.axis_index("strike"), lax.axis_index("depth"))
+    for d, (ref, low, high) in enumerate(((gx, xu, xd), (gy, yu, yd), (gz, zu, zd))):
+        neighbours(ref, index[d], counts[d], *FIRST_ROWS[d], low, high)
+    zd_own = hz.at[pl.ds(8, 8)]
+    (xu2, xd2), (yu2, yd2), (zu2, zd2) = (sides(ref, *n) for ref, n in zip((hx2, hy2, hz2), SECOND_ROWS))
     widen(rig, rw)
     step_scale(rho, scale)
     lane = lane_of()
@@ -356,10 +377,13 @@
 
 
 def second_kernel(
-    now, prev, rig, rho, xu2, xd2, yu2, yd2, zu2, zd2, zd2_own, mx, my, mz, xd, yd, zd,
-    out, rw, scale, acc,
+    counts, now, prev, rig, rho, gx, gy, gz, hz, mx, my, mz, xd, yd, zd,
+    out, rw, scale, acc, xu2, xd2, yu2, yd2, zu2, zd2,
 ):
     index = (lax.axis_index("normal"), lax.axis_index("strike"), lax.axis_index("depth"))
+    for d, (ref, low, high) in enumerate(((gx, xu2, xd2), (gy, yu2, yd2), (gz, zu2, zd2))):
+        neighbours(ref, index[d], counts[d], *SECOND_ROWS[d], low, high)
+    zd2_own = hz.at[pl.ds(8, 8)]
     widen(rig, rw)
     step_scale(rho, scale)
     closing_z = zu2[...] + mz[...] * zd2_own[...]
@@ -379,7 +403,7 @@
     )
 
 
-def patch_kernel(copies, count_d, count_s, slip, nodes, ids, out):
+def patch_kernel(count_d, slip, nodes, ids, out):
     pairs = nodes.shape[-1]
     node = nodes[...]
     hot_z = (lax.broadcasted_iota(jnp.int32, (NZL, pairs), 0) == (node & (NZL - 1))).astype(F32)
@@ -396,17 +420,16 @@
         spread.append(jnp.where(hot_slot, picked, 0.0))
     spread.append(jnp.zeros((32, pairs), F32))
     hot_d = (lax.broadcasted_iota(jnp.int32, (8, pairs), 0) == owner_d).astype(F32)
-    tile = lax.dot_general(
+    out[...] = lax.dot_general(
         hot_d, jnp.concatenate(spread, axis=0), (((1,), (1,)), ((), ())), precision=HIGHEST,
         preferred_element_type=F32,
     )
-    for n in range(copies):
-        out[pl.ds(count_d * n, count_d), :] = tile[:count_d, :]
 
 
 def final_kernel(tiles, out):
     mine = lax.axis_index("strike") * 2
-    summed = jnp.sum(tiles[...], axis=0, keepdims=True)
+    row = lax.broadcasted_iota(jnp.int32, (8, NZL), 0) == lax.axis_index("depth")
+    summed = jnp.sum(jnp.where(row, tiles[...], 0.0), axis=0, keepdims=True)
     lane = lax.broadcasted_iota(jnp.int32, (2, NZL), 1)
     place = lax.broadcasted_iota(jnp.int32, (2, NZL), 0)
     for c in range(3):
@@ -425,52 +448,42 @@
     )
 
 
-def upward(value, axis):
-    count = lax.axis_size(axis)
-    return lax.ppermute(value, axis, [(i, i + 1) for i in range(count - 1)])
-
-
-def downward(value, axis):
-    count = lax.axis_size(axis)
-    return lax.ppermute(value, axis, [(i + 1, i) for i in range(count - 1)])
-
-
 def exchange(messages):
-    axes = ("normal", "normal", "strike", "strike", "depth", "depth")
     return [
-        (upward if i % 2 == 0 else downward)(message, axis) for i, (message, axis) in enumerate(zip(messages, axes))
+        lax.all_gather(message, axis, axis=0, tiled=True)
+        for message, axis in zip(messages, ("normal", "strike", "depth"))
     ]
 
 
 def local(field_now, field_prev, rigidity, density, fault_nodes, patch_ids):
-    count_n, count_s, count_d = (lax.axis_size(a) for a in ("normal", "strike", "depth"))
+    axes = ("normal", "strike", "depth")
+    counts = tuple(lax.axis_size(a) for a in axes)
     flat = (3, ROWS, NZL)
     now, prev = field_now.reshape(flat), field_prev.reshape(flat)
     rig, rho = rigidity.reshape(ROWS, NZL), density.reshape(ROWS, NZL)
-    sent = call(
-        pack_kernel, "pack", [(112, NZL), (64, NZL), (56, NZL), (32, NZL), (8, NZL), (8, NZL)], [(ROWS, NZL)],
-        flops=2_000_000, moved=400_000,
-    )(now, rig)
+    first_sizes = [(up + down, NZL) for up, down in FIRST_ROWS]
+    second_sizes = [(up + down, NZL) for up, down in SECOND_ROWS]
+    sent = call(pack_kernel, "pack", first_sizes, [(ROWS, NZL)], flops=2_000_000, moved=400_000)(now, rig)
     got = exchange(sent)
     mid, *rest = call(
-        functools.partial(first_kernel, count_n // 2), "first",
-        [flat, (48, NZL), (48, NZL), (24, NZL), (24, NZL), (8, NZL), (8, NZL), (16, NZL), (8, NZL), (8, NZL), (48, NZL)],
-        [(ROWS, NZL), (ROWS, NZL), flat, (48, NZL)], flops=10_000_000, moved=900_000,
-    )(now, prev, rig, rho, *got, sent[5])
-    sent2, weights, slip = rest[:6], rest[6:9], rest[9]
+        functools.partial(first_kernel, counts), "first",
+        [flat] + second_sizes + [(16, NZL), (8, NZL), (8, NZL), (48, NZL)] + [(n[1], NZL) for n in FIRST_ROWS],
+        [(ROWS, NZL), (ROWS, NZL), flat, (48, NZL)] + [(n[0], NZL) for n in FIRST_ROWS],
+        flops=10_000_000, moved=900_000,
+    )(now, prev, rig, rho, *got, sent[2])
+    sent2, weights, slip, kept = rest[:3], rest[3:6], rest[6], rest[7:]
+    nodes, ids = fault_nodes.reshape(1, -1), patch_ids.reshape(1, -1)
+    (tile,) = call(
+        functools.partial(patch_kernel, counts[2]), "patch", [(8, NZL)], flops=10_000_000, moved=60_000,
+    )(slip, nodes, ids)
+    sums = lax.psum(tile, axes)
     got2 = exchange(sent2)
-    nodes, ids = fault_nodes.reshape(1, -1), patch_ids.reshape(1, -1)
-    (tiles,) = call(
-        functools.partial(patch_kernel, count_n, count_d, count_s), "patch", [(count_n * count_d, NZL)],
-        flops=10_000_000, moved=60_000,
-    )(slip, nodes, ids)
-    tiles = lax.all_to_all(tiles, ("normal", "depth"), 0, 0, tiled=True)
-    row = jnp.sum(tiles, axis=0, keepdims=True)
-    rows = lax.all_to_all(jnp.broadcast_to(row, (count_s, NZL)), "strike", 0, 0, tiled=True)
-    (share,) = call(final_kernel, "final", [(2, 3)], flops=10_000, moved=10_000)(rows)
+    (share,) = call(final_kernel, "final", [(2, 3)], flops=10_000, moved=10_000)(sums)
     (following,) = call(
-        second_kernel, "second", [flat], [(ROWS, NZL), (ROWS, NZL), flat], flops=10_000_000, moved=900_000,
-    )(mid, now, rig, rho, *got2, sent2[5], *weights, got[1], got[3], got[5])
+        functools.partial(second_kernel, counts), "second", [flat],
+        [(ROWS, NZL), (ROWS, NZL), flat] + [(n, NZL) for pair in SECOND_ROWS for n in pair],
+        flops=10_000_000, moved=900_000,
+    )(mid, now, rig, rho, *got2, sent2[2], *weights, *kept)
     return following.reshape(field_now.shape), mid.reshape(field_now.shape), share
 
 

time: 93.4 us -> 287 us (3.07)
  the two profiles are of different devices: /device:TPU:161 before, /device:TPU:2 now
where the time goes in v2:
time: 287 us
  blocking collectives  275 us (96%)
  Pallas kernels  8.57 us (3%)
    all_gather x6, blocking collectives, exchange(): lax.all_gather(message, axis, axis=0, tiled=True)  175 us
    psum x1, blocking collectives, local(): sums = lax.psum(tile, axes)  100 us

profile of v2, /device:TPU:2, one launch (start us, length us, event | category | flops | bytes accessed | tf_op | source)
XLA Modules:
  0.0 286.7 jit_solution(12862721759779196534)
XLA Ops:
  0.6 0.0 copy-start
  0.6 0.9 copy-done
  1.6 0.0 copy-start.2
  1.6 0.8 copy-done.2
  2.3 0.3 pack.1
  2.6 15.4 %all_gather.20.gz = f32[128,128]{1,0:T(8,128)S(1)} all-gather(f32[16,128]{1,0:T(8,128)S(1)} %get-tuple-element.19.hz), channel_id=1, replica_groups=mesh['normal'=4,'strike'=16,'depth'=8] {'depth'}, dimensions={0}, use_global_device_ids=true | all-gather | bytes 73728 | tf_op jit(solution)/shard_map/all_gather | solution.py:453
  18.1 14.5 %all_gather.18.gx = f32[704,128]{1,0:T(8,128)S(1)} all-gather(f32[176,128]{1,0:T(8,128)S(1)} %get-tuple-element.17), channel_id=1, replica_groups=mesh['normal'=4,'strike'=16,'depth'=8] {'normal'}, dimensions={0}, use_global_device_ids=true | all-gather | bytes 450560 | tf_op jit(solution)/shard_map/all_gather | solution.py:453
  32.6 0.0 copy-start.4
  32.6 0.0 copy-start.6
  32.6 64.0 %all_gather.19.gy = f32[1408,128]{1,0:T(8,128)S(1)} all-gather(f32[88,128]{1,0:T(8,128)S(1)} %get-tuple-element.18), channel_id=1, replica_groups=mesh['normal'=4,'strike'=16,'depth'=8] {'strike'}, dimensions={0}, use_global_device_ids=true | all-gather | bytes 765952 | tf_op jit(solution)/shard_map/all_gather | solution.py:453
  96.6 0.0 copy-done.4
  96.6 0.0 copy-done.6
  96.6 0.0 copy-start.8
  96.6 3.7 %first.1 = (f32[3,128,128]{2,1,0:T(8,128)}, f32[96,128]{1,0:T(8,128)S(1)}, f32[48,128]{1,0:T(8,128)S(1)}, f32[16,128]{1,0:T(8,128)S(1)}, f32[16,128]{1,0:T(8,128...) custom-call(f32[3,128,128]{2,1,0:T(8,128)S(1)} %bitcast.9, ...), custom_call_target="tpu_custom_call" | custom-call | flops 10000000 | bytes 900000 | tf_op jit(solution)/shard_map/first/pallas_call | solution.py:468
  100.3 0.0 copy-start.7
  100.3 0.0 copy-done.8
  100.3 0.7 copy-done.7
  101.0 0.4 patch.1
  101.5 100.4 %psum.7.tiles = f32[8,128]{1,0:T(8,128)S(1)} all-reduce(f32[8,128]{1,0:T(8,128)S(1)} %patch.1), channel_id=1, replica_groups=mesh['normal'=4,'strike'=16,'depth'=8] {'normal','strike','depth'}, use_global_device_ids=true, to_apply=%region_0.0 | all-reduce | flops 1024 | bytes 8192 | tf_op jit(solution)/shard_map/psum | solution.py:479
  201.9 0.7 final.1
  202.5 12.7 %all_gather.23.gz = f32[128,128]{1,0:T(8,128)S(1)} all-gather(f32[16,128]{1,0:T(8,128)S(1)} %get-tuple-element.23.hz), channel_id=1, replica_groups=mesh['normal'=4,'strike'=16,'depth'=8] {'depth'}, dimensions={0}, use_global_device_ids=true | all-gather | bytes 73728 | tf_op jit(solution)/shard_map/all_gather | solution.py:453
  215.2 0.0 copy-start.5
  215.2 14.1 %all_gather.21.gx = f32[384,128]{1,0:T(8,128)S(1)} all-gather(f32[96,128]{1,0:T(8,128)S(1)} %get-tuple-element.21), channel_id=1, replica_groups=mesh['normal'=4,'strike'=16,'depth'=8] {'normal'}, dimensions={0}, use_global_device_ids=true | all-gather | bytes 245760 | tf_op jit(solution)/shard_map/all_gather | solution.py:453
  229.3 0.0 copy-start.1
  229.3 0.0 copy-start.3
  229.3 53.9 %all_gather.22.gy = f32[768,128]{1,0:T(8,128)S(1)} all-gather(f32[48,128]{1,0:T(8,128)S(1)} %get-tuple-element.22), channel_id=1, replica_groups=mesh['normal'=4,'strike'=16,'depth'=8] {'strike'}, dimensions={0}, use_global_device_ids=true | all-gather | bytes 417792 | tf_op jit(solution)/shard_map/all_gather | solution.py:453
  283.3 0.0 copy-done.5
  283.3 0.0 copy-done.1
  283.3 0.0 copy-done.3
  283.3 3.5 %second.1 = f32[3,128,128]{2,1,0:T(8,128)} custom-call(f32[3,128,128]{2,1,0:T(8,128)S(1)} %copy-done.5, f32[3,128,128]{2,1,0:T(8,128)S(1)} %bitcast.10, bf16[128,128]{1,0:T(8,128)(2,1)S(1)} %bitcast.13, bf16[128,128]{1,0:T(8,128)(2,1)S(1)} %bitcast.17, f32[384,128]{1,0:T(8,128)S(1)} %all_gather.21.gx, f32[768,128]{1,0:T(8,128)S(1)} %all_gather.22.gy, ...), custom_call_target="tpu_custom_call" | custom-call | flops 10000000 | bytes 900000 | tf_op jit(solution)/shard_map/second/pallas_call | solution.py:482
Async XLA Ops:
  0.6 0.9 copy-start
  1.6 0.8 copy-start.2
  32.6 64.0 %copy-start.4 = (f32[3,8,16,128]{3,2,1,0:T(8,128)S(1)}, f32[3,8,16,128]{3,2,1,0:T(8,128)}, u32[]{:S(2)}) copy-start(f32[3,8,16,128]{3,2,1,0:T(8,128)} %param.7) | copy-start | bytes 589828
  32.6 64.0 %copy-start.6 = (bf16[8,16,128]{2,1,0:T(8,128)(2,1)S(1)}, bf16[8,16,128]{2,1,0:T(8,128)(2,1)}, u32[]{:S(2)}) copy-start(bf16[8,16,128]{2,1,0:T(8,128)(2,1)} %param.9) | copy-start | bytes 98308
  96.6 3.7 %copy-start.8 = (s32[1,1,256]{2,1,0:T(1,128)S(1)}, s32[1,1,256]{2,1,0:T(1,128)}, u32[]{:S(2)}) copy-start(s32[1,1,256]{2,1,0:T(1,128)} %param.11) | copy-start | bytes 3076
  100.3 0.7 copy-start.7
  215.2 68.0 %copy-start.5 = (f32[3,128,128]{2,1,0:T(8,128)S(1)}, f32[3,128,128]{2,1,0:T(8,128)}, u32[]{:S(2)}) copy-start(f32[3,128,128]{2,1,0:T(8,128)} %get-tuple-element.20.now) | copy-start | bytes 589828
  229.3 54.0 %copy-start.1 = (f32[3,8,16,128]{3,2,1,0:T(8,128)S(1)}, f32[3,8,16,128]{3,2,1,0:T(8,128)}, u32[]{:S(2)}) copy-start(f32[3,8,16,128]{3,2,1,0:T(8,128)} %param.6) | copy-start | bytes 589828
  229.3 54.0 %copy-start.3 = (bf16[8,16,128]{2,1,0:T(8,128)(2,1)S(1)}, bf16[8,16,128]{2,1,0:T(8,128)(2,1)}, u32[]{:S(2)}) copy-start(bf16[8,16,128]{2,1,0:T(8,128)(2,1)} %param.8) | copy-start | bytes 98308

commit v3 on v2

--- a/solution.py
+++ b/solution.py
@@ -141,23 +141,45 @@
         dst[pl.ds(x * NYL, NYL), :] = src[pl.ds(x * NYL, NYL), :].astype(F32)
 
 
-def sides(ref, up, down):
-    return ref.at[pl.ds(0, up)], ref.at[pl.ds(up, down)]
-
-
-def neighbours(gathered, index, count, up, down, low, high):
-    below = pl.multiple_of(jnp.maximum(index - 1, 0) * (up + down), 8)
-    above = pl.multiple_of(jnp.minimum(index + 1, count - 1) * (up + down) + up, 8)
-    low[...] = jnp.where(index > 0, gathered[pl.ds(below, up), :], 0.0)
-    high[...] = jnp.where(index < count - 1, gathered[pl.ds(above, down), :], 0.0)
-
-
 FIRST_ROWS = ((112, 64), (56, 32), (8, 8))
 SECOND_ROWS = ((48, 48), (24, 24), (8, 8))
 
 
-def pack_kernel(now, rig, hx, hy, hz, rw):
-    (xu, xd), (yu, yd), (zu, zd) = (sides(ref, *n) for ref, n in zip((hx, hy, hz), FIRST_ROWS))
+def place():
+    return tuple(lax.axis_index(axis) for axis in ("normal", "strike", "depth"))
+
+
+def paired(index, up, down, near, far):
+    even = (index & 1) == 0
+    rows = pl.ds(0, down.shape[0])
+    near[...] = up[...]
+    far[...] = up[...]
+    near[rows, :] = jnp.where(even, up[rows, :], down[...])
+    far[rows, :] = jnp.where(even, down[...], up[rows, :])
+
+
+def unpaired(index, near, far, low, high):
+    even = (index & 1) == 0
+    rows = pl.ds(0, high.shape[0])
+    low[...] = jnp.where(even, far[...], near[...])
+    high[...] = jnp.where(even, near[rows, :], far[rows, :])
+
+
+def beside(index, count, got, stride, low, high):
+    below = pl.multiple_of(jnp.maximum(index - 1, 0) * stride, 8)
+    above = pl.multiple_of(jnp.minimum(index + 1, count - 1) * stride, 8)
+    low[...] = jnp.where(index > 0, got[pl.ds(below, low.shape[0]), :], 0.0)
+    high[...] = jnp.where(index < count - 1, got[pl.ds(above, high.shape[0]), :], 0.0)
+
+
+def pack_kernel(
+    now_hbm, rig_hbm, xa, xb, ya, yb, za, zb, zd, now, rig, rw, xu, xd, yu, yd, zu, sems,
+):
+    copies = [pltpu.make_async_copy(rig_hbm, rig, sems.at[0]), pltpu.make_async_copy(now_hbm, now, sems.at[1])]
+    for copy in copies:
+        copy.start()
+    for copy in copies:
+        copy.wait()
     widen(rig, rw)
     lane = lane_of()
     for half in range(2):
@@ -188,6 +210,10 @@
         lane < 64, interleaved(parts + [open_scale(r)], lane, 0), interleaved(grads + [None], lane, 64)
     )
     zd[...] = first_lanes(lambda c, rows: now[c, rows, :], lambda rows: rw[rows, :], lane)
+    index = place()
+    paired(index[0], xu, xd, xa, xb)
+    paired(index[1], yu, yd, ya, yb)
+    paired(index[2], zu, zd, za, zb)
 
 
 def from_fourth(tile, lane):
@@ -299,16 +325,15 @@
 
 
 def first_kernel(
-    counts, now, prev, rig, rho, gx, gy, gz, hz,
-    out, hx2, hy2, hz2, mx, my, mz, slip, xd, yd, zd,
-    rw, scale, acc, early, xu, yu, zu,
+    counts, now, prev, rig, rho, xa, xb, ya, yb, za, zb, zd_own, nodes, ids,
+    out, kept, to_normal, ya2, yb2, zu2, zd2, mx, my, mz, xd, yd, zd,
+    rw, scale, acc, early, slip, xu, yu, zu, xu2, xd2, yu2, yd2,
 ):
     middle = counts[0] // 2
-    index = (lax.axis_index("normal"), lax.axis_index("strike"), lax.axis_index("depth"))
-    for d, (ref, low, high) in enumerate(((gx, xu, xd), (gy, yu, yd), (gz, zu, zd))):
-        neighbours(ref, index[d], counts[d], *FIRST_ROWS[d], low, high)
-    zd_own = hz.at[pl.ds(8, 8)]
-    (xu2, xd2), (yu2, yd2), (zu2, zd2) = (sides(ref, *n) for ref, n in zip((hx2, hy2, hz2), SECOND_ROWS))
+    index = place()
+    unpaired(index[0], xa, xb, xu, xd)
+    unpaired(index[1], ya, yb, yu, yd)
+    unpaired(index[2], za, zb, zu, zd)
     widen(rig, rw)
     step_scale(rho, scale)
     lane = lane_of()
@@ -335,6 +360,7 @@
 
     def store(c, x, rows, plane, after):
         out[c, rows, :] = after
+        kept[c, rows, :] = after
         if x == 0:
             xd2[plane, :] = after
 
@@ -374,16 +400,39 @@
         sent.append(part + kappa * below * grad)
     zu2[...] = interleaved(sent + [None], lane, 0)
     zd2[...] = first_lanes(lambda c, rows: out[c, rows, :], None, lane)
+    paired(index[1], yu2, yd2, ya2, yb2)
+    tile = patch_tile(counts[2], slip[...], nodes[...], ids[...])
+    for n in range(counts[0]):
+        to_normal[pl.ds(56 * n, 48), :] = jnp.where(n > index[0], xu2[...], xd2[...])
+        to_normal[pl.ds(56 * n + 48, 8), :] = tile
+
+
+def relay_kernel(counts, got, zu2, zd2, to_depth):
+    index = lax.axis_index("depth")
+    tile = got[pl.ds(48, 8), :]
+    for n in range(1, counts[0]):
+        tile = tile + got[pl.ds(56 * n + 48, 8), :]
+    for d in range(counts[2]):
+        to_depth[pl.ds(16 * d, 8), :] = jnp.where(d > index, zu2[...], zd2[...])
+        to_depth[pl.ds(16 * d + 8, 8), :] = jnp.broadcast_to(tile[d : d + 1, :], (8, NZL))
+
+
+def sum_kernel(counts, got, to_strike):
+    row = got[pl.ds(8, 8), :]
+    for d in range(1, counts[2]):
+        row = row + got[pl.ds(16 * d + 8, 8), :]
+    for half in range(counts[1] // 8 or 1):
+        to_strike[pl.ds(8 * half, min(8, counts[1])), :] = row[: min(8, counts[1]), :]
 
 
 def second_kernel(
-    counts, now, prev, rig, rho, gx, gy, gz, hz, mx, my, mz, xd, yd, zd,
+    counts, now, prev, rig, rho, got_x, ya2, yb2, got_z, zd2_own, mx, my, mz, xd, yd, zd,
     out, rw, scale, acc, xu2, xd2, yu2, yd2, zu2, zd2,
 ):
-    index = (lax.axis_index("normal"), lax.axis_index("strike"), lax.axis_index("depth"))
-    for d, (ref, low, high) in enumerate(((gx, xu2, xd2), (gy, yu2, yd2), (gz, zu2, zd2))):
-        neighbours(ref, index[d], counts[d], *SECOND_ROWS[d], low, high)
-    zd2_own = hz.at[pl.ds(8, 8)]
+    index = place()
+    beside(index[0], counts[0], got_x, 56, xu2, xd2)
+    unpaired(index[1], ya2, yb2, yu2, yd2)
+    beside(index[2], counts[2], got_z, 16, zu2, zd2)
     widen(rig, rw)
     step_scale(rho, scale)
     closing_z = zu2[...] + mz[...] * zd2_own[...]
@@ -403,13 +452,11 @@
     )
 
 
-def patch_kernel(count_d, slip, nodes, ids, out):
-    pairs = nodes.shape[-1]
-    node = nodes[...]
+def patch_tile(count_d, slip, node, patch):
+    pairs = node.shape[-1]
     hot_z = (lax.broadcasted_iota(jnp.int32, (NZL, pairs), 0) == (node & (NZL - 1))).astype(F32)
-    at_z = jnp.dot(slip[...], hot_z, precision=HIGHEST, preferred_element_type=F32)
+    at_z = jnp.dot(slip, hot_z, precision=HIGHEST, preferred_element_type=F32)
     row_y = lax.broadcasted_iota(jnp.int32, (NYL, pairs), 0) == (node >> 7)
-    patch = ids[...]
     owner = patch >> 1
     owner_d = owner & (count_d - 1)
     slot = ((owner >> (count_d.bit_length() - 1)) << 1) + (patch & 1)
@@ -420,7 +467,7 @@
         spread.append(jnp.where(hot_slot, picked, 0.0))
     spread.append(jnp.zeros((32, pairs), F32))
     hot_d = (lax.broadcasted_iota(jnp.int32, (8, pairs), 0) == owner_d).astype(F32)
-    out[...] = lax.dot_general(
+    return lax.dot_general(
         hot_d, jnp.concatenate(spread, axis=0), (((1,), (1,)), ((), ())), precision=HIGHEST,
         preferred_element_type=F32,
     )
@@ -428,8 +475,7 @@
 
 def final_kernel(tiles, out):
     mine = lax.axis_index("strike") * 2
-    row = lax.broadcasted_iota(jnp.int32, (8, NZL), 0) == lax.axis_index("depth")
-    summed = jnp.sum(jnp.where(row, tiles[...], 0.0), axis=0, keepdims=True)
+    summed = jnp.sum(tiles[...], axis=0, keepdims=True)
     lane = lax.broadcasted_iota(jnp.int32, (2, NZL), 1)
     place = lax.broadcasted_iota(jnp.int32, (2, NZL), 0)
     for c in range(3):
@@ -437,53 +483,68 @@
         out[:, pl.ds(c, 1)] = jnp.sum(jnp.where(hit, summed, 0.0), axis=1, keepdims=True)
 
 
-def call(kernel, name, outs, scratch=(), flops=0, moved=0):
+def call(kernel, name, outs, scratch=(), flops=0, moved=0, in_specs=None):
+    specs = {} if in_specs is None else {"in_specs": in_specs}
     return pl.pallas_call(
         kernel,
         out_shape=[jax.ShapeDtypeStruct(shape, F32) for shape in outs],
-        scratch_shapes=[pltpu.VMEM(shape, F32) for shape in scratch],
+        scratch_shapes=[pltpu.VMEM(shape, F32) if isinstance(shape, tuple) else shape for shape in scratch],
         compiler_params=pltpu.CompilerParams(vmem_limit_bytes=16 * 2**20),
         cost_estimate=pl.CostEstimate(flops=flops, bytes_accessed=moved, transcendentals=0),
         name=name,
+        **specs,
     )
 
 
-def exchange(messages):
-    return [
-        lax.all_gather(message, axis, axis=0, tiled=True)
-        for message, axis in zip(messages, ("normal", "strike", "depth"))
-    ]
+def swap_near(value, axis):
+    return lax.ppermute(value, axis, [(i, i ^ 1) for i in range(lax.axis_size(axis))])
+
+
+def swap_far(value, axis):
+    lower = range(1, lax.axis_size(axis) - 1, 2)
+    return lax.ppermute(value, axis, [(i, i + 1) for i in lower] + [(i + 1, i) for i in lower])
 
 
 def local(field_now, field_prev, rigidity, density, fault_nodes, patch_ids):
     axes = ("normal", "strike", "depth")
     counts = tuple(lax.axis_size(a) for a in axes)
-    flat = (3, ROWS, NZL)
+    flat, block, tile = (3, ROWS, NZL), (ROWS, NZL), (8, NZL)
     now, prev = field_now.reshape(flat), field_prev.reshape(flat)
-    rig, rho = rigidity.reshape(ROWS, NZL), density.reshape(ROWS, NZL)
-    first_sizes = [(up + down, NZL) for up, down in FIRST_ROWS]
-    second_sizes = [(up + down, NZL) for up, down in SECOND_ROWS]
-    sent = call(pack_kernel, "pack", first_sizes, [(ROWS, NZL)], flops=2_000_000, moved=400_000)(now, rig)
-    got = exchange(sent)
-    mid, *rest = call(
+    rig, rho = rigidity.reshape(block), density.reshape(block)
+    nodes, ids = fault_nodes.reshape(1, -1), patch_ids.reshape(1, -1)
+    ups = [(up, NZL) for up, _ in FIRST_ROWS]
+    downs = [(down, NZL) for _, down in FIRST_ROWS]
+    xa, xb, ya, yb, za, zb, zd = call(
+        pack_kernel, "pack", [shape for shape in ups for _ in range(2)] + [tile],
+        [pltpu.VMEM(flat, F32), pltpu.VMEM(block, jnp.bfloat16), block, ups[0], downs[0], ups[1], downs[1], ups[2],
+         pltpu.SemaphoreType.DMA((2,))],
+        flops=2_000_000, moved=400_000, in_specs=[pl.BlockSpec(memory_space=pl.ANY)] * 2,
+    )(now, rig)
+    ya, yb = swap_near(ya, "strike"), swap_far(yb, "strike")
+    xa, xb = swap_near(xa, "normal"), swap_far(xb, "normal")
+    zb, za = swap_far(zb, "depth"), swap_near(za, "depth")
+    mid, kept, to_normal, ya2, yb2, zu2, zd2, *held = call(
         functools.partial(first_kernel, counts), "first",
-        [flat] + second_sizes + [(16, NZL), (8, NZL), (8, NZL), (48, NZL)] + [(n[1], NZL) for n in FIRST_ROWS],
-        [(ROWS, NZL), (ROWS, NZL), flat, (48, NZL)] + [(n[0], NZL) for n in FIRST_ROWS],
+        [flat, flat, (56 * counts[0], NZL), (24, NZL), (24, NZL), tile, tile, (16, NZL), tile, tile] + downs,
+        [block, block, flat, (48, NZL), (48, NZL)] + ups + [(48, NZL), (48, NZL), (24, NZL), (24, NZL)],
         flops=10_000_000, moved=900_000,
-    )(now, prev, rig, rho, *got, sent[2])
-    sent2, weights, slip, kept = rest[:3], rest[3:6], rest[6], rest[7:]
-    nodes, ids = fault_nodes.reshape(1, -1), patch_ids.reshape(1, -1)
-    (tile,) = call(
-        functools.partial(patch_kernel, counts[2]), "patch", [(8, NZL)], flops=10_000_000, moved=60_000,
-    )(slip, nodes, ids)
-    sums = lax.psum(tile, axes)
-    got2 = exchange(sent2)
-    (share,) = call(final_kernel, "final", [(2, 3)], flops=10_000, moved=10_000)(sums)
+    )(now, prev, rig, rho, xa, xb, ya, yb, za, zb, zd, nodes, ids)
+    ya2, yb2 = swap_near(ya2, "strike"), swap_far(yb2, "strike")
+    got_x = lax.all_to_all(to_normal, "normal", 0, 0, tiled=True)
+    (to_depth,) = call(
+        functools.partial(relay_kernel, counts), "relay", [(16 * counts[2], NZL)], flops=10_000, moved=200_000,
+    )(got_x, zu2, zd2)
+    got_z = lax.all_to_all(to_depth, "depth", 0, 0, tiled=True)
+    (to_strike,) = call(
+        functools.partial(sum_kernel, counts), "add", [(counts[1], NZL)], flops=10_000, moved=80_000,
+    )(got_z)
+    got_s = lax.all_to_all(to_strike, "strike", 0, 0, tiled=True)
+    (share,) = call(final_kernel, "final", [(2, 3)], flops=10_000, moved=10_000)(got_s)
     (following,) = call(
         functools.partial(second_kernel, counts), "second", [flat],
-        [(ROWS, NZL), (ROWS, NZL), flat] + [(n, NZL) for pair in SECOND_ROWS for n in pair],
+        [block, block, flat] + [(n, NZL) for pair in SECOND_ROWS for n in pair],
         flops=10_000_000, moved=900_000,
-    )(mid, now, rig, rho, *got2, sent2[2], *weights, *kept)
+    )(kept, now, rig, rho, got_x, ya2, yb2, got_z, zd2, *held)
     return following.reshape(field_now.shape), mid.reshape(field_now.shape), share
 
 

time: 287 us -> 84.7 us (0.30)
  the two profiles are of different devices: /device:TPU:2 before, /device:TPU:24 now
where the time goes in v3:
time: 84.7 us; the launch traced here: 84.1 us
  starting transfers between devices  40.8 us (48%)
  blocking collectives  26.2 us (31%)
  Pallas kernels  9.06 us (11%)
  waiting for transfers between devices  4.85 us (6%)
  local copies, waits for them, and re-layouts  2.36 us (3%)
    ppermute x4, starting transfers between devices, swap_far(): lax.ppermute(value, axis, [(i, i + 1) for i in lower] + [(i + 1, i) for i...  18.8 us
    all_to_all x1, blocking collectives, local(): got_z = lax.all_to_all(to_depth, 'depth', 0, 0, tiled=True)  14.2 us
    all_to_all x1, blocking collectives, local(): got_x = lax.all_to_all(to_normal, 'normal', 0, 0, tiled=True)  12 us
    ppermute x4, starting transfers between devices, swap_near(): lax.ppermute(value, axis, [(i, i ^ 1) for i in range(lax.axis_size(axis))])  11.2 us
    all_to_all x1, starting transfers between devices, local(): got_s = lax.all_to_all(to_strike, 'strike', 0, 0, tiled=True)  10.8 us
    pallas_call x1, Pallas kernels, local(): call(functools.partial(first_kernel, counts), 'first', [flat, flat, (56 *...  3.74 us
    ppermute x4, waiting for transfers between devices, swap_far(): lax.ppermute(value, axis, [(i, i + 1) for i in lower] + [(i + 1, i) for i...  3.71 us
    pallas_call x1, Pallas kernels, local(): call(functools.partial(second_kernel, counts), 'second', [flat], [block,...  3.44 us
  transfers between devices with their start and end apart: 9, of which 2 were waited for; matrix products, arithmetic and copies ran while one was open for 0% of the time, Pallas kernels for 4%

profile of v3, /device:TPU:24, one launch (start us, length us, event | category | flops | bytes accessed | tf_op | source)
XLA Modules:
  0.0 84.1 jit_solution(13296397505791947112)
XLA Ops:
  0.6 0.0 copy-start
  0.6 0.9 %copy-done = f32[3,8,16,128]{3,2,1,0:T(8,128)S(1)} copy-done((f32[3,8,16,128]{3,2,1,0:T(8,128)S(1)}, f32[3,8,16,128]{3,2,1,0:T(8,128)}, u32[]{:S(2)}) %copy-start) | copy-done | bytes 196632
  1.6 0.8 copy-done.2
  2.3 0.6 pack.1
  2.9 3.8 %collective-permute-start = (f32[112,128]{1,0:T(8,128)S(1)}, f32[112,128]{1,0:T(8,128)S(1)}, u32[]{:S(2)}, u32[]{:S(2)}) collective-permute-start(f32[112,128]{1,0:T(8,128)S(1)} %get-tuple-element.23), channel_id=1, source_target_pairs={{0,128},{128,0},{256,384},{384,256},{1,129},{129,1},{257,385},{385... | collective-permute-start | bytes 172040 | tf_op jit(solution)/shard_map/ppermute | solution.py:500
  6.8 0.7 collective-permute-start.1
  7.4 2.7 %collective-permute-start.2 = (f32[56,128]{1,0:T(8,128)S(1)}, f32[56,128]{1,0:T(8,128)S(1)}, u32[]{:S(2)}, u32[]{:S(2)}) collective-permute-start(f32[56,128]{1,0:T(8,128)S(1)} %get-tuple-element.25), channel_id=1, source_target_pairs={{0,8},{8,0},{16,24},{24,16},{32,40},{40,32},{48,56},{56,48},{64,72... | collective-permute-start | bytes 86024 | tf_op jit(solution)/shard_map/ppermute | solution.py:500
  10.1 9.6 %collective-permute-start.3 = (f32[56,128]{1,0:T(8,128)S(1)}, f32[56,128]{1,0:T(8,128)S(1)}, u32[]{:S(2)}, u32[]{:S(2)}) collective-permute-start(f32[56,128]{1,0:T(8,128)S(1)} %get-tuple-element.26), channel_id=1, source_target_pairs={{8,16},{24,32},{40,48},{56,64},{72,80},{88,96},{104,112},{16,8},{3... | collective-permute-start | bytes 86024 | tf_op jit(solution)/shard_map/ppermute | solution.py:505
  19.7 1.9 %collective-permute-start.4 = (f32[8,128]{1,0:T(8,128)S(1)}, f32[8,128]{1,0:T(8,128)S(1)}, u32[]{:S(2)}, u32[]{:S(2)}) collective-permute-start(f32[8,128]{1,0:T(8,128)S(1)} %get-tuple-element.27), channel_id=1, source_target_pairs={{0,1},{1,0},{2,3},{3,2},{4,5},{5,4},{6,7},{7,6},{8,9},{9,8},{10,11... | collective-permute-start | bytes 12296 | tf_op jit(solution)/shard_map/ppermute | solution.py:500
  21.6 1.1 %collective-permute-done.4.za = f32[8,128]{1,0:T(8,128)S(1)} collective-permute-done((f32[8,128]{1,0:T(8,128)S(1)}, f32[8,128]{1,0:T(8,128)S(1)}, u32[]{:S(2)}, u32[]{:S(2)}) %collective-permute-start.4) | collective-permute-done | bytes 4128 | tf_op jit(solution)/shard_map/ppermute | solution.py:500
  22.8 0.7 collective-permute-start.5
  23.4 0.0 collective-permute-done.5.zb
  23.4 0.0 collective-permute-done.2.ya
  23.4 0.0 collective-permute-done.3.yb
  23.5 0.0 collective-permute-done.xa
  23.5 0.0 collective-permute-done.1.xb
  23.5 0.0 copy-start.7
  23.5 0.0 copy-start.6
  23.5 0.6 copy-done.7
  24.2 0.0 copy-done.6
  24.2 3.7 %first.1 = (f32[3,128,128]{2,1,0:T(8,128)}, f32[3,128,128]{2,1,0:T(8,128)S(1)}, f32[224,128]{1,0:T(8,128)S(1)}, f32[24,128]{1,0:T(8,128)S(1)}, f32[24,128]{1,0:T...) custom-call(f32[3,128,128]{2,1,0:T(8,128)S(1)} %bitcast.17, ...), custom_call_target="tpu_custom_call" | custom-call | flops 10000000 | bytes 900000 | tf_op jit(solution)/shard_map/first/pallas_call | solution.py:526
  27.9 12.0 %all_to_all.33 = f32[4,56,128]{2,1,0:T(8,128)S(1)} all-to-all(f32[4,56,128]{2,1,0:T(8,128)S(1)} %bitcast.30), channel_id=1, replica_groups=mesh['normal'=4,'strike'=16,'depth'=8] {'normal'}, dimensions={0} | all-to-all | bytes 229376 | tf_op jit(solution)/shard_map/all_to_all | solution.py:533
  40.0 14.2 %all_to_all.34 = f32[8,16,128]{2,1,0:T(8,128)S(1)} all-to-all(f32[8,16,128]{2,1,0:T(8,128)S(1)} %bitcast.26), channel_id=1, replica_groups=mesh['normal'=4,'strike'=16,'depth'=8] {'depth'}, dimensions={0} | all-to-all | bytes 131072 | tf_op jit(solution)/shard_map/all_to_all | solution.py:537
  54.2 0.6 add.1
  54.8 10.8 %all-to-all-start.2 = ((f32[16,1,128]{2,1,0:T(1,128)}), f32[16,1,128]{2,1,0:T(1,128)S(1)}, u32[]{:S(2)}, u32[]{:S(2)}) async-start(f32[16,1,128]{2,1,0:T(1,128)} %bitcast.13), calls=%async_computation.2 | async-start | bytes 16384 | tf_op jit(solution)/shard_map/all_to_all | solution.py:541
  65.6 2.8 %collective-permute-start.6 = (f32[24,128]{1,0:T(8,128)S(1)}, f32[24,128]{1,0:T(8,128)S(1)}, u32[]{:S(2)}, u32[]{:S(2)}) collective-permute-start(f32[24,128]{1,0:T(8,128)S(1)} %get-tuple-element.32), channel_id=1, source_target_pairs={{0,8},{8,0},{16,24},{24,16},{32,40},{40,32},{48,56},{56,48},{64,72... | collective-permute-start | bytes 36872 | tf_op jit(solution)/shard_map/ppermute | solution.py:500
  68.4 7.9 %collective-permute-start.7 = (f32[24,128]{1,0:T(8,128)S(1)}, f32[24,128]{1,0:T(8,128)S(1)}, u32[]{:S(2)}, u32[]{:S(2)}) collective-permute-start(f32[24,128]{1,0:T(8,128)S(1)} %get-tuple-element.33), channel_id=1, source_target_pairs={{8,16},{24,32},{40,48},{56,64},{72,80},{88,96},{104,112},{16,8},{3... | collective-permute-start | bytes 36872 | tf_op jit(solution)/shard_map/ppermute | solution.py:505
  76.3 0.0 collective-permute-done.6.ya2
  76.3 3.7 %collective-permute-done.7.yb2 = f32[24,128]{1,0:T(8,128)S(1)} collective-permute-done((f32[24,128]{1,0:T(8,128)S(1)}, f32[24,128]{1,0:T(8,128)S(1)}, u32[]{:S(2)}, u32[]{:S(2)}) %collective-permute-start.7) | collective-permute-done | bytes 12320 | tf_op jit(solution)/shard_map/ppermute | solution.py:505
  80.0 3.4 %second.1 = f32[3,128,128]{2,1,0:T(8,128)} custom-call(f32[3,128,128]{2,1,0:T(8,128)S(1)} %get-tuple-element.30.now, f32[3,128,128]{2,1,0:T(8,128)S(1)} %bitcast.18, bf16[128,128]{1,0:T(8,128)(2,1)S(1)} %bitcast.25, bf16[128,128]{1,0:T(8,128)(2,1)S(1)} %bitcast.29, f32[224,128]{1,0:T(8,128)S(1)} %bitcast.20, f32[24,128]{1,0:T(8,128)S(1)} %collective-permute-done.6.ya2, ...), custom_call_target="tpu_custom_call" | custom-call | flops 10000000 | bytes 900000 | tf_op jit(solution)/shard_map/second/pallas_call | solution.py:543
  83.4 0.0 all-to-all-done.2
  83.4 0.7 final.1
  (10 shorter events, 0.0 us)
Async XLA Ops:
  0.6 0.9 %copy-start = (f32[3,8,16,128]{3,2,1,0:T(8,128)S(1)}, f32[3,8,16,128]{3,2,1,0:T(8,128)}, u32[]{:S(2)}) copy-start(f32[3,8,16,128]{3,2,1,0:T(8,128)} %param.6) | copy-start | bytes 589828
  1.6 0.8 copy-start.2
  2.3 21.2 %copy-start.4 = (f32[3,8,16,128]{3,2,1,0:T(8,128)S(1)}, f32[3,8,16,128]{3,2,1,0:T(8,128)}, u32[]{:S(2)}) copy-start(f32[3,8,16,128]{3,2,1,0:T(8,128)} %param.7) | copy-start | bytes 589828
  2.3 21.2 %copy-start.5 = (bf16[8,16,128]{2,1,0:T(8,128)(2,1)S(1)}, bf16[8,16,128]{2,1,0:T(8,128)(2,1)}, u32[]{:S(2)}) copy-start(bf16[8,16,128]{2,1,0:T(8,128)(2,1)} %param.9) | copy-start | bytes 98308
  2.9 20.5 %collective-permute-start = (f32[112,128]{1,0:T(8,128)S(1)}, f32[112,128]{1,0:T(8,128)S(1)}, u32[]{:S(2)}, u32[]{:S(2)}) collective-permute-start(f32[112,128]{1,0:T(8,128)S(1)} %get-tuple-element.23), channel_id=1, source_target_pairs={{0,128},{128,0},{256,384},{384,256},{1,129},{129,1},{257,385},{385... | collective-permute-start | bytes 172040 | tf_op jit(solution)/shard_map/ppermute | solution.py:500
  6.8 16.7 %collective-permute-start.1 = (f32[112,128]{1,0:T(8,128)S(1)}, f32[112,128]{1,0:T(8,128)S(1)}, u32[]{:S(2)}, u32[]{:S(2)}) collective-permute-start(f32[112,128]{1,0:T(8,128)S(1)} %get-tuple-element.24), channel_id=1, source_target_pairs={{128,256},{256,128},{129,257},{257,129},{130,258},{258,130},{131,2... | collective-permute-start | bytes 172040 | tf_op jit(solution)/shard_map/ppermute | solution.py:505
  7.4 16.0 %collective-permute-start.2 = (f32[56,128]{1,0:T(8,128)S(1)}, f32[56,128]{1,0:T(8,128)S(1)}, u32[]{:S(2)}, u32[]{:S(2)}) collective-permute-start(f32[56,128]{1,0:T(8,128)S(1)} %get-tuple-element.25), channel_id=1, source_target_pairs={{0,8},{8,0},{16,24},{24,16},{32,40},{40,32},{48,56},{56,48},{64,72... | collective-permute-start | bytes 86024 | tf_op jit(solution)/shard_map/ppermute | solution.py:500
  10.1 13.3 %collective-permute-start.3 = (f32[56,128]{1,0:T(8,128)S(1)}, f32[56,128]{1,0:T(8,128)S(1)}, u32[]{:S(2)}, u32[]{:S(2)}) collective-permute-start(f32[56,128]{1,0:T(8,128)S(1)} %get-tuple-element.26), channel_id=1, source_target_pairs={{8,16},{24,32},{40,48},{56,64},{72,80},{88,96},{104,112},{16,8},{3... | collective-permute-start | bytes 86024 | tf_op jit(solution)/shard_map/ppermute | solution.py:505
  19.7 3.1 %collective-permute-start.4 = (f32[8,128]{1,0:T(8,128)S(1)}, f32[8,128]{1,0:T(8,128)S(1)}, u32[]{:S(2)}, u32[]{:S(2)}) collective-permute-start(f32[8,128]{1,0:T(8,128)S(1)} %get-tuple-element.27), channel_id=1, source_target_pairs={{0,1},{1,0},{2,3},{3,2},{4,5},{5,4},{6,7},{7,6},{8,9},{9,8},{10,11... | collective-permute-start | bytes 12296 | tf_op jit(solution)/shard_map/ppermute | solution.py:500
  22.8 0.7 collective-permute-start.5
  23.5 0.7 copy-start.7
  23.5 0.7 copy-start.6
  39.9 40.1 %copy-start.1 = (f32[3,8,16,128]{3,2,1,0:T(8,128)S(1)}, f32[3,8,16,128]{3,2,1,0:T(8,128)}, u32[]{:S(2)}) copy-start(f32[3,8,16,128]{3,2,1,0:T(8,128)} %param.6) | copy-start | bytes 589828
  54.8 25.2 %copy-start.3 = (bf16[8,16,128]{2,1,0:T(8,128)(2,1)S(1)}, bf16[8,16,128]{2,1,0:T(8,128)(2,1)}, u32[]{:S(2)}) copy-start(bf16[8,16,128]{2,1,0:T(8,128)(2,1)} %param.8) | copy-start | bytes 98308
  54.8 28.7 %all-to-all-start.2 = ((f32[16,1,128]{2,1,0:T(1,128)}), f32[16,1,128]{2,1,0:T(1,128)S(1)}, u32[]{:S(2)}, u32[]{:S(2)}) async-start(f32[16,1,128]{2,1,0:T(1,128)} %bitcast.13), calls=%async_computation.2 | async-start | bytes 16384 | tf_op jit(solution)/shard_map/all_to_all | solution.py:541
  65.6 10.7 %collective-permute-start.6 = (f32[24,128]{1,0:T(8,128)S(1)}, f32[24,128]{1,0:T(8,128)S(1)}, u32[]{:S(2)}, u32[]{:S(2)}) collective-permute-start(f32[24,128]{1,0:T(8,128)S(1)} %get-tuple-element.32), channel_id=1, source_target_pairs={{0,8},{8,0},{16,24},{24,16},{32,40},{40,32},{48,56},{56,48},{64,72... | collective-permute-start | bytes 36872 | tf_op jit(solution)/shard_map/ppermute | solution.py:500
  68.4 11.6 %collective-permute-start.7 = (f32[24,128]{1,0:T(8,128)S(1)}, f32[24,128]{1,0:T(8,128)S(1)}, u32[]{:S(2)}, u32[]{:S(2)}) collective-permute-start(f32[24,128]{1,0:T(8,128)S(1)} %get-tuple-element.33), channel_id=1, source_target_pairs={{8,16},{24,32},{40,48},{56,64},{72,80},{88,96},{104,112},{16,8},{3... | collective-permute-start | bytes 36872 | tf_op jit(solution)/shard_map/ppermute | solution.py:505

commit v4 on v3

--- a/solution.py
+++ b/solution.py
@@ -141,8 +141,8 @@
         dst[pl.ds(x * NYL, NYL), :] = src[pl.ds(x * NYL, NYL), :].astype(F32)
 
 
-FIRST_ROWS = ((112, 64), (56, 32), (8, 8))
-SECOND_ROWS = ((48, 48), (24, 24), (8, 8))
+X_UP, X_DOWN = 112, 64
+Y_UP, Y_DOWN = 136, 64
 
 
 def place():
@@ -172,9 +172,7 @@
     high[...] = jnp.where(index < count - 1, got[pl.ds(above, high.shape[0]), :], 0.0)
 
 
-def pack_kernel(
-    now_hbm, rig_hbm, xa, xb, ya, yb, za, zb, zd, now, rig, rw, xu, xd, yu, yd, zu, sems,
-):
+def pack_kernel(now_hbm, rig_hbm, xa, xb, za, zb, zd, now, rig, rw, xu, xd, zu, sems):
     copies = [pltpu.make_async_copy(rig_hbm, rig, sems.at[0]), pltpu.make_async_copy(now_hbm, now, sems.at[1])]
     for copy in copies:
         copy.start()
@@ -191,14 +189,6 @@
             xu[pl.ds(16 * c + 8 * half, 8), :] = part
             xu[pl.ds(48 + 16 * c + 8 * half, 8), :] = grad
             xd[pl.ds(16 * c + 8 * half, 8), :] = now[c, x_rows(0, half), :]
-    r = [rw[y_rows(12 + a), :] for a in range(4)]
-    yu[pl.ds(48, 8), :] = open_scale(r)
-    yd[pl.ds(24, 8), :] = rw[y_rows(0), :]
-    for c in range(3):
-        part, grad = open_terms([now[c, y_rows(12 + a), :] for a in range(4)], r)
-        yu[pl.ds(8 * c, 8), :] = part
-        yu[pl.ds(24 + 8 * c, 8), :] = grad
-        yd[pl.ds(8 * c, 8), :] = now[c, y_rows(0), :]
     back = lambda t: [rolled(t, 3 - a) for a in range(4)]
     r = back(last_lanes(lambda rows: rw[rows, :], lane))
     parts, grads = [], []
@@ -212,7 +202,6 @@
     zd[...] = first_lanes(lambda c, rows: now[c, rows, :], lambda rows: rw[rows, :], lane)
     index = place()
     paired(index[0], xu, xd, xa, xb)
-    paired(index[1], yu, yd, ya, yb)
     paired(index[2], zu, zd, za, zb)
 
 
@@ -231,9 +220,10 @@
     at_z = jnp.where(index_z == 0, 2.0, 1.0).astype(F32)
 
     def along_y(c, carry):
-        v = [now[c, y_rows(y), :] for y in range(NYL)] + [high_v[1][pl.ds(8 * c, 8), :]]
-        r = [rw[y_rows(y), :] for y in range(NYL)] + [high_r[1][...]]
-        carried = low[1](c, v[0])
+        none = jnp.zeros((8, NZL), F32)
+        v = [now[c, y_rows(y), :] for y in range(NYL)] + [high_v[1][pl.ds(8 * c, 8), :] if high_v[1] is not None else none]
+        r = [rw[y_rows(y), :] for y in range(NYL)] + [high_r[1][...] if high_r[1] is not None else none]
+        carried = low[1](c, v[0]) if low[1] is not None else none
         for e in range(4):
             terms = element(v[4 * e : 4 * e + 5], r[4 * e : 4 * e + 5])
             head = terms[0] * at_y if e == 0 else terms[0]
@@ -324,54 +314,113 @@
     return jnp.where((pos == 0) & is_first, np.float32(W0), out)
 
 
-def first_kernel(
-    counts, now, prev, rig, rho, xa, xb, ya, yb, za, zb, zd_own, nodes, ids,
-    out, kept, to_normal, ya2, yb2, zu2, zd2, mx, my, mz, xd, yd, zd,
-    rw, scale, acc, early, slip, xu, yu, zu, xu2, xd2, yu2, yd2,
+def half_kernel(
+    counts, now, prev, rig, rho, xa, xb, za, zb, zd_own,
+    base, ya, yb, early, mx, mz, xd, zd, rw, scale,
+    acc, xu, zu, yu, yd,
 ):
-    middle = counts[0] // 2
     index = place()
     unpaired(index[0], xa, xb, xu, xd)
-    unpaired(index[1], ya, yb, yu, yd)
     unpaired(index[2], za, zb, zu, zd)
     widen(rig, rw)
     step_scale(rho, scale)
     lane = lane_of()
-    has = [(i > 0).astype(F32) for i in index]
+    has_x, has_z = (index[0] > 0).astype(F32), (index[2] > 0).astype(F32)
+    kappa, diagonal = np.float32(KAPPA), np.float32(KAPPA * D[4, 4])
     for half in range(2):
         rows = pl.ds(8 * half, 8)
-        mx[rows, :] = (xu[pl.ds(96 + 8 * half, 8), :] + np.float32(KAPPA * D[4, 4]) * rw[x_rows(0, half), :]) * has[0]
-    my[...] = (yu[pl.ds(48, 8), :] + np.float32(KAPPA * D[4, 4]) * rw[y_rows(0), :]) * has[1]
+        mx[rows, :] = (xu[pl.ds(96 + 8 * half, 8), :] + diagonal * rw[x_rows(0, half), :]) * has_x
     own, above = zd_own[...], zu[...]
     r_first = from_fourth(own, lane)
-    scale_z = (from_fourth(above, lane) + np.float32(KAPPA * D[4, 4]) * r_first) * has[2]
+    scale_z = (from_fourth(above, lane) + diagonal * r_first) * has_z
     mz[...] = scale_z
-    closing_z = above + np.float32(KAPPA) * r_first * rolled(above, 64) + scale_z * own
-    kappa = np.float32(KAPPA)
+    closing_z = above + kappa * r_first * rolled(above, 64) + scale_z * own
 
     def low_x(c, offset, plane, v0):
         rows = pl.ds(pl.multiple_of(offset, 8), 8)
         grad = xu[pl.ds(pl.multiple_of(48 + 16 * c + offset, 8), 8), :]
         return xu[plane, :] + kappa * rw[rows, :] * grad + mx[rows, :] * v0
 
-    def low_y(c, v0):
-        grad = yu[pl.ds(pl.multiple_of(24 + 8 * c, 8), 8), :]
-        return yu[pl.ds(pl.multiple_of(8 * c, 8), 8), :] + kappa * rw[y_rows(0), :] * grad + my[...] * v0
-
     def store(c, x, rows, plane, after):
-        out[c, rows, :] = after
-        kept[c, rows, :] = after
-        if x == 0:
-            xd2[plane, :] = after
+        base[c, rows, :] = after
 
     def on_first(c, plane, carried, term):
         early[plane, :] = carried - term
 
     below = zd[...]
     advance(
-        now, prev, rw, (low_x, low_y), (xd, yd), (xd.at[pl.ds(48, 16)], yd.at[pl.ds(24, 8)]), scale,
+        now, prev, rw, (low_x, None), (xd, None), (xd.at[pl.ds(48, 16)], None), scale,
         below, rolled(below, -3), closing_z, index, store, acc, on_first,
     )
+
+    r = [rw[y_rows(12 + a), :] for a in range(4)]
+    by_value, by_flux = open_response([scale[y_rows(12 + a), :] for a in range(4)], r)
+    planes = [open_scale(r), *open_terms(by_value, r), *open_terms(by_flux, r)]
+    for n, plane in enumerate(planes):
+        yu[pl.ds(96 + 8 * n, 8), :] = plane
+    for c in range(3):
+        planes = open_terms([now[c, y_rows(12 + a), :] for a in range(4)], r)
+        planes += open_terms([base[c, y_rows(12 + a), :] for a in range(4)], r)
+        for n, plane in enumerate(planes):
+            yu[pl.ds(24 * n + 8 * c, 8), :] = plane
+        yd[pl.ds(8 * c, 8), :] = now[c, y_rows(0), :]
+        yd[pl.ds(24 + 8 * c, 8), :] = base[c, y_rows(0), :]
+    yd[pl.ds(48, 8), :] = rw[y_rows(0), :]
+    yd[pl.ds(56, 8), :] = scale[y_rows(0), :]
+    paired(index[1], yu, yd, ya, yb)
+
+
+def open_response(scale, r):
+    by_value = [scale[a] * total([(E[a, b] * D[b, 4], r[b]) for b in range(4)]) for a in range(4)]
+    by_flux = [scale[a] * np.float32(E[a, 4]) for a in range(4)]
+    return by_value, by_flux
+
+
+def whole_kernel(
+    counts, base, now, rw, scale, early, ya, yb, mx, xd, zd, nodes, ids,
+    out, kept, to_normal, zu2, zd2, my, y_low, y_high, r_high,
+    slip, yu, yd, xu2, xd2,
+):
+    middle = counts[0] // 2
+    index = place()
+    lane = lane_of()
+    kappa, diagonal = np.float32(KAPPA), np.float32(KAPPA * D[4, 4])
+    d44 = np.float32(D[4, 4])
+    unpaired(index[1], ya, yb, yu, yd)
+    for c in range(3):
+        for k in range(16):
+            rows = pl.ds(8 * k, 8)
+            values = base[c, rows, :]
+            out[c, rows, :] = values
+            kept[c, rows, :] = values
+    r = [rw[y_rows(12 + a), :] for a in range(4)]
+    by_value, by_flux = open_response([scale[y_rows(12 + a), :] for a in range(4)], r)
+    own_scale = open_scale(r)
+    r0, s0 = rw[y_rows(0), :], scale[y_rows(0), :]
+    r_above, s_above = yd[pl.ds(48, 8), :], yd[pl.ds(56, 8), :]
+    r_high[...] = r_above
+    gain, value_part, value_grad, flux_part, flux_grad = (yu[pl.ds(96 + 8 * n, 8), :] for n in range(5))
+    gain = (gain + diagonal * r0) * (index[1] > 0).astype(F32)
+    my[...] = gain
+    for c in range(3):
+        plane = pl.ds(8 * c, 8)
+        part, grad, part2, grad2 = (yu[pl.ds(24 * n + 8 * c, 8), :] for n in range(4))
+        v0 = now[c, y_rows(0), :]
+        after = base[c, y_rows(0), :] - s0 * (part + kappa * r0 * grad + gain * v0)
+        out[c, y_rows(0), :] = after
+        kept[c, y_rows(0), :] = after
+        flux = r0 * (grad + d44 * v0)
+        y_low[plane, :] = (part2 - value_part * v0 - flux_part * flux) + kappa * r0 * (
+            grad2 - value_grad * v0 - flux_grad * flux
+        )
+        above = yd[plane, :]
+        part, grad = open_terms([now[c, y_rows(12 + a), :] for a in range(4)], r)
+        flux = r_above * (grad + d44 * above)
+        y_high[plane, :] = yd[pl.ds(24 + 8 * c, 8), :] - s_above * (part + own_scale * above + kappa * flux)
+        for a in range(4):
+            after = base[c, y_rows(12 + a), :] - by_value[a] * above - by_flux[a] * flux
+            out[c, y_rows(12 + a), :] = after
+            kept[c, y_rows(12 + a), :] = after
 
     on_one, on_two = index[0] == middle - 1, index[0] == middle
     for half in range(2):
@@ -385,22 +434,17 @@
             part, grad = open_terms(v[4:], r[4:8])
             sent = part + kappa * r[8] * grad
             xu2[plane, :] = sent
+            xd2[plane, :] = v[0]
             here = early[plane, :] + mx[rows, :] * v[0] - first_term(v[:5], r[:5])
             slip[plane, :] = face * jnp.where(on_one, sent, jnp.where(on_two, here, 0.0))
-    r = [rw[y_rows(12 + a), :] for a in range(4)]
-    for c in range(3):
-        part, grad = open_terms([out[c, y_rows(12 + a), :] for a in range(4)], r)
-        yu2[pl.ds(8 * c, 8), :] = part + kappa * yd[pl.ds(24, 8), :] * grad
-        yd2[pl.ds(8 * c, 8), :] = out[c, y_rows(0), :]
     back = lambda t: [rolled(t, 3 - a) for a in range(4)]
     r = back(last_lanes(lambda rows: rw[rows, :], lane))
     sent = []
     for c in range(3):
         part, grad = open_terms(back(last_lanes(lambda rows: out[c, rows, :], lane)), r)
-        sent.append(part + kappa * below * grad)
+        sent.append(part + kappa * zd[...] * grad)
     zu2[...] = interleaved(sent + [None], lane, 0)
     zd2[...] = first_lanes(lambda c, rows: out[c, rows, :], None, lane)
-    paired(index[1], yu2, yd2, ya2, yb2)
     tile = patch_tile(counts[2], slip[...], nodes[...], ids[...])
     for n in range(counts[0]):
         to_normal[pl.ds(56 * n, 48), :] = jnp.where(n > index[0], xu2[...], xd2[...])
@@ -426,28 +470,25 @@
 
 
 def second_kernel(
-    counts, now, prev, rig, rho, got_x, ya2, yb2, got_z, zd2_own, mx, my, mz, xd, yd, zd,
-    out, rw, scale, acc, xu2, xd2, yu2, yd2, zu2, zd2,
+    counts, now, prev, rw, scale, got_x, got_z, zd2_own, mx, my, mz, xd, zd, y_low, y_high, r_high,
+    out, acc, xu2, xd2, zu2, zd2,
 ):
     index = place()
     beside(index[0], counts[0], got_x, 56, xu2, xd2)
-    unpaired(index[1], ya2, yb2, yu2, yd2)
     beside(index[2], counts[2], got_z, 16, zu2, zd2)
-    widen(rig, rw)
-    step_scale(rho, scale)
     closing_z = zu2[...] + mz[...] * zd2_own[...]
 
     def low_x(c, offset, plane, v0):
         return xu2[plane, :] + mx[pl.ds(pl.multiple_of(offset, 8), 8), :] * v0
 
     def low_y(c, v0):
-        return yu2[pl.ds(pl.multiple_of(8 * c, 8), 8), :] + my[...] * v0
+        return y_low[pl.ds(pl.multiple_of(8 * c, 8), 8), :] + my[...] * v0
 
     def store(c, x, rows, plane, after):
         out[c, rows, :] = after
 
     advance(
-        now, prev, rw, (low_x, low_y), (xd2, yd2), (xd.at[pl.ds(48, 16)], yd.at[pl.ds(24, 8)]), scale,
+        now, prev, rw, (low_x, low_y), (xd2, y_high), (xd.at[pl.ds(48, 16)], r_high), scale,
         zd2[...], rolled(zd[...], -3), closing_z, index, store, acc, lambda *args: None,
     )
 
@@ -512,24 +553,27 @@
     now, prev = field_now.reshape(flat), field_prev.reshape(flat)
     rig, rho = rigidity.reshape(block), density.reshape(block)
     nodes, ids = fault_nodes.reshape(1, -1), patch_ids.reshape(1, -1)
-    ups = [(up, NZL) for up, _ in FIRST_ROWS]
-    downs = [(down, NZL) for _, down in FIRST_ROWS]
-    xa, xb, ya, yb, za, zb, zd = call(
-        pack_kernel, "pack", [shape for shape in ups for _ in range(2)] + [tile],
-        [pltpu.VMEM(flat, F32), pltpu.VMEM(block, jnp.bfloat16), block, ups[0], downs[0], ups[1], downs[1], ups[2],
+    x_up, x_down, y_up, y_down = ((n, NZL) for n in (X_UP, X_DOWN, Y_UP, Y_DOWN))
+    faces, strip = (48, NZL), (24, NZL)
+    xa, xb, za, zb, zd_own = call(
+        pack_kernel, "pack", [x_up, x_up, tile, tile, tile],
+        [pltpu.VMEM(flat, F32), pltpu.VMEM(block, jnp.bfloat16), block, x_up, x_down, tile,
          pltpu.SemaphoreType.DMA((2,))],
         flops=2_000_000, moved=400_000, in_specs=[pl.BlockSpec(memory_space=pl.ANY)] * 2,
     )(now, rig)
-    ya, yb = swap_near(ya, "strike"), swap_far(yb, "strike")
     xa, xb = swap_near(xa, "normal"), swap_far(xb, "normal")
     zb, za = swap_far(zb, "depth"), swap_near(za, "depth")
-    mid, kept, to_normal, ya2, yb2, zu2, zd2, *held = call(
-        functools.partial(first_kernel, counts), "first",
-        [flat, flat, (56 * counts[0], NZL), (24, NZL), (24, NZL), tile, tile, (16, NZL), tile, tile] + downs,
-        [block, block, flat, (48, NZL), (48, NZL)] + ups + [(48, NZL), (48, NZL), (24, NZL), (24, NZL)],
-        flops=10_000_000, moved=900_000,
-    )(now, prev, rig, rho, xa, xb, ya, yb, za, zb, zd, nodes, ids)
-    ya2, yb2 = swap_near(ya2, "strike"), swap_far(yb2, "strike")
+    base, ya, yb, early, mx, mz, xd, zd, rw, scale = call(
+        functools.partial(half_kernel, counts), "half",
+        [flat, y_up, y_up, faces, (16, NZL), tile, x_down, tile, block, block],
+        [flat, x_up, tile, y_up, y_down], flops=10_000_000, moved=900_000,
+    )(now, prev, rig, rho, xa, xb, za, zb, zd_own)
+    yb, ya = swap_far(yb, "strike"), swap_near(ya, "strike")
+    mid, kept, to_normal, zu2, zd2, my, y_low, y_high, r_high = call(
+        functools.partial(whole_kernel, counts), "whole",
+        [flat, flat, (56 * counts[0], NZL), tile, tile, tile, strip, strip, tile],
+        [faces, y_up, y_down, faces, faces], flops=2_000_000, moved=900_000,
+    )(base, now, rw, scale, early, ya, yb, mx, xd, zd, nodes, ids)
     got_x = lax.all_to_all(to_normal, "normal", 0, 0, tiled=True)
     (to_depth,) = call(
         functools.partial(relay_kernel, counts), "relay", [(16 * counts[2], NZL)], flops=10_000, moved=200_000,
@@ -541,10 +585,9 @@
     got_s = lax.all_to_all(to_strike, "strike", 0, 0, tiled=True)
     (share,) = call(final_kernel, "final", [(2, 3)], flops=10_000, moved=10_000)(got_s)
     (following,) = call(
-        functools.partial(second_kernel, counts), "second", [flat],
-        [block, block, flat] + [(n, NZL) for pair in SECOND_ROWS for n in pair],
+        functools.partial(second_kernel, counts), "second", [flat], [flat, faces, faces, tile, tile],
         flops=10_000_000, moved=900_000,
-    )(kept, now, rig, rho, got_x, ya2, yb2, got_z, zd2, *held)
+    )(kept, now, rw, scale, got_x, got_z, zd2, mx, my, mz, xd, zd, y_low, y_high, r_high)
     return following.reshape(field_now.shape), mid.reshape(field_now.shape), share
 
 

time: 84.7 us -> 89 us (1.051)
  the two profiles are of different devices: /device:TPU:24 before, /device:TPU:1 now
where the time goes in v4:
time: 89 us; the launch traced here: 88.5 us
  starting transfers between devices  40.3 us (45%)
  blocking collectives  20.2 us (23%)
  waiting for transfers between devices  15.6 us (18%)
  Pallas kernels  9.26 us (10%)
  local copies, waits for them, and re-layouts  2.39 us (3%)
    all_to_all x1, starting transfers between devices, local(): got_s = lax.all_to_all(to_strike, 'strike', 0, 0, tiled=True)  24.4 us
    ppermute x3, starting transfers between devices, swap_near(): lax.ppermute(value, axis, [(i, i ^ 1) for i in range(lax.axis_size(axis))])  12.6 us
    all_to_all x1, blocking collectives, local(): got_x = lax.all_to_all(to_normal, 'normal', 0, 0, tiled=True)  10.2 us
    all_to_all x1, waiting for transfers between devices, local(): got_s = lax.all_to_all(to_strike, 'strike', 0, 0, tiled=True)  10.2 us
    all_to_all x1, blocking collectives, local(): got_z = lax.all_to_all(to_depth, 'depth', 0, 0, tiled=True)  9.97 us
    pallas_call x1, Pallas kernels, local(): call(functools.partial(second_kernel, counts), 'second', [flat], [flat, f...  3.45 us
    ppermute x3, starting transfers between devices, swap_far(): lax.ppermute(value, axis, [(i, i + 1) for i in lower] + [(i + 1, i) for i...  3.25 us
    ppermute x3, waiting for transfers between devices, swap_far(): lax.ppermute(value, axis, [(i, i + 1) for i in lower] + [(i + 1, i) for i...  2.99 us
  transfers between devices with their start and end apart: 7, of which 3 were waited for; matrix products, arithmetic and copies ran while one was open for 0% of the time, Pallas kernels for 4%

profile of v4, /device:TPU:1, one launch (start us, length us, event | category | flops | bytes accessed | tf_op | source)
XLA Modules:
  0.0 88.5 jit_solution(5100254541510300291)
XLA Ops:
  0.6 0.0 copy-start
  0.6 0.9 %copy-done = f32[3,8,16,128]{3,2,1,0:T(8,128)S(1)} copy-done((f32[3,8,16,128]{3,2,1,0:T(8,128)S(1)}, f32[3,8,16,128]{3,2,1,0:T(8,128)}, u32[]{:S(2)}) %copy-start) | copy-done | bytes 196632
  1.6 0.0 copy-start.3
  1.6 0.8 copy-done.3
  2.3 0.0 copy-start.2
  2.3 0.6 pack.1
  2.9 4.4 %collective-permute-start = (f32[112,128]{1,0:T(8,128)S(1)}, f32[112,128]{1,0:T(8,128)S(1)}, u32[]{:S(2)}, u32[]{:S(2)}) collective-permute-start(f32[112,128]{1,0:T(8,128)S(1)} %get-tuple-element.27), channel_id=1, source_target_pairs={{0,128},{128,0},{256,384},{384,256},{1,129},{129,1},{257,385},{385... | collective-permute-start | bytes 172040 | tf_op jit(solution)/shard_map/ppermute | solution.py:541
  7.3 0.7 collective-permute-start.1
  8.0 6.3 %collective-permute-start.2 = (f32[8,128]{1,0:T(8,128)S(1)}, f32[8,128]{1,0:T(8,128)S(1)}, u32[]{:S(2)}, u32[]{:S(2)}) collective-permute-start(f32[8,128]{1,0:T(8,128)S(1)} %get-tuple-element.29), channel_id=1, source_target_pairs={{0,1},{1,0},{2,3},{3,2},{4,5},{5,4},{6,7},{7,6},{8,9},{9,8},{10,11... | collective-permute-start | bytes 12296 | tf_op jit(solution)/shard_map/ppermute | solution.py:541
  14.3 1.9 %collective-permute-start.3 = (f32[8,128]{1,0:T(8,128)S(1)}, f32[8,128]{1,0:T(8,128)S(1)}, u32[]{:S(2)}, u32[]{:S(2)}) collective-permute-start(f32[8,128]{1,0:T(8,128)S(1)} %get-tuple-element.30), channel_id=1, source_target_pairs={{1,2},{3,4},{5,6},{2,1},{4,3},{6,5},{9,10},{11,12},{13,14},{10,9},... | collective-permute-start | bytes 12296 | tf_op jit(solution)/shard_map/ppermute | solution.py:546
  16.3 0.0 collective-permute-done.2.za
  16.3 3.0 %collective-permute-done.3.zb = f32[8,128]{1,0:T(8,128)S(1)} collective-permute-done((f32[8,128]{1,0:T(8,128)S(1)}, f32[8,128]{1,0:T(8,128)S(1)}, u32[]{:S(2)}, u32[]{:S(2)}) %collective-permute-start.3) | collective-permute-done | bytes 4128 | tf_op jit(solution)/shard_map/ppermute | solution.py:546
  19.3 0.0 collective-permute-done.xa
  19.3 0.0 collective-permute-done.1.xb
  19.3 0.0 copy-done.2
  19.3 0.0 copy-done.4
  19.3 2.9 %half.1 = (f32[3,128,128]{2,1,0:T(8,128)S(1)}, f32[136,128]{1,0:T(8,128)S(1)}, f32[136,128]{1,0:T(8,128)S(1)}, f32[48,128]{1,0:T(8,128)S(1)}, f32[16,128]{1,0:T(...) custom-call(f32[3,128,128]{2,1,0:T(8,128)S(1)} %bitcast.17, ...), custom_call_target="tpu_custom_call" | custom-call | flops 10000000 | bytes 900000 | tf_op jit(solution)/shard_map/half/pallas_call | solution.py:566
  22.1 1.9 %collective-permute-start.4 = (f32[136,128]{1,0:T(8,128)S(1)}, f32[136,128]{1,0:T(8,128)S(1)}, u32[]{:S(2)}, u32[]{:S(2)}) collective-permute-start(f32[136,128]{1,0:T(8,128)S(1)} %get-tuple-element.36), channel_id=1, source_target_pairs={{0,8},{8,0},{16,24},{24,16},{32,40},{40,32},{48,56},{56,48},{64,72... | collective-permute-start | bytes 208904 | tf_op jit(solution)/shard_map/ppermute | solution.py:541
  24.1 0.7 collective-permute-start.5
  24.7 2.5 %collective-permute-done.4.ya = f32[136,128]{1,0:T(8,128)S(1)} collective-permute-done((f32[136,128]{1,0:T(8,128)S(1)}, f32[136,128]{1,0:T(8,128)S(1)}, u32[]{:S(2)}, u32[]{:S(2)}) %collective-permute-start.4) | collective-permute-done | bytes 69664 | tf_op jit(solution)/shard_map/ppermute | solution.py:541
  27.2 0.0 collective-permute-done.5.yb
  27.2 0.7 copy-done.6
  27.9 0.0 copy-done.5
  27.9 1.1 %whole.1 = (f32[3,128,128]{2,1,0:T(8,128)}, f32[3,128,128]{2,1,0:T(8,128)S(1)}, f32[224,128]{1,0:T(8,128)S(1)}, f32[8,128]{1,0:T(8,128)S(1)}, f32[8,128]{1,0:T(8...) custom-call(f32[3,128,128]{2,1,0:T(8,128)S(1)} %get-tuple-element.32.bas, ...), custom_call_target="tpu_custom_call" | custom-call | flops 2000000 | bytes 900000 | tf_op jit(solution)/shard_map/whole/pallas_call | solution.py:572
  29.0 10.2 %all_to_all.33 = f32[4,56,128]{2,1,0:T(8,128)S(1)} all-to-all(f32[4,56,128]{2,1,0:T(8,128)S(1)} %bitcast.28), channel_id=1, replica_groups=mesh['normal'=4,'strike'=16,'depth'=8] {'normal'}, dimensions={0} | all-to-all | bytes 229376 | tf_op jit(solution)/shard_map/all_to_all | solution.py:577
  39.2 10.0 %all_to_all.34 = f32[8,16,128]{2,1,0:T(8,128)S(1)} all-to-all(f32[8,16,128]{2,1,0:T(8,128)S(1)} %bitcast.24), channel_id=1, replica_groups=mesh['normal'=4,'strike'=16,'depth'=8] {'depth'}, dimensions={0} | all-to-all | bytes 131072 | tf_op jit(solution)/shard_map/all_to_all | solution.py:581
  49.2 0.6 add.1
  49.8 24.4 %all-to-all-start.2 = ((f32[16,1,128]{2,1,0:T(1,128)}), f32[16,1,128]{2,1,0:T(1,128)S(1)}, u32[]{:S(2)}, u32[]{:S(2)}) async-start(f32[16,1,128]{2,1,0:T(1,128)} %bitcast.13), calls=%async_computation.2 | async-start | bytes 16384 | tf_op jit(solution)/shard_map/all_to_all | solution.py:585
  74.2 0.0 copy-done.1
  74.3 3.4 %second.1 = f32[3,128,128]{2,1,0:T(8,128)} custom-call(f32[3,128,128]{2,1,0:T(8,128)S(1)} %get-tuple-element.41.now, f32[3,128,128]{2,1,0:T(8,128)S(1)} %bitcast.19, f32[128,128]{1,0:T(8,128)S(1)} %get-tuple-element.33.rw, f32[128,128]{1,0:T(8,128)S(1)} %get-tuple-element.34.scale, f32[224,128]{1,0:T(8,128)S(1)} %bitcast.21, f32[128,128]{1,0:T(8,128)S(1)} %bitcast.23, ...), custom_call_target="tpu_custom_call" | custom-call | flops 10000000 | bytes 900000 | tf_op jit(solution)/shard_map/second/pallas_call | solution.py:587
  77.7 10.2 %all-to-all-done.2 = f32[16,1,128]{2,1,0:T(1,128)S(1)} async-done(((f32[16,1,128]{2,1,0:T(1,128)}), f32[16,1,128]{2,1,0:T(1,128)S(1)}, u32[]{:S(2)}, u32[]{:S(2)}) %all-to-all-start.2) | async-done | bytes 8224 | tf_op jit(solution)/shard_map/all_to_all | solution.py:585
  87.9 0.7 final.1
  (5 shorter events, 0.0 us)
Async XLA Ops:
  0.6 0.9 %copy-start = (f32[3,8,16,128]{3,2,1,0:T(8,128)S(1)}, f32[3,8,16,128]{3,2,1,0:T(8,128)}, u32[]{:S(2)}) copy-start(f32[3,8,16,128]{3,2,1,0:T(8,128)} %param.6) | copy-start | bytes 589828
  1.6 0.8 copy-start.3
  2.3 16.9 %copy-start.2 = (f32[3,8,16,128]{3,2,1,0:T(8,128)S(1)}, f32[3,8,16,128]{3,2,1,0:T(8,128)}, u32[]{:S(2)}) copy-start(f32[3,8,16,128]{3,2,1,0:T(8,128)} %param.7) | copy-start | bytes 589828
  2.3 16.9 %copy-start.4 = (bf16[8,16,128]{2,1,0:T(8,128)(2,1)S(1)}, bf16[8,16,128]{2,1,0:T(8,128)(2,1)}, u32[]{:S(2)}) copy-start(bf16[8,16,128]{2,1,0:T(8,128)(2,1)} %param.9) | copy-start | bytes 98308
  2.9 16.3 %collective-permute-start = (f32[112,128]{1,0:T(8,128)S(1)}, f32[112,128]{1,0:T(8,128)S(1)}, u32[]{:S(2)}, u32[]{:S(2)}) collective-permute-start(f32[112,128]{1,0:T(8,128)S(1)} %get-tuple-element.27), channel_id=1, source_target_pairs={{0,128},{128,0},{256,384},{384,256},{1,129},{129,1},{257,385},{385... | collective-permute-start | bytes 172040 | tf_op jit(solution)/shard_map/ppermute | solution.py:541
  7.3 11.9 %collective-permute-start.1 = (f32[112,128]{1,0:T(8,128)S(1)}, f32[112,128]{1,0:T(8,128)S(1)}, u32[]{:S(2)}, u32[]{:S(2)}) collective-permute-start(f32[112,128]{1,0:T(8,128)S(1)} %get-tuple-element.28), channel_id=1, source_target_pairs={{128,256},{256,128},{129,257},{257,129},{130,258},{258,130},{131,2... | collective-permute-start | bytes 172040 | tf_op jit(solution)/shard_map/ppermute | solution.py:546
  8.0 8.3 %collective-permute-start.2 = (f32[8,128]{1,0:T(8,128)S(1)}, f32[8,128]{1,0:T(8,128)S(1)}, u32[]{:S(2)}, u32[]{:S(2)}) collective-permute-start(f32[8,128]{1,0:T(8,128)S(1)} %get-tuple-element.29), channel_id=1, source_target_pairs={{0,1},{1,0},{2,3},{3,2},{4,5},{5,4},{6,7},{7,6},{8,9},{9,8},{10,11... | collective-permute-start | bytes 12296 | tf_op jit(solution)/shard_map/ppermute | solution.py:541
  14.3 4.9 %collective-permute-start.3 = (f32[8,128]{1,0:T(8,128)S(1)}, f32[8,128]{1,0:T(8,128)S(1)}, u32[]{:S(2)}, u32[]{:S(2)}) collective-permute-start(f32[8,128]{1,0:T(8,128)S(1)} %get-tuple-element.30), channel_id=1, source_target_pairs={{1,2},{3,4},{5,6},{2,1},{4,3},{6,5},{9,10},{11,12},{13,14},{10,9},... | collective-permute-start | bytes 12296 | tf_op jit(solution)/shard_map/ppermute | solution.py:546
  22.1 5.1 %collective-permute-start.4 = (f32[136,128]{1,0:T(8,128)S(1)}, f32[136,128]{1,0:T(8,128)S(1)}, u32[]{:S(2)}, u32[]{:S(2)}) collective-permute-start(f32[136,128]{1,0:T(8,128)S(1)} %get-tuple-element.36), channel_id=1, source_target_pairs={{0,8},{8,0},{16,24},{24,16},{32,40},{40,32},{48,56},{56,48},{64,72... | collective-permute-start | bytes 208904 | tf_op jit(solution)/shard_map/ppermute | solution.py:541
  24.1 3.1 %collective-permute-start.5 = (f32[136,128]{1,0:T(8,128)S(1)}, f32[136,128]{1,0:T(8,128)S(1)}, u32[]{:S(2)}, u32[]{:S(2)}) collective-permute-start(f32[136,128]{1,0:T(8,128)S(1)} %get-tuple-element.37), channel_id=1, source_target_pairs={{8,16},{24,32},{40,48},{56,64},{72,80},{88,96},{104,112},{16,8},{3... | collective-permute-start | bytes 208904 | tf_op jit(solution)/shard_map/ppermute | solution.py:546
  27.2 0.7 copy-start.6
  27.2 0.7 copy-start.5
  39.2 35.0 %copy-start.1 = (f32[3,8,16,128]{3,2,1,0:T(8,128)S(1)}, f32[3,8,16,128]{3,2,1,0:T(8,128)}, u32[]{:S(2)}) copy-start(f32[3,8,16,128]{3,2,1,0:T(8,128)} %param.6) | copy-start | bytes 589828
  49.8 38.0 %all-to-all-start.2 = ((f32[16,1,128]{2,1,0:T(1,128)}), f32[16,1,128]{2,1,0:T(1,128)S(1)}, u32[]{:S(2)}, u32[]{:S(2)}) async-start(f32[16,1,128]{2,1,0:T(1,128)} %bitcast.13), calls=%async_computation.2 | async-start | bytes 16384 | tf_op jit(solution)/shard_map/all_to_all | solution.py:585

commit v5 on v4

--- a/solution.py
+++ b/solution.py
@@ -316,7 +316,7 @@
 
 def half_kernel(
     counts, now, prev, rig, rho, xa, xb, za, zb, zd_own,
-    base, ya, yb, early, mx, mz, xd, zd, rw, scale,
+    base, yb, ya, early, mx, mz, xd, zd, rw, scale,
     acc, xu, zu, yu, yd,
 ):
     index = place()
@@ -377,15 +377,18 @@
 
 
 def whole_kernel(
-    counts, base, now, rw, scale, early, ya, yb, mx, xd, zd, nodes, ids,
-    out, kept, to_normal, zu2, zd2, my, y_low, y_high, r_high,
-    slip, yu, yd, xu2, xd2,
+    counts, base, now, rw, scale, early, yb, ya, mx, xd, zd, nodes_hbm, ids_hbm,
+    out, kept, to_depth, xa2, xb2, zd2, my, y_low, y_high, r_high,
+    slip, yu, yd, xu2, xd2, zu2, nodes, ids, sems,
 ):
     middle = counts[0] // 2
     index = place()
     lane = lane_of()
     kappa, diagonal = np.float32(KAPPA), np.float32(KAPPA * D[4, 4])
     d44 = np.float32(D[4, 4])
+    copies = [pltpu.make_async_copy(nodes_hbm, nodes, sems.at[0]), pltpu.make_async_copy(ids_hbm, ids, sems.at[1])]
+    for copy in copies:
+        copy.start()
     unpaired(index[1], ya, yb, yu, yd)
     for c in range(3):
         for k in range(16):
@@ -445,36 +448,29 @@
         sent.append(part + kappa * zd[...] * grad)
     zu2[...] = interleaved(sent + [None], lane, 0)
     zd2[...] = first_lanes(lambda c, rows: out[c, rows, :], None, lane)
+    paired(index[0], xu2, xd2, xa2, xb2)
+    for copy in copies:
+        copy.wait()
     tile = patch_tile(counts[2], slip[...], nodes[...], ids[...])
-    for n in range(counts[0]):
-        to_normal[pl.ds(56 * n, 48), :] = jnp.where(n > index[0], xu2[...], xd2[...])
-        to_normal[pl.ds(56 * n + 48, 8), :] = tile
-
-
-def relay_kernel(counts, got, zu2, zd2, to_depth):
-    index = lax.axis_index("depth")
-    tile = got[pl.ds(48, 8), :]
-    for n in range(1, counts[0]):
-        tile = tile + got[pl.ds(56 * n + 48, 8), :]
     for d in range(counts[2]):
-        to_depth[pl.ds(16 * d, 8), :] = jnp.where(d > index, zu2[...], zd2[...])
+        to_depth[pl.ds(16 * d, 8), :] = jnp.where(d > index[2], zu2[...], zd2[...])
         to_depth[pl.ds(16 * d + 8, 8), :] = jnp.broadcast_to(tile[d : d + 1, :], (8, NZL))
 
 
-def sum_kernel(counts, got, to_strike):
+def sum_kernel(counts, got, to_face):
     row = got[pl.ds(8, 8), :]
     for d in range(1, counts[2]):
         row = row + got[pl.ds(16 * d + 8, 8), :]
-    for half in range(counts[1] // 8 or 1):
-        to_strike[pl.ds(8 * half, min(8, counts[1])), :] = row[: min(8, counts[1]), :]
+    for k in range(counts[0] * counts[1] // 8):
+        to_face[pl.ds(8 * k, 8), :] = row
 
 
 def second_kernel(
-    counts, now, prev, rw, scale, got_x, got_z, zd2_own, mx, my, mz, xd, zd, y_low, y_high, r_high,
+    counts, now, prev, rw, scale, xa2, xb2, got_z, zd2_own, mx, my, mz, xd, zd, y_low, y_high, r_high,
     out, acc, xu2, xd2, zu2, zd2,
 ):
     index = place()
-    beside(index[0], counts[0], got_x, 56, xu2, xd2)
+    unpaired(index[0], xa2, xb2, xu2, xd2)
     beside(index[2], counts[2], got_z, 16, zu2, zd2)
     closing_z = zu2[...] + mz[...] * zd2_own[...]
 
@@ -559,35 +555,35 @@
         pack_kernel, "pack", [x_up, x_up, tile, tile, tile],
         [pltpu.VMEM(flat, F32), pltpu.VMEM(block, jnp.bfloat16), block, x_up, x_down, tile,
          pltpu.SemaphoreType.DMA((2,))],
-        flops=2_000_000, moved=400_000, in_specs=[pl.BlockSpec(memory_space=pl.ANY)] * 2,
+        flops=2_000_000, moved=400_000, in_specs=[pl.BlockSpec(memory_space=pltpu.HBM)] * 2,
     )(now, rig)
     xa, xb = swap_near(xa, "normal"), swap_far(xb, "normal")
     zb, za = swap_far(zb, "depth"), swap_near(za, "depth")
-    base, ya, yb, early, mx, mz, xd, zd, rw, scale = call(
+    base, yb, ya, early, mx, mz, xd, zd, rw, scale = call(
         functools.partial(half_kernel, counts), "half",
         [flat, y_up, y_up, faces, (16, NZL), tile, x_down, tile, block, block],
         [flat, x_up, tile, y_up, y_down], flops=10_000_000, moved=900_000,
     )(now, prev, rig, rho, xa, xb, za, zb, zd_own)
     yb, ya = swap_far(yb, "strike"), swap_near(ya, "strike")
-    mid, kept, to_normal, zu2, zd2, my, y_low, y_high, r_high = call(
+    inside, outside = pl.BlockSpec(memory_space=pltpu.VMEM), pl.BlockSpec(memory_space=pltpu.HBM)
+    mid, kept, to_depth, xa2, xb2, zd2, my, y_low, y_high, r_high = call(
         functools.partial(whole_kernel, counts), "whole",
-        [flat, flat, (56 * counts[0], NZL), tile, tile, tile, strip, strip, tile],
-        [faces, y_up, y_down, faces, faces], flops=2_000_000, moved=900_000,
-    )(base, now, rw, scale, early, ya, yb, mx, xd, zd, nodes, ids)
-    got_x = lax.all_to_all(to_normal, "normal", 0, 0, tiled=True)
-    (to_depth,) = call(
-        functools.partial(relay_kernel, counts), "relay", [(16 * counts[2], NZL)], flops=10_000, moved=200_000,
-    )(got_x, zu2, zd2)
+        [flat, flat, (16 * counts[2], NZL), faces, faces, tile, tile, strip, strip, tile],
+        [faces, y_up, y_down, faces, faces, tile, pltpu.VMEM(nodes.shape, jnp.int32), pltpu.VMEM(ids.shape, jnp.int32),
+         pltpu.SemaphoreType.DMA((2,))],
+        flops=2_000_000, moved=900_000, in_specs=[inside] * 10 + [outside] * 2,
+    )(base, now, rw, scale, early, yb, ya, mx, xd, zd, nodes, ids)
     got_z = lax.all_to_all(to_depth, "depth", 0, 0, tiled=True)
-    (to_strike,) = call(
-        functools.partial(sum_kernel, counts), "add", [(counts[1], NZL)], flops=10_000, moved=80_000,
+    (to_face,) = call(
+        functools.partial(sum_kernel, counts), "add", [(counts[0] * counts[1], NZL)], flops=10_000, moved=80_000,
     )(got_z)
-    got_s = lax.all_to_all(to_strike, "strike", 0, 0, tiled=True)
-    (share,) = call(final_kernel, "final", [(2, 3)], flops=10_000, moved=10_000)(got_s)
+    got_face = lax.all_to_all(to_face, ("normal", "strike"), 0, 0, tiled=True)
+    xa2, xb2 = swap_near(xa2, "normal"), swap_far(xb2, "normal")
+    (share,) = call(final_kernel, "final", [(2, 3)], flops=10_000, moved=10_000)(got_face)
     (following,) = call(
         functools.partial(second_kernel, counts), "second", [flat], [flat, faces, faces, tile, tile],
         flops=10_000_000, moved=900_000,
-    )(kept, now, rw, scale, got_x, got_z, zd2, mx, my, mz, xd, zd, y_low, y_high, r_high)
+    )(kept, now, rw, scale, xa2, xb2, got_z, zd2, mx, my, mz, xd, zd, y_low, y_high, r_high)
     return following.reshape(field_now.shape), mid.reshape(field_now.shape), share
 
 

time: 89 us -> 78.9 us (0.89)
  blocking collectives: 20.2 us -> 9.42 us
  starting transfers between devices: 40.3 us -> 44.6 us
  waiting for transfers between devices: 15.6 us -> 11.8 us
    all_to_all x1 -> x0, blocking collectives: 10.2 us -> none  [local(): got_x = lax.all_to_all(to_normal, 'normal', 0, 0, tiled=True)]
    all_to_all x1, waiting for transfers between devices: 10.2 us -> 4.69 us  [local(): got_face = lax.all_to_all(to_face, ('normal', 'strike'), 0, 0, tiled=True)]
    ppermute x3 -> x4, starting transfers between devices: 12.6 us -> 15.9 us  [swap_near(): lax.ppermute(value, axis, [(i, i ^ 1) for i in range(lax.axis_size(axis))])]
    ppermute x3 -> x4, waiting for transfers between devices: 2.46 us -> 4.16 us  [swap_near(): lax.ppermute(value, axis, [(i, i ^ 1) for i in range(lax.axis_size(axis))])]
    ppermute x3 -> x4, starting transfers between devices: 3.25 us -> 3.91 us  [swap_far(): lax.ppermute(value, axis, [(i, i + 1) for i in lower] + [(i + 1, i) for i...]
    pallas_call x4 -> x3, Pallas kernels: 2.36 us -> 2.41 us  [the longest x1 1.14 us: local(): call(functools.partial(whole_kernel, counts), 'whole', [flat, flat, (16 *...]
    ppermute x3 -> x4, waiting for transfers between devices: 2.99 us -> 3 us  [swap_far(): lax.ppermute(value, axis, [(i, i + 1) for i in lower] + [(i + 1, i) for i...]
  transfers between devices with their start and end apart: 7 -> 9, of which waited for: 3 -> 4; matrix products, arithmetic and copies ran while one was open for 0% -> 0% of each run, Pallas kernels for 4% -> 4%
where the time goes in v5:
time: 78.9 us; the launch traced here: 78.4 us
  starting transfers between devices  44.6 us (57%)
  waiting for transfers between devices  11.8 us (15%)
  blocking collectives  9.42 us (12%)
  Pallas kernels  9.31 us (12%)
  local copies, waits for them, and re-layouts  2.39 us (3%)
    all_to_all x1, starting transfers between devices, local(): got_face = lax.all_to_all(to_face, ('normal', 'strike'), 0, 0, tiled=True)  24.8 us
    ppermute x4, starting transfers between devices, swap_near(): lax.ppermute(value, axis, [(i, i ^ 1) for i in range(lax.axis_size(axis))])  15.9 us
    all_to_all x1, blocking collectives, local(): got_z = lax.all_to_all(to_depth, 'depth', 0, 0, tiled=True)  9.42 us
    all_to_all x1, waiting for transfers between devices, local(): got_face = lax.all_to_all(to_face, ('normal', 'strike'), 0, 0, tiled=True)  4.69 us
    ppermute x4, waiting for transfers between devices, swap_near(): lax.ppermute(value, axis, [(i, i ^ 1) for i in range(lax.axis_size(axis))])  4.16 us
    ppermute x4, starting transfers between devices, swap_far(): lax.ppermute(value, axis, [(i, i + 1) for i in lower] + [(i + 1, i) for i...  3.91 us
    pallas_call x1, Pallas kernels, local(): call(functools.partial(second_kernel, counts), 'second', [flat], [flat, f...  3.45 us
    ppermute x4, waiting for transfers between devices, swap_far(): lax.ppermute(value, axis, [(i, i + 1) for i in lower] + [(i + 1, i) for i...  3 us
  transfers between devices with their start and end apart: 9, of which 4 were waited for; matrix products, arithmetic and copies ran while one was open for 0% of the time, Pallas kernels for 4%

profile of v5, /device:TPU:1, one launch (start us, length us, event | category | flops | bytes accessed | tf_op | source)
XLA Modules:
  0.0 78.4 jit_solution(11915504684676512863)
XLA Ops:
  0.6 0.0 copy-start
  0.6 0.9 %copy-done = f32[3,8,16,128]{3,2,1,0:T(8,128)S(1)} copy-done((f32[3,8,16,128]{3,2,1,0:T(8,128)S(1)}, f32[3,8,16,128]{3,2,1,0:T(8,128)}, u32[]{:S(2)}) %copy-start) | copy-done | bytes 196632
  1.6 0.8 copy-done.3
  2.3 0.6 pack.1
  2.9 4.4 %collective-permute-start = (f32[112,128]{1,0:T(8,128)S(1)}, f32[112,128]{1,0:T(8,128)S(1)}, u32[]{:S(2)}, u32[]{:S(2)}) collective-permute-start(f32[112,128]{1,0:T(8,128)S(1)} %get-tuple-element.28), channel_id=1, source_target_pairs={{0,128},{128,0},{256,384},{384,256},{1,129},{129,1},{257,385},{385... | collective-permute-start | bytes 172040 | tf_op jit(solution)/shard_map/ppermute | solution.py:537
  7.3 0.7 collective-permute-start.1
  8.0 6.3 %collective-permute-start.2 = (f32[8,128]{1,0:T(8,128)S(1)}, f32[8,128]{1,0:T(8,128)S(1)}, u32[]{:S(2)}, u32[]{:S(2)}) collective-permute-start(f32[8,128]{1,0:T(8,128)S(1)} %get-tuple-element.30), channel_id=1, source_target_pairs={{0,1},{1,0},{2,3},{3,2},{4,5},{5,4},{6,7},{7,6},{8,9},{9,8},{10,11... | collective-permute-start | bytes 12296 | tf_op jit(solution)/shard_map/ppermute | solution.py:537
  14.3 1.9 %collective-permute-start.3 = (f32[8,128]{1,0:T(8,128)S(1)}, f32[8,128]{1,0:T(8,128)S(1)}, u32[]{:S(2)}, u32[]{:S(2)}) collective-permute-start(f32[8,128]{1,0:T(8,128)S(1)} %get-tuple-element.31), channel_id=1, source_target_pairs={{1,2},{3,4},{5,6},{2,1},{4,3},{6,5},{9,10},{11,12},{13,14},{10,9},... | collective-permute-start | bytes 12296 | tf_op jit(solution)/shard_map/ppermute | solution.py:542
  16.3 0.0 collective-permute-done.2.za
  16.3 3.0 %collective-permute-done.3.zb = f32[8,128]{1,0:T(8,128)S(1)} collective-permute-done((f32[8,128]{1,0:T(8,128)S(1)}, f32[8,128]{1,0:T(8,128)S(1)}, u32[]{:S(2)}, u32[]{:S(2)}) %collective-permute-start.3) | collective-permute-done | bytes 4128 | tf_op jit(solution)/shard_map/ppermute | solution.py:542
  19.3 0.0 collective-permute-done.xa
  19.3 0.0 collective-permute-done.1.xb
  19.3 0.0 copy-done.2
  19.3 2.9 %half.1 = (f32[3,128,128]{2,1,0:T(8,128)S(1)}, f32[136,128]{1,0:T(8,128)S(1)}, f32[136,128]{1,0:T(8,128)S(1)}, f32[48,128]{1,0:T(8,128)S(1)}, f32[16,128]{1,0:T(...) custom-call(f32[3,128,128]{2,1,0:T(8,128)S(1)} %bitcast.15, ...), custom_call_target="tpu_custom_call" | custom-call | flops 10000000 | bytes 900000 | tf_op jit(solution)/shard_map/half/pallas_call | solution.py:562
  22.1 0.7 collective-permute-start.4
  22.8 2.3 %collective-permute-start.5 = (f32[136,128]{1,0:T(8,128)S(1)}, f32[136,128]{1,0:T(8,128)S(1)}, u32[]{:S(2)}, u32[]{:S(2)}) collective-permute-start(f32[136,128]{1,0:T(8,128)S(1)} %get-tuple-element.38), channel_id=1, source_target_pairs={{0,8},{8,0},{16,24},{24,16},{32,40},{40,32},{48,56},{56,48},{64,72... | collective-permute-start | bytes 208904 | tf_op jit(solution)/shard_map/ppermute | solution.py:537
  25.1 0.0 collective-permute-done.4.yb
  25.1 2.8 %collective-permute-done.5.ya = f32[136,128]{1,0:T(8,128)S(1)} collective-permute-done((f32[136,128]{1,0:T(8,128)S(1)}, f32[136,128]{1,0:T(8,128)S(1)}, u32[]{:S(2)}, u32[]{:S(2)}) %collective-permute-start.5) | collective-permute-done | bytes 69664 | tf_op jit(solution)/shard_map/ppermute | solution.py:537
  27.9 0.7 copy-done.6
  28.5 0.0 copy-done.5
  28.6 1.1 %whole.1 = (f32[3,128,128]{2,1,0:T(8,128)}, f32[3,128,128]{2,1,0:T(8,128)S(1)}, f32[128,128]{1,0:T(8,128)S(1)}, f32[48,128]{1,0:T(8,128)S(1)}, f32[48,128]{1,0:T...) custom-call(f32[3,128,128]{2,1,0:T(8,128)S(1)} %get-tuple-element.33, ...), custom_call_target="tpu_custom_call" | custom-call | flops 2000000 | bytes 900000 | tf_op jit(solution)/shard_map/whole/pallas_call | solution.py:569
  29.7 0.0 copy-start.1
  29.7 9.4 %all_to_all.22 = f32[8,16,128]{2,1,0:T(8,128)S(1)} all-to-all(f32[8,16,128]{2,1,0:T(8,128)S(1)} %bitcast.24), channel_id=1, replica_groups=mesh['normal'=4,'strike'=16,'depth'=8] {'depth'}, dimensions={0} | all-to-all | bytes 131072 | tf_op jit(solution)/shard_map/all_to_all | solution.py:576
  39.1 0.6 add.1
  39.8 24.8 %all-to-all-start.1 = ((f32[64,1,128]{2,1,0:T(1,128)}), f32[64,1,128]{2,1,0:T(1,128)S(1)}, u32[]{:S(2)}, u32[]{:S(2)}) async-start(f32[64,1,128]{2,1,0:T(1,128)} %bitcast.11), calls=%async_computation.1 | async-start | bytes 65536 | tf_op jit(solution)/shard_map/all_to_all | solution.py:580
  64.6 2.9 %collective-permute-start.6 = (f32[48,128]{1,0:T(8,128)S(1)}, f32[48,128]{1,0:T(8,128)S(1)}, u32[]{:S(2)}, u32[]{:S(2)}) collective-permute-start(f32[48,128]{1,0:T(8,128)S(1)} %get-tuple-element.43), channel_id=1, source_target_pairs={{0,128},{128,0},{256,384},{384,256},{1,129},{129,1},{257,385},{385... | collective-permute-start | bytes 73736 | tf_op jit(solution)/shard_map/ppermute | solution.py:537
  67.5 0.7 collective-permute-start.7
  68.2 1.4 %collective-permute-done.6.xa2 = f32[48,128]{1,0:T(8,128)S(1)} collective-permute-done((f32[48,128]{1,0:T(8,128)S(1)}, f32[48,128]{1,0:T(8,128)S(1)}, u32[]{:S(2)}, u32[]{:S(2)}) %collective-permute-start.6) | collective-permute-done | bytes 24608 | tf_op jit(solution)/shard_map/ppermute | solution.py:537
  69.6 0.0 collective-permute-done.7.xb2
  69.6 3.4 %second.1 = f32[3,128,128]{2,1,0:T(8,128)} custom-call(f32[3,128,128]{2,1,0:T(8,128)S(1)} %get-tuple-element.42.now, f32[3,128,128]{2,1,0:T(8,128)S(1)} %bitcast.17, f32[128,128]{1,0:T(8,128)S(1)} %get-tuple-element.34.rw, f32[128,128]{1,0:T(8,128)S(1)} %get-tuple-element.35.scale, f32[48,128]{1,0:T(8,128)S(1)} %collective-permute-done.6.xa2, ...), custom_call_target="tpu_custom_call" | custom-call | flops 10000000 | bytes 900000 | tf_op jit(solution)/shard_map/second/pallas_call | solution.py:583
  73.0 4.7 %all-to-all-done.1 = f32[64,1,128]{2,1,0:T(1,128)S(1)} async-done(((f32[64,1,128]{2,1,0:T(1,128)}), f32[64,1,128]{2,1,0:T(1,128)S(1)}, u32[]{:S(2)}, u32[]{:S(2)}) %all-to-all-start.1) | async-done | bytes 32800 | tf_op jit(solution)/shard_map/all_to_all | solution.py:580
  77.7 0.7 final.1
  (7 shorter events, 0.0 us)
Async XLA Ops:
  0.6 0.9 %copy-start = (f32[3,8,16,128]{3,2,1,0:T(8,128)S(1)}, f32[3,8,16,128]{3,2,1,0:T(8,128)}, u32[]{:S(2)}) copy-start(f32[3,8,16,128]{3,2,1,0:T(8,128)} %param.6) | copy-start | bytes 589828
  1.6 0.8 copy-start.3
  2.3 16.9 %copy-start.2 = (f32[3,8,16,128]{3,2,1,0:T(8,128)S(1)}, f32[3,8,16,128]{3,2,1,0:T(8,128)}, u32[]{:S(2)}) copy-start(f32[3,8,16,128]{3,2,1,0:T(8,128)} %param.7) | copy-start | bytes 589828
  2.3 16.9 %copy-start.4 = (bf16[8,16,128]{2,1,0:T(8,128)(2,1)S(1)}, bf16[8,16,128]{2,1,0:T(8,128)(2,1)}, u32[]{:S(2)}) copy-start(bf16[8,16,128]{2,1,0:T(8,128)(2,1)} %param.9) | copy-start | bytes 98308
  2.9 16.3 %collective-permute-start = (f32[112,128]{1,0:T(8,128)S(1)}, f32[112,128]{1,0:T(8,128)S(1)}, u32[]{:S(2)}, u32[]{:S(2)}) collective-permute-start(f32[112,128]{1,0:T(8,128)S(1)} %get-tuple-element.28), channel_id=1, source_target_pairs={{0,128},{128,0},{256,384},{384,256},{1,129},{129,1},{257,385},{385... | collective-permute-start | bytes 172040 | tf_op jit(solution)/shard_map/ppermute | solution.py:537
  7.3 11.9 %collective-permute-start.1 = (f32[112,128]{1,0:T(8,128)S(1)}, f32[112,128]{1,0:T(8,128)S(1)}, u32[]{:S(2)}, u32[]{:S(2)}) collective-permute-start(f32[112,128]{1,0:T(8,128)S(1)} %get-tuple-element.29), channel_id=1, source_target_pairs={{128,256},{256,128},{129,257},{257,129},{130,258},{258,130},{131,2... | collective-permute-start | bytes 172040 | tf_op jit(solution)/shard_map/ppermute | solution.py:542
  8.0 8.3 %collective-permute-start.2 = (f32[8,128]{1,0:T(8,128)S(1)}, f32[8,128]{1,0:T(8,128)S(1)}, u32[]{:S(2)}, u32[]{:S(2)}) collective-permute-start(f32[8,128]{1,0:T(8,128)S(1)} %get-tuple-element.30), channel_id=1, source_target_pairs={{0,1},{1,0},{2,3},{3,2},{4,5},{5,4},{6,7},{7,6},{8,9},{9,8},{10,11... | collective-permute-start | bytes 12296 | tf_op jit(solution)/shard_map/ppermute | solution.py:537
  14.3 4.9 %collective-permute-start.3 = (f32[8,128]{1,0:T(8,128)S(1)}, f32[8,128]{1,0:T(8,128)S(1)}, u32[]{:S(2)}, u32[]{:S(2)}) collective-permute-start(f32[8,128]{1,0:T(8,128)S(1)} %get-tuple-element.31), channel_id=1, source_target_pairs={{1,2},{3,4},{5,6},{2,1},{4,3},{6,5},{9,10},{11,12},{13,14},{10,9},... | collective-permute-start | bytes 12296 | tf_op jit(solution)/shard_map/ppermute | solution.py:542
  22.1 3.0 %collective-permute-start.4 = (f32[136,128]{1,0:T(8,128)S(1)}, f32[136,128]{1,0:T(8,128)S(1)}, u32[]{:S(2)}, u32[]{:S(2)}) collective-permute-start(f32[136,128]{1,0:T(8,128)S(1)} %get-tuple-element.37), channel_id=1, source_target_pairs={{8,16},{24,32},{40,48},{56,64},{72,80},{88,96},{104,112},{16,8},{3... | collective-permute-start | bytes 208904 | tf_op jit(solution)/shard_map/ppermute | solution.py:542
  22.8 5.1 %collective-permute-start.5 = (f32[136,128]{1,0:T(8,128)S(1)}, f32[136,128]{1,0:T(8,128)S(1)}, u32[]{:S(2)}, u32[]{:S(2)}) collective-permute-start(f32[136,128]{1,0:T(8,128)S(1)} %get-tuple-element.38), channel_id=1, source_target_pairs={{0,8},{8,0},{16,24},{24,16},{32,40},{40,32},{48,56},{56,48},{64,72... | collective-permute-start | bytes 208904 | tf_op jit(solution)/shard_map/ppermute | solution.py:537
  27.9 0.7 copy-start.6
  27.9 0.7 copy-start.5
  29.7 39.9 %copy-start.1 = (f32[3,8,16,128]{3,2,1,0:T(8,128)S(1)}, f32[3,8,16,128]{3,2,1,0:T(8,128)}, u32[]{:S(2)}) copy-start(f32[3,8,16,128]{3,2,1,0:T(8,128)} %param.6) | copy-start | bytes 589828
  39.8 38.0 %all-to-all-start.1 = ((f32[64,1,128]{2,1,0:T(1,128)}), f32[64,1,128]{2,1,0:T(1,128)S(1)}, u32[]{:S(2)}, u32[]{:S(2)}) async-start(f32[64,1,128]{2,1,0:T(1,128)} %bitcast.11), calls=%async_computation.1 | async-start | bytes 65536 | tf_op jit(solution)/shard_map/all_to_all | solution.py:580
  64.6 5.0 %collective-permute-start.6 = (f32[48,128]{1,0:T(8,128)S(1)}, f32[48,128]{1,0:T(8,128)S(1)}, u32[]{:S(2)}, u32[]{:S(2)}) collective-permute-start(f32[48,128]{1,0:T(8,128)S(1)} %get-tuple-element.43), channel_id=1, source_target_pairs={{0,128},{128,0},{256,384},{384,256},{1,129},{129,1},{257,385},{385... | collective-permute-start | bytes 73736 | tf_op jit(solution)/shard_map/ppermute | solution.py:537
  67.5 2.1 %collective-permute-start.7 = (f32[48,128]{1,0:T(8,128)S(1)}, f32[48,128]{1,0:T(8,128)S(1)}, u32[]{:S(2)}, u32[]{:S(2)}) collective-permute-start(f32[48,128]{1,0:T(8,128)S(1)} %get-tuple-element.44), channel_id=1, source_target_pairs={{128,256},{256,128},{129,257},{257,129},{130,258},{258,130},{131,2... | collective-permute-start | bytes 73736 | tf_op jit(solution)/shard_map/ppermute | solution.py:542

commit v6 on v5

--- a/solution.py
+++ b/solution.py
@@ -165,9 +165,9 @@
     high[...] = jnp.where(even, near[rows, :], far[rows, :])
 
 
-def beside(index, count, got, stride, low, high):
-    below = pl.multiple_of(jnp.maximum(index - 1, 0) * stride, 8)
-    above = pl.multiple_of(jnp.minimum(index + 1, count - 1) * stride, 8)
+def beside(index, count, got, group, low, high):
+    below = pl.multiple_of((group * count + jnp.maximum(index - 1, 0)) * 8, 8)
+    above = pl.multiple_of((group * count + jnp.minimum(index + 1, count - 1)) * 8, 8)
     low[...] = jnp.where(index > 0, got[pl.ds(below, low.shape[0]), :], 0.0)
     high[...] = jnp.where(index < count - 1, got[pl.ds(above, high.shape[0]), :], 0.0)
 
@@ -315,10 +315,12 @@
 
 
 def half_kernel(
-    counts, now, prev, rig, rho, xa, xb, za, zb, zd_own,
-    base, yb, ya, early, mx, mz, xd, zd, rw, scale,
+    counts, now, prev, rig, rho, xa, xb, za, zb, zd_own, nodes_in, ids_in,
+    base, yb, ya, early, mx, mz, xd, zd, rw, scale, nodes, ids,
     acc, xu, zu, yu, yd,
 ):
+    nodes[...] = nodes_in[...]
+    ids[...] = ids_in[...]
     index = place()
     unpaired(index[0], xa, xb, xu, xd)
     unpaired(index[2], za, zb, zu, zd)
@@ -377,18 +379,15 @@
 
 
 def whole_kernel(
-    counts, base, now, rw, scale, early, yb, ya, mx, xd, zd, nodes_hbm, ids_hbm,
+    counts, base, now, rw, scale, early, yb, ya, mx, xd, zd, nodes, ids,
     out, kept, to_depth, xa2, xb2, zd2, my, y_low, y_high, r_high,
-    slip, yu, yd, xu2, xd2, zu2, nodes, ids, sems,
+    slip, yu, yd, xu2, xd2, zu2,
 ):
     middle = counts[0] // 2
     index = place()
     lane = lane_of()
     kappa, diagonal = np.float32(KAPPA), np.float32(KAPPA * D[4, 4])
     d44 = np.float32(D[4, 4])
-    copies = [pltpu.make_async_copy(nodes_hbm, nodes, sems.at[0]), pltpu.make_async_copy(ids_hbm, ids, sems.at[1])]
-    for copy in copies:
-        copy.start()
     unpaired(index[1], ya, yb, yu, yd)
     for c in range(3):
         for k in range(16):
@@ -449,20 +448,30 @@
     zu2[...] = interleaved(sent + [None], lane, 0)
     zd2[...] = first_lanes(lambda c, rows: out[c, rows, :], None, lane)
     paired(index[0], xu2, xd2, xa2, xb2)
-    for copy in copies:
-        copy.wait()
     tile = patch_tile(counts[2], slip[...], nodes[...], ids[...])
     for d in range(counts[2]):
-        to_depth[pl.ds(16 * d, 8), :] = jnp.where(d > index[2], zu2[...], zd2[...])
-        to_depth[pl.ds(16 * d + 8, 8), :] = jnp.broadcast_to(tile[d : d + 1, :], (8, NZL))
-
-
-def sum_kernel(counts, got, to_face):
-    row = got[pl.ds(8, 8), :]
-    for d in range(1, counts[2]):
-        row = row + got[pl.ds(16 * d + 8, 8), :]
-    for k in range(counts[0] * counts[1] // 8):
-        to_face[pl.ds(8 * k, 8), :] = row
+        chunk = with_row(jnp.where(d > index[2], zu2[...], zd2[...]), tile[d : d + 1, :], lane)
+        for n in range(counts[0]):
+            to_depth[pl.ds(8 * (n * counts[2] + d), 8), :] = chunk
+
+
+def with_row(halo, row, lane):
+    sub = lax.broadcasted_iota(jnp.int32, (8, NZL), 0)
+    row = jnp.broadcast_to(row, (8, NZL))
+    spread = jnp.where(sub == 0, rolled(row, 64), jnp.where(sub == 1, row, 0.0))
+    return jnp.where(lane < 64, halo, spread)
+
+
+def sum_kernel(counts, got, to_strike):
+    total_tile = got[pl.ds(0, 8), :]
+    for n in range(1, counts[0] * counts[2]):
+        total_tile = total_tile + got[pl.ds(8 * n, 8), :]
+    lane = lane_of()
+    low = jnp.broadcast_to(rolled(total_tile, 64)[0:1, :], (8, NZL))
+    high = jnp.broadcast_to(total_tile[1:2, :], (8, NZL))
+    row = jnp.where(lane < 64, low, high)
+    for k in range((counts[1] + 7) // 8):
+        to_strike[pl.ds(8 * k, min(8, counts[1])), :] = row[: min(8, counts[1]), :]
 
 
 def second_kernel(
@@ -471,7 +480,7 @@
 ):
     index = place()
     unpaired(index[0], xa2, xb2, xu2, xd2)
-    beside(index[2], counts[2], got_z, 16, zu2, zd2)
+    beside(index[2], counts[2], got_z, index[0], zu2, zd2)
     closing_z = zu2[...] + mz[...] * zd2_own[...]
 
     def low_x(c, offset, plane, v0):
@@ -524,7 +533,7 @@
     specs = {} if in_specs is None else {"in_specs": in_specs}
     return pl.pallas_call(
         kernel,
-        out_shape=[jax.ShapeDtypeStruct(shape, F32) for shape in outs],
+        out_shape=[jax.ShapeDtypeStruct(o, F32) if isinstance(o, tuple) else jax.typeof(o) for o in outs],
         scratch_shapes=[pltpu.VMEM(shape, F32) if isinstance(shape, tuple) else shape for shape in scratch],
         compiler_params=pltpu.CompilerParams(vmem_limit_bytes=16 * 2**20),
         cost_estimate=pl.CostEstimate(flops=flops, bytes_accessed=moved, transcendentals=0),
@@ -559,25 +568,22 @@
     )(now, rig)
     xa, xb = swap_near(xa, "normal"), swap_far(xb, "normal")
     zb, za = swap_far(zb, "depth"), swap_near(za, "depth")
-    base, yb, ya, early, mx, mz, xd, zd, rw, scale = call(
+    base, yb, ya, early, mx, mz, xd, zd, rw, scale, nodes, ids = call(
         functools.partial(half_kernel, counts), "half",
-        [flat, y_up, y_up, faces, (16, NZL), tile, x_down, tile, block, block],
+        [flat, y_up, y_up, faces, (16, NZL), tile, x_down, tile, block, block, nodes, ids],
         [flat, x_up, tile, y_up, y_down], flops=10_000_000, moved=900_000,
-    )(now, prev, rig, rho, xa, xb, za, zb, zd_own)
+    )(now, prev, rig, rho, xa, xb, za, zb, zd_own, nodes, ids)
     yb, ya = swap_far(yb, "strike"), swap_near(ya, "strike")
-    inside, outside = pl.BlockSpec(memory_space=pltpu.VMEM), pl.BlockSpec(memory_space=pltpu.HBM)
     mid, kept, to_depth, xa2, xb2, zd2, my, y_low, y_high, r_high = call(
         functools.partial(whole_kernel, counts), "whole",
-        [flat, flat, (16 * counts[2], NZL), faces, faces, tile, tile, strip, strip, tile],
-        [faces, y_up, y_down, faces, faces, tile, pltpu.VMEM(nodes.shape, jnp.int32), pltpu.VMEM(ids.shape, jnp.int32),
-         pltpu.SemaphoreType.DMA((2,))],
-        flops=2_000_000, moved=900_000, in_specs=[inside] * 10 + [outside] * 2,
+        [flat, flat, (8 * counts[0] * counts[2], NZL), faces, faces, tile, tile, strip, strip, tile],
+        [faces, y_up, y_down, faces, faces, tile], flops=2_000_000, moved=900_000,
     )(base, now, rw, scale, early, yb, ya, mx, xd, zd, nodes, ids)
-    got_z = lax.all_to_all(to_depth, "depth", 0, 0, tiled=True)
-    (to_face,) = call(
-        functools.partial(sum_kernel, counts), "add", [(counts[0] * counts[1], NZL)], flops=10_000, moved=80_000,
+    got_z = lax.all_to_all(to_depth, ("normal", "depth"), 0, 0, tiled=True)
+    (to_strike,) = call(
+        functools.partial(sum_kernel, counts), "add", [(counts[1], NZL)], flops=10_000, moved=150_000,
     )(got_z)
-    got_face = lax.all_to_all(to_face, ("normal", "strike"), 0, 0, tiled=True)
+    got_face = lax.all_to_all(to_strike, "strike", 0, 0, tiled=True)
     xa2, xb2 = swap_near(xa2, "normal"), swap_far(xb2, "normal")
     (share,) = call(final_kernel, "final", [(2, 3)], flops=10_000, moved=10_000)(got_face)
     (following,) = call(

time: 78.9 us -> 82.3 us (1.043)
  blocking collectives: 9.42 us -> 17.8 us
  starting transfers between devices: 44.6 us -> 38.6 us
  waiting for transfers between devices: 11.8 us -> 13 us
    all_to_all x1, blocking collectives: 9.42 us -> 17.8 us  [local(): got_z = lax.all_to_all(to_depth, ('normal', 'depth'), 0, 0, tiled=True)]
    all_to_all x1, starting transfers between devices: 24.8 us -> 19.4 us  [local(): got_face = lax.all_to_all(to_strike, 'strike', 0, 0, tiled=True)]
where the time goes in v6:
time: 82.3 us; the launch traced here: 81.8 us
  starting transfers between devices  38.6 us (47%)
  blocking collectives  17.8 us (22%)
  waiting for transfers between devices  13 us (16%)
  Pallas kernels  9.38 us (11%)
  local copies, waits for them, and re-layouts  2.36 us (3%)
    all_to_all x1, starting transfers between devices, local(): got_face = lax.all_to_all(to_strike, 'strike', 0, 0, tiled=True)  19.4 us
    all_to_all x1, blocking collectives, local(): got_z = lax.all_to_all(to_depth, ('normal', 'depth'), 0, 0, tiled=True)  17.8 us
    ppermute x4, starting transfers between devices, swap_near(): lax.ppermute(value, axis, [(i, i ^ 1) for i in range(lax.axis_size(axis))])  15.3 us
    all_to_all x1, waiting for transfers between devices, local(): got_face = lax.all_to_all(to_strike, 'strike', 0, 0, tiled=True)  5.3 us
    ppermute x4, waiting for transfers between devices, swap_near(): lax.ppermute(value, axis, [(i, i ^ 1) for i in range(lax.axis_size(axis))])  4.67 us
    ppermute x4, starting transfers between devices, swap_far(): lax.ppermute(value, axis, [(i, i + 1) for i in lower] + [(i + 1, i) for i...  3.91 us
    pallas_call x1, Pallas kernels, local(): call(functools.partial(second_kernel, counts), 'second', [flat], [flat, f...  3.45 us
    ppermute x4, waiting for transfers between devices, swap_far(): lax.ppermute(value, axis, [(i, i + 1) for i in lower] + [(i + 1, i) for i...  3 us
  transfers between devices with their start and end apart: 9, of which 4 were waited for; matrix products, arithmetic and copies ran while one was open for 0% of the time, Pallas kernels for 4%

profile of v6, /device:TPU:1, one launch (start us, length us, event | category | flops | bytes accessed | tf_op | source)
XLA Modules:
  0.0 81.8 jit_solution(8698973551988050588)
XLA Ops:
  0.6 0.0 copy-start
  0.6 0.9 %copy-done = f32[3,8,16,128]{3,2,1,0:T(8,128)S(1)} copy-done((f32[3,8,16,128]{3,2,1,0:T(8,128)S(1)}, f32[3,8,16,128]{3,2,1,0:T(8,128)}, u32[]{:S(2)}) %copy-start) | copy-done | bytes 196632
  1.6 0.8 copy-done.3
  2.3 0.6 pack.1
  2.9 4.4 %collective-permute-start = (f32[112,128]{1,0:T(8,128)S(1)}, f32[112,128]{1,0:T(8,128)S(1)}, u32[]{:S(2)}, u32[]{:S(2)}) collective-permute-start(f32[112,128]{1,0:T(8,128)S(1)} %get-tuple-element.30), channel_id=1, source_target_pairs={{0,128},{128,0},{256,384},{384,256},{1,129},{129,1},{257,385},{385... | collective-permute-start | bytes 172040 | tf_op jit(solution)/shard_map/ppermute | solution.py:546
  7.3 0.7 collective-permute-start.1
  8.0 6.3 %collective-permute-start.2 = (f32[8,128]{1,0:T(8,128)S(1)}, f32[8,128]{1,0:T(8,128)S(1)}, u32[]{:S(2)}, u32[]{:S(2)}) collective-permute-start(f32[8,128]{1,0:T(8,128)S(1)} %get-tuple-element.32), channel_id=1, source_target_pairs={{0,1},{1,0},{2,3},{3,2},{4,5},{5,4},{6,7},{7,6},{8,9},{9,8},{10,11... | collective-permute-start | bytes 12296 | tf_op jit(solution)/shard_map/ppermute | solution.py:546
  14.3 1.9 %collective-permute-start.3 = (f32[8,128]{1,0:T(8,128)S(1)}, f32[8,128]{1,0:T(8,128)S(1)}, u32[]{:S(2)}, u32[]{:S(2)}) collective-permute-start(f32[8,128]{1,0:T(8,128)S(1)} %get-tuple-element.33), channel_id=1, source_target_pairs={{1,2},{3,4},{5,6},{2,1},{4,3},{6,5},{9,10},{11,12},{13,14},{10,9},... | collective-permute-start | bytes 12296 | tf_op jit(solution)/shard_map/ppermute | solution.py:551
  16.3 0.0 collective-permute-done.2.za
  16.3 3.0 %collective-permute-done.3.zb = f32[8,128]{1,0:T(8,128)S(1)} collective-permute-done((f32[8,128]{1,0:T(8,128)S(1)}, f32[8,128]{1,0:T(8,128)S(1)}, u32[]{:S(2)}, u32[]{:S(2)}) %collective-permute-start.3) | collective-permute-done | bytes 4128 | tf_op jit(solution)/shard_map/ppermute | solution.py:551
  19.3 0.0 collective-permute-done.xa
  19.3 0.0 collective-permute-done.1.xb
  19.3 0.0 copy-start.5
  19.3 0.0 copy-done.2
  19.3 0.6 copy-done.6
  19.9 0.0 copy-done.5
  20.0 2.9 %half.1 = (f32[3,128,128]{2,1,0:T(8,128)S(1)}, f32[136,128]{1,0:T(8,128)S(1)}, f32[136,128]{1,0:T(8,128)S(1)}, f32[48,128]{1,0:T(8,128)S(1)}, f32[16,128]{1,0:T(...) custom-call(f32[3,128,128]{2,1,0:T(8,128)S(1)} %bitcast.15, ...), custom_call_target="tpu_custom_call" | custom-call | flops 10000000 | bytes 900000 | tf_op jit(solution)/shard_map/half/pallas_call | solution.py:571
  22.8 0.7 collective-permute-start.4
  23.5 2.3 %collective-permute-start.5 = (f32[136,128]{1,0:T(8,128)S(1)}, f32[136,128]{1,0:T(8,128)S(1)}, u32[]{:S(2)}, u32[]{:S(2)}) collective-permute-start(f32[136,128]{1,0:T(8,128)S(1)} %get-tuple-element.40), channel_id=1, source_target_pairs={{0,8},{8,0},{16,24},{24,16},{32,40},{40,32},{48,56},{56,48},{64,72... | collective-permute-start | bytes 208904 | tf_op jit(solution)/shard_map/ppermute | solution.py:546
  25.8 0.0 collective-permute-done.4.yb
  25.8 2.8 %collective-permute-done.5.ya = f32[136,128]{1,0:T(8,128)S(1)} collective-permute-done((f32[136,128]{1,0:T(8,128)S(1)}, f32[136,128]{1,0:T(8,128)S(1)}, u32[]{:S(2)}, u32[]{:S(2)}) %collective-permute-start.5) | collective-permute-done | bytes 69664 | tf_op jit(solution)/shard_map/ppermute | solution.py:546
  28.5 1.1 %whole.1 = (f32[3,128,128]{2,1,0:T(8,128)}, f32[3,128,128]{2,1,0:T(8,128)S(1)}, f32[256,128]{1,0:T(8,128)S(1)}, f32[48,128]{1,0:T(8,128)S(1)}, f32[48,128]{1,0:T...) custom-call(f32[3,128,128]{2,1,0:T(8,128)S(1)} %get-tuple-element.35, ...), custom_call_target="tpu_custom_call" | custom-call | flops 2000000 | bytes 900000 | tf_op jit(solution)/shard_map/whole/pallas_call | solution.py:577
  29.7 17.8 %all_to_all.22 = f32[32,8,128]{2,1,0:T(8,128)S(1)} all-to-all(f32[32,8,128]{2,1,0:T(8,128)S(1)} %bitcast.23), channel_id=1, replica_groups=mesh['normal'=4,'strike'=16,'depth'=8] {'normal','depth'}, dimensions={0} | all-to-all | bytes 262144 | tf_op jit(solution)/shard_map/all_to_all | solution.py:582
  47.5 0.7 add.1
  48.2 19.4 %all-to-all-start.1 = ((f32[16,1,128]{2,1,0:T(1,128)}), f32[16,1,128]{2,1,0:T(1,128)S(1)}, u32[]{:S(2)}, u32[]{:S(2)}) async-start(f32[16,1,128]{2,1,0:T(1,128)} %bitcast.11), calls=%async_computation.1 | async-start | bytes 16384 | tf_op jit(solution)/shard_map/all_to_all | solution.py:586
  67.6 2.3 %collective-permute-start.6 = (f32[48,128]{1,0:T(8,128)S(1)}, f32[48,128]{1,0:T(8,128)S(1)}, u32[]{:S(2)}, u32[]{:S(2)}) collective-permute-start(f32[48,128]{1,0:T(8,128)S(1)} %get-tuple-element.47), channel_id=1, source_target_pairs={{0,128},{128,0},{256,384},{384,256},{1,129},{129,1},{257,385},{385... | collective-permute-start | bytes 73736 | tf_op jit(solution)/shard_map/ppermute | solution.py:546
  69.9 0.7 collective-permute-start.7
  70.5 1.9 %collective-permute-done.6.xa2 = f32[48,128]{1,0:T(8,128)S(1)} collective-permute-done((f32[48,128]{1,0:T(8,128)S(1)}, f32[48,128]{1,0:T(8,128)S(1)}, u32[]{:S(2)}, u32[]{:S(2)}) %collective-permute-start.6) | collective-permute-done | bytes 24608 | tf_op jit(solution)/shard_map/ppermute | solution.py:546
  72.4 0.0 collective-permute-done.7.xb2
  72.4 3.4 %second.1 = f32[3,128,128]{2,1,0:T(8,128)} custom-call(f32[3,128,128]{2,1,0:T(8,128)S(1)} %get-tuple-element.46.now, f32[3,128,128]{2,1,0:T(8,128)S(1)} %bitcast.17, f32[128,128]{1,0:T(8,128)S(1)} %get-tuple-element.36.rw, f32[128,128]{1,0:T(8,128)S(1)} %get-tuple-element.37.scale, f32[48,128]{1,0:T(8,128)S(1)} %collective-permute-done.6.xa2, ...), custom_call_target="tpu_custom_call" | custom-call | flops 10000000 | bytes 900000 | tf_op jit(solution)/shard_map/second/pallas_call | solution.py:589
  75.9 5.3 %all-to-all-done.1 = f32[16,1,128]{2,1,0:T(1,128)S(1)} async-done(((f32[16,1,128]{2,1,0:T(1,128)}), f32[16,1,128]{2,1,0:T(1,128)S(1)}, u32[]{:S(2)}, u32[]{:S(2)}) %all-to-all-start.1) | async-done | bytes 8224 | tf_op jit(solution)/shard_map/all_to_all | solution.py:586
  81.2 0.7 final.1
  (7 shorter events, 0.0 us)
Async XLA Ops:
  0.6 0.9 %copy-start = (f32[3,8,16,128]{3,2,1,0:T(8,128)S(1)}, f32[3,8,16,128]{3,2,1,0:T(8,128)}, u32[]{:S(2)}) copy-start(f32[3,8,16,128]{3,2,1,0:T(8,128)} %param.6) | copy-start | bytes 589828
  1.6 0.8 copy-start.3
  2.3 17.0 %copy-start.2 = (f32[3,8,16,128]{3,2,1,0:T(8,128)S(1)}, f32[3,8,16,128]{3,2,1,0:T(8,128)}, u32[]{:S(2)}) copy-start(f32[3,8,16,128]{3,2,1,0:T(8,128)} %param.7) | copy-start | bytes 589828
  2.3 17.0 %copy-start.4 = (bf16[8,16,128]{2,1,0:T(8,128)(2,1)S(1)}, bf16[8,16,128]{2,1,0:T(8,128)(2,1)}, u32[]{:S(2)}) copy-start(bf16[8,16,128]{2,1,0:T(8,128)(2,1)} %param.9) | copy-start | bytes 98308
  2.9 16.3 %collective-permute-start = (f32[112,128]{1,0:T(8,128)S(1)}, f32[112,128]{1,0:T(8,128)S(1)}, u32[]{:S(2)}, u32[]{:S(2)}) collective-permute-start(f32[112,128]{1,0:T(8,128)S(1)} %get-tuple-element.30), channel_id=1, source_target_pairs={{0,128},{128,0},{256,384},{384,256},{1,129},{129,1},{257,385},{385... | collective-permute-start | bytes 172040 | tf_op jit(solution)/shard_map/ppermute | solution.py:546
  7.3 11.9 %collective-permute-start.1 = (f32[112,128]{1,0:T(8,128)S(1)}, f32[112,128]{1,0:T(8,128)S(1)}, u32[]{:S(2)}, u32[]{:S(2)}) collective-permute-start(f32[112,128]{1,0:T(8,128)S(1)} %get-tuple-element.31), channel_id=1, source_target_pairs={{128,256},{256,128},{129,257},{257,129},{130,258},{258,130},{131,2... | collective-permute-start | bytes 172040 | tf_op jit(solution)/shard_map/ppermute | solution.py:551
  8.0 8.3 %collective-permute-start.2 = (f32[8,128]{1,0:T(8,128)S(1)}, f32[8,128]{1,0:T(8,128)S(1)}, u32[]{:S(2)}, u32[]{:S(2)}) collective-permute-start(f32[8,128]{1,0:T(8,128)S(1)} %get-tuple-element.32), channel_id=1, source_target_pairs={{0,1},{1,0},{2,3},{3,2},{4,5},{5,4},{6,7},{7,6},{8,9},{9,8},{10,11... | collective-permute-start | bytes 12296 | tf_op jit(solution)/shard_map/ppermute | solution.py:546
  14.3 4.9 %collective-permute-start.3 = (f32[8,128]{1,0:T(8,128)S(1)}, f32[8,128]{1,0:T(8,128)S(1)}, u32[]{:S(2)}, u32[]{:S(2)}) collective-permute-start(f32[8,128]{1,0:T(8,128)S(1)} %get-tuple-element.33), channel_id=1, source_target_pairs={{1,2},{3,4},{5,6},{2,1},{4,3},{6,5},{9,10},{11,12},{13,14},{10,9},... | collective-permute-start | bytes 12296 | tf_op jit(solution)/shard_map/ppermute | solution.py:551
  19.3 0.7 copy-start.6
  19.3 0.7 copy-start.5
  22.8 3.0 %collective-permute-start.4 = (f32[136,128]{1,0:T(8,128)S(1)}, f32[136,128]{1,0:T(8,128)S(1)}, u32[]{:S(2)}, u32[]{:S(2)}) collective-permute-start(f32[136,128]{1,0:T(8,128)S(1)} %get-tuple-element.39), channel_id=1, source_target_pairs={{8,16},{24,32},{40,48},{56,64},{72,80},{88,96},{104,112},{16,8},{3... | collective-permute-start | bytes 208904 | tf_op jit(solution)/shard_map/ppermute | solution.py:551
  23.5 5.1 %collective-permute-start.5 = (f32[136,128]{1,0:T(8,128)S(1)}, f32[136,128]{1,0:T(8,128)S(1)}, u32[]{:S(2)}, u32[]{:S(2)}) collective-permute-start(f32[136,128]{1,0:T(8,128)S(1)} %get-tuple-element.40), channel_id=1, source_target_pairs={{0,8},{8,0},{16,24},{24,16},{32,40},{40,32},{48,56},{56,48},{64,72... | collective-permute-start | bytes 208904 | tf_op jit(solution)/shard_map/ppermute | solution.py:546
  29.7 42.8 %copy-start.1 = (f32[3,8,16,128]{3,2,1,0:T(8,128)S(1)}, f32[3,8,16,128]{3,2,1,0:T(8,128)}, u32[]{:S(2)}) copy-start(f32[3,8,16,128]{3,2,1,0:T(8,128)} %param.6) | copy-start | bytes 589828
  48.2 33.0 %all-to-all-start.1 = ((f32[16,1,128]{2,1,0:T(1,128)}), f32[16,1,128]{2,1,0:T(1,128)S(1)}, u32[]{:S(2)}, u32[]{:S(2)}) async-start(f32[16,1,128]{2,1,0:T(1,128)} %bitcast.11), calls=%async_computation.1 | async-start | bytes 16384 | tf_op jit(solution)/shard_map/all_to_all | solution.py:586
  67.6 4.9 %collective-permute-start.6 = (f32[48,128]{1,0:T(8,128)S(1)}, f32[48,128]{1,0:T(8,128)S(1)}, u32[]{:S(2)}, u32[]{:S(2)}) collective-permute-start(f32[48,128]{1,0:T(8,128)S(1)} %get-tuple-element.47), channel_id=1, source_target_pairs={{0,128},{128,0},{256,384},{384,256},{1,129},{129,1},{257,385},{385... | collective-permute-start | bytes 73736 | tf_op jit(solution)/shard_map/ppermute | solution.py:546
  69.9 2.6 %collective-permute-start.7 = (f32[48,128]{1,0:T(8,128)S(1)}, f32[48,128]{1,0:T(8,128)S(1)}, u32[]{:S(2)}, u32[]{:S(2)}) collective-permute-start(f32[48,128]{1,0:T(8,128)S(1)} %get-tuple-element.48), channel_id=1, source_target_pairs={{128,256},{256,128},{129,257},{257,129},{130,258},{258,130},{131,2... | collective-permute-start | bytes 73736 | tf_op jit(solution)/shard_map/ppermute | solution.py:551

commit v7 on v5

--- a/solution.py
+++ b/solution.py
@@ -165,14 +165,14 @@
     high[...] = jnp.where(even, near[rows, :], far[rows, :])
 
 
-def beside(index, count, got, stride, low, high):
-    below = pl.multiple_of(jnp.maximum(index - 1, 0) * stride, 8)
-    above = pl.multiple_of(jnp.minimum(index + 1, count - 1) * stride, 8)
+def beside(index, count, got, low, high):
+    below = pl.multiple_of((jnp.maximum(index - 1, 0)) * 8, 8)
+    above = pl.multiple_of((jnp.minimum(index + 1, count - 1)) * 8, 8)
     low[...] = jnp.where(index > 0, got[pl.ds(below, low.shape[0]), :], 0.0)
     high[...] = jnp.where(index < count - 1, got[pl.ds(above, high.shape[0]), :], 0.0)
 
 
-def pack_kernel(now_hbm, rig_hbm, xa, xb, za, zb, zd, now, rig, rw, xu, xd, zu, sems):
+def pack_kernel(now_hbm, rig_hbm, xa, xb, za, zb, zd, tails, now, rig, rw, xu, xd, zu, sems):
     copies = [pltpu.make_async_copy(rig_hbm, rig, sems.at[0]), pltpu.make_async_copy(now_hbm, now, sems.at[1])]
     for copy in copies:
         copy.start()
@@ -190,10 +190,12 @@
             xu[pl.ds(48 + 16 * c + 8 * half, 8), :] = grad
             xd[pl.ds(16 * c + 8 * half, 8), :] = now[c, x_rows(0, half), :]
     back = lambda t: [rolled(t, 3 - a) for a in range(4)]
-    r = back(last_lanes(lambda rows: rw[rows, :], lane))
+    tails[pl.ds(24, 8), :] = last_lanes(lambda rows: rw[rows, :], lane)
+    r = back(tails[pl.ds(24, 8), :])
     parts, grads = [], []
     for c in range(3):
-        part, grad = open_terms(back(last_lanes(lambda rows: now[c, rows, :], lane)), r)
+        tails[pl.ds(8 * c, 8), :] = last_lanes(lambda rows: now[c, rows, :], lane)
+        part, grad = open_terms(back(tails[pl.ds(8 * c, 8), :]), r)
         parts.append(part)
         grads.append(grad)
     zu[...] = jnp.where(
@@ -203,14 +205,6 @@
     index = place()
     paired(index[0], xu, xd, xa, xb)
     paired(index[2], zu, zd, za, zb)
-
-
-def from_fourth(tile, lane):
-    phase = lane & 3
-    out = tile
-    for j in range(3):
-        out = jnp.where(phase == j, rolled(tile, j - 3), out)
-    return out
 
 
 def advance(now, prev, rw, low, high_v, high_r, scale, ghost_z, ghost_rz, closing_z, index, store, acc, on_first):
@@ -234,6 +228,7 @@
         return carry
 
     lax.fori_loop(0, 3, along_y, 0)
+    alone = ghost_z is None
 
     lane = lane_of()
     phase = lane & 3
@@ -251,13 +246,15 @@
         offset = half * 8
         rows = [pl.ds(pl.multiple_of(x * NYL + offset, 8), 8) for x in range(NXL)]
         plane = pl.ds(pl.multiple_of(16 * c + offset, 8), 8)
-        v = [now[c, rows[x], :] for x in range(NXL)] + [high_v[0][plane, :]]
-        r = [rw[rows[x], :] for x in range(NXL)] + [high_r[0][pl.ds(pl.multiple_of(offset, 8), 8), :]]
-        carried = low[0](c, offset, plane, v[0])
+        none = jnp.zeros((8, NZL), F32)
+        v = [now[c, rows[x], :] for x in range(NXL)] + [none if alone else high_v[0][plane, :]]
+        r = [rw[rows[x], :] for x in range(NXL)]
+        r.append(none if alone else high_r[0][pl.ds(pl.multiple_of(offset, 8), 8), :])
+        carried = none if alone else low[0](c, offset, plane, v[0])
         back = NZL - (4 * half + c)
-        ghost_v = pltpu.roll(ghost_z, back, 1)
-        ghost_r = pltpu.roll(ghost_rz, NZL - 4 * half, 1)
-        closing = pltpu.roll(closing_z, back, 1)
+        ghost_v = 0.0 if alone else pltpu.roll(ghost_z, back, 1)
+        ghost_r = 0.0 if alone else pltpu.roll(ghost_rz, NZL - 4 * half, 1)
+        closing = 0.0 if alone else pltpu.roll(closing_z, back, 1)
         for e in range(2):
             terms = element(v[4 * e : 4 * e + 5], r[4 * e : 4 * e + 5])
             if e == 0:
@@ -267,8 +264,8 @@
                 force = terms[a] + acc[c, rows[x], :]
                 if a == 0:
                     force = (terms[0] * at_x if e == 0 else terms[0]) + carried + acc[c, rows[x], :]
-                vx = jnp.where(first, rolled(ghost_v, -8 * x), v[x])
-                rx = jnp.where(first, rolled(ghost_r, -8 * x), r[x])
+                vx = jnp.where(first, ghost_v if alone else rolled(ghost_v, -8 * x), v[x])
+                rx = jnp.where(first, ghost_r if alone else rolled(ghost_r, -8 * x), r[x])
                 vm = [v[x]] + [rolled(v[x], k) for k in range(1, 4)]
                 vp = [None] + [rolled(vx, -k) for k in range(1, 5)]
                 g = gm[0] * v[x]
@@ -290,7 +287,7 @@
                 tail = last[3] * q + last[4] * q4
                 for b in range(3):
                     tail = tail + last[b] * qm[3 - b]
-                tail = jnp.where(first, rolled(closing, -8 * x), rolled(tail, 1))
+                tail = jnp.where(first, closing if alone else rolled(closing, -8 * x), rolled(tail, 1))
                 force = force + own * edge + tail
                 after = (v[x] + v[x]) - prev[c, rows[x], :] - scale[rows[x], :] * force
                 store(c, x, rows[x], plane, after)
@@ -314,44 +311,89 @@
     return jnp.where((pos == 0) & is_first, np.float32(W0), out)
 
 
-def half_kernel(
-    counts, now, prev, rig, rho, xa, xb, za, zb, zd_own,
-    base, yb, ya, early, mx, mz, xd, zd, rw, scale,
-    acc, xu, zu, yu, yd,
+def inner_kernel(now, prev, rig, rho, nodes_in, ids_in, base, term, rw, scale, nodes, ids, acc):
+    nodes[...] = nodes_in[...]
+    ids[...] = ids_in[...]
+    widen(rig, rw)
+    step_scale(rho, scale)
+
+    def store(c, x, rows, plane, after):
+        base[c, rows, :] = after
+
+    def on_first(c, plane, carried, own):
+        term[plane, :] = own
+
+    nothing = (None, None)
+    advance(now, prev, rw, nothing, nothing, nothing, scale, None, None, None, place(), store, acc, on_first)
+
+
+def spread_from(tile, lane, source):
+    phase = lane & 3
+    out = tile
+    for j in range(4):
+        if j != source:
+            out = jnp.where(phase == j, rolled(tile, j - source), out)
+    return out
+
+
+def edge_kernel(
+    counts, inner, now, rw, scale, term, tails, xa, xb, za, zb, zd_own,
+    base, yb, ya, early, mx, mz, xd, zd,
+    xu, zu, yu, yd,
 ):
     index = place()
     unpaired(index[0], xa, xb, xu, xd)
     unpaired(index[2], za, zb, zu, zd)
-    widen(rig, rw)
-    step_scale(rho, scale)
     lane = lane_of()
+    phase = lane & 3
     has_x, has_z = (index[0] > 0).astype(F32), (index[2] > 0).astype(F32)
-    kappa, diagonal = np.float32(KAPPA), np.float32(KAPPA * D[4, 4])
+    kappa, diagonal, d44 = np.float32(KAPPA), np.float32(KAPPA * D[4, 4]), np.float32(D[4, 4])
+
+    own, above, below = zd_own[...], zu[...], zd[...]
+    r_first = spread_from(own, lane, 3)
+    gain = (spread_from(above, lane, 3) + diagonal * r_first) * has_z
+    mz[...] = gain
+    s_first = jnp.zeros((8, NZL), F32)
+    for k in range(16):
+        s_first = jnp.where(lane == 4 * k, rolled(scale[pl.ds(8 * k, 8), :], 4 * k), s_first)
+    closing = spread_from(s_first, lane, 0) * (above + kappa * r_first * rolled(above, 64) + gain * own)
+    r_tail = tails[pl.ds(24, 8), :]
+    s_tail = last_lanes(lambda rows: scale[rows, :], lane)
+    weights = [
+        lane_table(phase, [E[a, a + k] * D[a + k, 4] if 0 <= a + k <= 3 else 0 for a in range(4)]) for k in range(-3, 4)
+    ]
+    by_value = s_tail * sum(w * rolled(r_tail, -k) for w, k in zip(weights, range(-3, 4)))
+    by_flux = s_tail * lane_table(phase, [E[a, 4] for a in range(4)])
+    r_below = spread_from(below, lane, 3)
+    last = lane >= NZL - 4
+    for c in range(3):
+        tail = tails[pl.ds(8 * c, 8), :]
+        grad = spread_from(total([(D[4, a], rolled(tail, 3 - a)) for a in range(4)]), lane, 3)
+        value = spread_from(below, lane, c)
+        taken = by_value * value + by_flux * (r_below * (grad + d44 * value))
+        for k in range(16):
+            rows = pl.ds(8 * k, 8)
+            off = jnp.where(lane == 0, rolled(closing, -(4 * k + c)), 0.0)
+            base[c, rows, :] = inner[c, rows, :] - jnp.where(last, rolled(taken, NZL - 4 - 4 * k), off)
+
     for half in range(2):
         rows = pl.ds(8 * half, 8)
-        mx[rows, :] = (xu[pl.ds(96 + 8 * half, 8), :] + diagonal * rw[x_rows(0, half), :]) * has_x
-    own, above = zd_own[...], zu[...]
-    r_first = from_fourth(own, lane)
-    scale_z = (from_fourth(above, lane) + diagonal * r_first) * has_z
-    mz[...] = scale_z
-    closing_z = above + kappa * r_first * rolled(above, 64) + scale_z * own
-
-    def low_x(c, offset, plane, v0):
-        rows = pl.ds(pl.multiple_of(offset, 8), 8)
-        grad = xu[pl.ds(pl.multiple_of(48 + 16 * c + offset, 8), 8), :]
-        return xu[plane, :] + kappa * rw[rows, :] * grad + mx[rows, :] * v0
-
-    def store(c, x, rows, plane, after):
-        base[c, rows, :] = after
-
-    def on_first(c, plane, carried, term):
-        early[plane, :] = carried - term
-
-    below = zd[...]
-    advance(
-        now, prev, rw, (low_x, None), (xd, None), (xd.at[pl.ds(48, 16)], None), scale,
-        below, rolled(below, -3), closing_z, index, store, acc, on_first,
-    )
+        r = [rw[x_rows(4 + a, half), :] for a in range(4)]
+        by_value, by_flux = open_response([scale[x_rows(4 + a, half), :] for a in range(4)], r)
+        r0, r8 = rw[x_rows(0, half), :], xd[pl.ds(48 + 8 * half, 8), :]
+        gain = (xu[pl.ds(96 + 8 * half, 8), :] + diagonal * r0) * has_x
+        mx[rows, :] = gain
+        for c in range(3):
+            plane = pl.ds(16 * c + 8 * half, 8)
+            grad = xu[pl.ds(48 + 16 * c + 8 * half, 8), :]
+            carried = xu[plane, :] + kappa * r0 * grad + gain * now[c, x_rows(0, half), :]
+            early[plane, :] = carried - term[plane, :]
+            base[c, x_rows(0, half), :] = base[c, x_rows(0, half), :] - scale[x_rows(0, half), :] * carried
+            value = xd[plane, :]
+            flux = r8 * (total([(D[4, a], now[c, x_rows(4 + a, half), :]) for a in range(4)]) + d44 * value)
+            for a in range(4):
+                at = x_rows(4 + a, half)
+                base[c, at, :] = base[c, at, :] - by_value[a] * value - by_flux[a] * flux
 
     r = [rw[y_rows(12 + a), :] for a in range(4)]
     by_value, by_flux = open_response([scale[y_rows(12 + a), :] for a in range(4)], r)
@@ -377,18 +419,15 @@
 
 
 def whole_kernel(
-    counts, base, now, rw, scale, early, yb, ya, mx, xd, zd, nodes_hbm, ids_hbm,
+    counts, base, now, rw, scale, early, yb, ya, mx, xd, zd, nodes, ids,
     out, kept, to_depth, xa2, xb2, zd2, my, y_low, y_high, r_high,
-    slip, yu, yd, xu2, xd2, zu2, nodes, ids, sems,
+    slip, yu, yd, xu2, xd2, zu2,
 ):
     middle = counts[0] // 2
     index = place()
     lane = lane_of()
     kappa, diagonal = np.float32(KAPPA), np.float32(KAPPA * D[4, 4])
     d44 = np.float32(D[4, 4])
-    copies = [pltpu.make_async_copy(nodes_hbm, nodes, sems.at[0]), pltpu.make_async_copy(ids_hbm, ids, sems.at[1])]
-    for copy in copies:
-        copy.start()
     unpaired(index[1], ya, yb, yu, yd)
     for c in range(3):
         for k in range(16):
@@ -449,18 +488,26 @@
     zu2[...] = interleaved(sent + [None], lane, 0)
     zd2[...] = first_lanes(lambda c, rows: out[c, rows, :], None, lane)
     paired(index[0], xu2, xd2, xa2, xb2)
-    for copy in copies:
-        copy.wait()
     tile = patch_tile(counts[2], slip[...], nodes[...], ids[...])
     for d in range(counts[2]):
-        to_depth[pl.ds(16 * d, 8), :] = jnp.where(d > index[2], zu2[...], zd2[...])
-        to_depth[pl.ds(16 * d + 8, 8), :] = jnp.broadcast_to(tile[d : d + 1, :], (8, NZL))
+        halo = jnp.where(d > index[2], zu2[...], zd2[...])
+        to_depth[pl.ds(8 * d, 8), :] = with_row(halo, tile[d : d + 1, :], lane)
+
+
+def with_row(halo, row, lane):
+    sub = lax.broadcasted_iota(jnp.int32, (8, NZL), 0)
+    row = jnp.broadcast_to(row, (8, NZL))
+    spread = jnp.where(sub == 0, rolled(row, 64), jnp.where(sub == 1, row, 0.0))
+    return jnp.where(lane < 64, halo, spread)
 
 
 def sum_kernel(counts, got, to_face):
-    row = got[pl.ds(8, 8), :]
+    summed = got[pl.ds(0, 8), :]
     for d in range(1, counts[2]):
-        row = row + got[pl.ds(16 * d + 8, 8), :]
+        summed = summed + got[pl.ds(8 * d, 8), :]
+    low = jnp.broadcast_to(rolled(summed, 64)[0:1, :], (8, NZL))
+    high = jnp.broadcast_to(summed[1:2, :], (8, NZL))
+    row = jnp.where(lane_of() < 64, low, high)
     for k in range(counts[0] * counts[1] // 8):
         to_face[pl.ds(8 * k, 8), :] = row
 
@@ -471,7 +518,7 @@
 ):
     index = place()
     unpaired(index[0], xa2, xb2, xu2, xd2)
-    beside(index[2], counts[2], got_z, 16, zu2, zd2)
+    beside(index[2], counts[2], got_z, zu2, zd2)
     closing_z = zu2[...] + mz[...] * zd2_own[...]
 
     def low_x(c, offset, plane, v0):
@@ -524,7 +571,7 @@
     specs = {} if in_specs is None else {"in_specs": in_specs}
     return pl.pallas_call(
         kernel,
-        out_shape=[jax.ShapeDtypeStruct(shape, F32) for shape in outs],
+        out_shape=[jax.ShapeDtypeStruct(o, F32) if isinstance(o, tuple) else jax.typeof(o) for o in outs],
         scratch_shapes=[pltpu.VMEM(shape, F32) if isinstance(shape, tuple) else shape for shape in scratch],
         compiler_params=pltpu.CompilerParams(vmem_limit_bytes=16 * 2**20),
         cost_estimate=pl.CostEstimate(flops=flops, bytes_accessed=moved, transcendentals=0),
@@ -551,27 +598,27 @@
     nodes, ids = fault_nodes.reshape(1, -1), patch_ids.reshape(1, -1)
     x_up, x_down, y_up, y_down = ((n, NZL) for n in (X_UP, X_DOWN, Y_UP, Y_DOWN))
     faces, strip = (48, NZL), (24, NZL)
-    xa, xb, za, zb, zd_own = call(
-        pack_kernel, "pack", [x_up, x_up, tile, tile, tile],
+    xa, xb, za, zb, zd_own, tails = call(
+        pack_kernel, "pack", [x_up, x_up, tile, tile, tile, (32, NZL)],
         [pltpu.VMEM(flat, F32), pltpu.VMEM(block, jnp.bfloat16), block, x_up, x_down, tile,
          pltpu.SemaphoreType.DMA((2,))],
         flops=2_000_000, moved=400_000, in_specs=[pl.BlockSpec(memory_space=pltpu.HBM)] * 2,
     )(now, rig)
     xa, xb = swap_near(xa, "normal"), swap_far(xb, "normal")
     zb, za = swap_far(zb, "depth"), swap_near(za, "depth")
-    base, yb, ya, early, mx, mz, xd, zd, rw, scale = call(
-        functools.partial(half_kernel, counts), "half",
-        [flat, y_up, y_up, faces, (16, NZL), tile, x_down, tile, block, block],
-        [flat, x_up, tile, y_up, y_down], flops=10_000_000, moved=900_000,
-    )(now, prev, rig, rho, xa, xb, za, zb, zd_own)
+    inner, term, rw, scale, nodes, ids = call(
+        inner_kernel, "inner", [flat, faces, block, block, nodes, ids], [flat], flops=10_000_000, moved=900_000,
+    )(now, prev, rig, rho, nodes, ids)
+    base, yb, ya, early, mx, mz, xd, zd = call(
+        functools.partial(edge_kernel, counts), "edge",
+        [flat, y_up, y_up, faces, (16, NZL), tile, x_down, tile],
+        [x_up, tile, y_up, y_down], flops=2_000_000, moved=900_000,
+    )(inner, now, rw, scale, term, tails, xa, xb, za, zb, zd_own)
     yb, ya = swap_far(yb, "strike"), swap_near(ya, "strike")
-    inside, outside = pl.BlockSpec(memory_space=pltpu.VMEM), pl.BlockSpec(memory_space=pltpu.HBM)
     mid, kept, to_depth, xa2, xb2, zd2, my, y_low, y_high, r_high = call(
         functools.partial(whole_kernel, counts), "whole",
-        [flat, flat, (16 * counts[2], NZL), faces, faces, tile, tile, strip, strip, tile],
-        [faces, y_up, y_down, faces, faces, tile, pltpu.VMEM(nodes.shape, jnp.int32), pltpu.VMEM(ids.shape, jnp.int32),
-         pltpu.SemaphoreType.DMA((2,))],
-        flops=2_000_000, moved=900_000, in_specs=[inside] * 10 + [outside] * 2,
+        [flat, flat, (8 * counts[2], NZL), faces, faces, tile, tile, strip, strip, tile],
+        [faces, y_up, y_down, faces, faces, tile], flops=2_000_000, moved=900_000,
     )(base, now, rw, scale, early, yb, ya, mx, xd, zd, nodes, ids)
     got_z = lax.all_to_all(to_depth, "depth", 0, 0, tiled=True)
     (to_face,) = call(

time: 78.9 us -> 77 us (0.976)
  waiting for transfers between devices: 11.8 us -> 7.76 us
  starting transfers between devices: 44.6 us -> 45.7 us
    ppermute x4, waiting for transfers between devices: 3 us -> 0.01 us  [swap_far(): lax.ppermute(value, axis, [(i, i + 1) for i in lower] + [(i + 1, i) for i...]
    ppermute x4, waiting for transfers between devices: 4.16 us -> 3.03 us  [swap_near(): lax.ppermute(value, axis, [(i, i ^ 1) for i in range(lax.axis_size(axis))])]
    ppermute x4, starting transfers between devices: 15.9 us -> 17 us  [swap_near(): lax.ppermute(value, axis, [(i, i ^ 1) for i in range(lax.axis_size(axis))])]
    unnamed x14 -> x16, local copies, waits for them, and re-layouts: 2.39 us -> 3.11 us
    pallas_call x3 -> x4, Pallas kernels: 4.59 us -> 4.19 us  [the longest x1 2.07 us: local(): call(inner_kernel, 'inner', [flat, faces, block, block, nodes, ids], [fla...]
  transfers between devices with their start and end apart: 9 -> 9, of which waited for: 4 -> 3; matrix products, arithmetic and copies ran while one was open for 0% -> 0% of each run, Pallas kernels for 4% -> 7%
where the time goes in v7:
time: 77 us; the launch traced here: 76.5 us
  starting transfers between devices  45.7 us (59%)
  blocking collectives  10.1 us (13%)
  Pallas kernels  8.98 us (12%)
  waiting for transfers between devices  7.76 us (10%)
  local copies, waits for them, and re-layouts  3.11 us (4%)
  between operations  0.81 us (1%)
    all_to_all x1, starting transfers between devices, local(): got_face = lax.all_to_all(to_face, ('normal', 'strike'), 0, 0, tiled=True)  24.8 us
    ppermute x4, starting transfers between devices, swap_near(): lax.ppermute(value, axis, [(i, i ^ 1) for i in range(lax.axis_size(axis))])  17 us
    all_to_all x1, blocking collectives, local(): got_z = lax.all_to_all(to_depth, 'depth', 0, 0, tiled=True)  10.1 us
    all_to_all x1, waiting for transfers between devices, local(): got_face = lax.all_to_all(to_face, ('normal', 'strike'), 0, 0, tiled=True)  4.73 us
    ppermute x4, starting transfers between devices, swap_far(): lax.ppermute(value, axis, [(i, i + 1) for i in lower] + [(i + 1, i) for i...  3.91 us
    pallas_call x1, Pallas kernels, local(): call(functools.partial(second_kernel, counts), 'second', [flat], [flat, f...  3.45 us
    unnamed x16, local copies, waits for them, and re-layouts  3.11 us
    ppermute x4, waiting for transfers between devices, swap_near(): lax.ppermute(value, axis, [(i, i ^ 1) for i in range(lax.axis_size(axis))])  3.03 us
  transfers between devices with their start and end apart: 9, of which 3 were waited for; matrix products, arithmetic and copies ran while one was open for 0% of the time, Pallas kernels for 7%

profile of v7, /device:TPU:1, one launch (start us, length us, event | category | flops | bytes accessed | tf_op | source)
XLA Modules:
  0.0 76.5 jit_solution(7598902477014405329)
XLA Ops:
  0.6 0.0 copy-start
  0.6 0.9 %copy-done = f32[3,8,16,128]{3,2,1,0:T(8,128)S(1)} copy-done((f32[3,8,16,128]{3,2,1,0:T(8,128)S(1)}, f32[3,8,16,128]{3,2,1,0:T(8,128)}, u32[]{:S(2)}) %copy-start) | copy-done | bytes 196632
  1.6 0.8 copy-done.3
  2.3 0.6 pack.1
  2.9 4.4 %collective-permute-start = (f32[112,128]{1,0:T(8,128)S(1)}, f32[112,128]{1,0:T(8,128)S(1)}, u32[]{:S(2)}, u32[]{:S(2)}) collective-permute-start(f32[112,128]{1,0:T(8,128)S(1)} %get-tuple-element.38), channel_id=1, source_target_pairs={{0,128},{128,0},{256,384},{384,256},{1,129},{129,1},{257,385},{385... | collective-permute-start | bytes 172040 | tf_op jit(solution)/shard_map/ppermute | solution.py:584
  7.3 0.7 collective-permute-start.1
  8.0 6.3 %collective-permute-start.2 = (f32[8,128]{1,0:T(8,128)S(1)}, f32[8,128]{1,0:T(8,128)S(1)}, u32[]{:S(2)}, u32[]{:S(2)}) collective-permute-start(f32[8,128]{1,0:T(8,128)S(1)} %get-tuple-element.40), channel_id=1, source_target_pairs={{0,1},{1,0},{2,3},{3,2},{4,5},{5,4},{6,7},{7,6},{8,9},{9,8},{10,11... | collective-permute-start | bytes 12296 | tf_op jit(solution)/shard_map/ppermute | solution.py:584
  14.3 1.9 %collective-permute-start.3 = (f32[8,128]{1,0:T(8,128)S(1)}, f32[8,128]{1,0:T(8,128)S(1)}, u32[]{:S(2)}, u32[]{:S(2)}) collective-permute-start(f32[8,128]{1,0:T(8,128)S(1)} %get-tuple-element.41), channel_id=1, source_target_pairs={{1,2},{3,4},{5,6},{2,1},{4,3},{6,5},{9,10},{11,12},{13,14},{10,9},... | collective-permute-start | bytes 12296 | tf_op jit(solution)/shard_map/ppermute | solution.py:589
  16.3 0.0 copy-start.7
  16.3 0.0 copy-start.6
  16.3 0.6 copy-done.7
  16.9 0.0 copy-done.6
  17.0 0.8 copy-done.5
  17.7 2.1 %inner.1 = (f32[3,128,128]{2,1,0:T(8,128)S(1)}, f32[48,128]{1,0:T(8,128)S(1)}, f32[128,128]{1,0:T(8,128)S(1)}, f32[128,128]{1,0:T(8,128)S(1)}, s32[1,256]{1,0:T(1,128)S(1)}, /*index=5*/s32[1,256]{1,0:T(1,128)S(1)}) custom-call(f32[3,128,128]{2,1,0:T(8,128)S(1)} %bitcast.15, f32[3,128,128]{2,1,0:T(8,128)S(1)} %bitcast.21, bf16[128,128]{1,0:T(8,128)(2,1)S(1)} %bitcast.23, ...), custom_call_target="tpu_custom_call" | custom-call | flops 10000000 | bytes 900000 | tf_op jit(solution)/shard_map/inner/pallas_call | solution.py:609
  19.8 0.0 collective-permute-done.2.za
  19.8 0.0 collective-permute-done.3.zb
  19.8 0.0 collective-permute-done.1.xb
  19.8 0.4 edge.1
  20.2 0.7 collective-permute-start.4
  20.9 3.4 %collective-permute-start.5 = (f32[136,128]{1,0:T(8,128)S(1)}, f32[136,128]{1,0:T(8,128)S(1)}, u32[]{:S(2)}, u32[]{:S(2)}) collective-permute-start(f32[136,128]{1,0:T(8,128)S(1)} %get-tuple-element.46), channel_id=1, source_target_pairs={{0,8},{8,0},{16,24},{24,16},{32,40},{40,32},{48,56},{56,48},{64,72... | collective-permute-start | bytes 208904 | tf_op jit(solution)/shard_map/ppermute | solution.py:584
  24.3 0.0 collective-permute-done.4.yb
  24.3 1.7 %collective-permute-done.5.ya = f32[136,128]{1,0:T(8,128)S(1)} collective-permute-done((f32[136,128]{1,0:T(8,128)S(1)}, f32[136,128]{1,0:T(8,128)S(1)}, u32[]{:S(2)}, u32[]{:S(2)}) %collective-permute-start.5) | collective-permute-done | bytes 69664 | tf_op jit(solution)/shard_map/ppermute | solution.py:584
  26.0 1.1 %whole.1 = (f32[3,128,128]{2,1,0:T(8,128)}, f32[3,128,128]{2,1,0:T(8,128)S(1)}, f32[64,128]{1,0:T(8,128)S(1)}, f32[48,128]{1,0:T(8,128)S(1)}, f32[48,128]{1,0:T(...) custom-call(f32[3,128,128]{2,1,0:T(8,128)S(1)} %get-tuple-element.43, ...), custom_call_target="tpu_custom_call" | custom-call | flops 2000000 | bytes 900000 | tf_op jit(solution)/shard_map/whole/pallas_call | solution.py:618
  27.1 10.1 %all_to_all.22 = f32[8,8,128]{2,1,0:T(8,128)S(1)} all-to-all(f32[8,8,128]{2,1,0:T(8,128)S(1)} %bitcast.26), channel_id=1, replica_groups=mesh['normal'=4,'strike'=16,'depth'=8] {'depth'}, dimensions={0} | all-to-all | bytes 65536 | tf_op jit(solution)/shard_map/all_to_all | solution.py:623
  37.2 0.7 add.1
  37.9 24.8 %all-to-all-start.1 = ((f32[64,1,128]{2,1,0:T(1,128)}), f32[64,1,128]{2,1,0:T(1,128)S(1)}, u32[]{:S(2)}, u32[]{:S(2)}) async-start(f32[64,1,128]{2,1,0:T(1,128)} %bitcast.11), calls=%async_computation.1 | async-start | bytes 65536 | tf_op jit(solution)/shard_map/all_to_all | solution.py:627
  62.7 2.9 %collective-permute-start.6 = (f32[48,128]{1,0:T(8,128)S(1)}, f32[48,128]{1,0:T(8,128)S(1)}, u32[]{:S(2)}, u32[]{:S(2)}) collective-permute-start(f32[48,128]{1,0:T(8,128)S(1)} %get-tuple-element.53), channel_id=1, source_target_pairs={{0,128},{128,0},{256,384},{384,256},{1,129},{129,1},{257,385},{385... | collective-permute-start | bytes 73736 | tf_op jit(solution)/shard_map/ppermute | solution.py:584
  65.6 0.7 collective-permute-start.7
  66.3 1.3 %collective-permute-done.6.xa2 = f32[48,128]{1,0:T(8,128)S(1)} collective-permute-done((f32[48,128]{1,0:T(8,128)S(1)}, f32[48,128]{1,0:T(8,128)S(1)}, u32[]{:S(2)}, u32[]{:S(2)}) %collective-permute-start.6) | collective-permute-done | bytes 24608 | tf_op jit(solution)/shard_map/ppermute | solution.py:584
  67.6 3.4 %second.1 = f32[3,128,128]{2,1,0:T(8,128)} custom-call(f32[3,128,128]{2,1,0:T(8,128)S(1)} %get-tuple-element.52.now, f32[3,128,128]{2,1,0:T(8,128)S(1)} %bitcast.18, f32[128,128]{1,0:T(8,128)S(1)} %get-tuple-element.34.rw, f32[128,128]{1,0:T(8,128)S(1)} %get-tuple-element.35.scale, f32[48,128]{1,0:T(8,128)S(1)} %collective-permute-done.6.xa2, ...), custom_call_target="tpu_custom_call" | custom-call | flops 10000000 | bytes 900000 | tf_op jit(solution)/shard_map/second/pallas_call | solution.py:630
  71.1 4.7 %all-to-all-done.1 = f32[64,1,128]{2,1,0:T(1,128)S(1)} async-done(((f32[64,1,128]{2,1,0:T(1,128)}), f32[64,1,128]{2,1,0:T(1,128)S(1)}, u32[]{:S(2)}, u32[]{:S(2)}) %all-to-all-start.1) | async-done | bytes 32800 | tf_op jit(solution)/shard_map/all_to_all | solution.py:627
  75.8 0.7 final.1
  (10 shorter events, 0.0 us)
Async XLA Ops:
  0.6 0.9 %copy-start = (f32[3,8,16,128]{3,2,1,0:T(8,128)S(1)}, f32[3,8,16,128]{3,2,1,0:T(8,128)}, u32[]{:S(2)}) copy-start(f32[3,8,16,128]{3,2,1,0:T(8,128)} %param.6) | copy-start | bytes 589828
  1.6 0.8 copy-start.3
  2.3 14.0 %copy-start.2 = (f32[3,8,16,128]{3,2,1,0:T(8,128)S(1)}, f32[3,8,16,128]{3,2,1,0:T(8,128)}, u32[]{:S(2)}) copy-start(f32[3,8,16,128]{3,2,1,0:T(8,128)} %param.7) | copy-start | bytes 589828
  2.3 14.0 %copy-start.4 = (bf16[8,16,128]{2,1,0:T(8,128)(2,1)S(1)}, bf16[8,16,128]{2,1,0:T(8,128)(2,1)}, u32[]{:S(2)}) copy-start(bf16[8,16,128]{2,1,0:T(8,128)(2,1)} %param.8) | copy-start | bytes 98308
  2.9 16.9 %collective-permute-start = (f32[112,128]{1,0:T(8,128)S(1)}, f32[112,128]{1,0:T(8,128)S(1)}, u32[]{:S(2)}, u32[]{:S(2)}) collective-permute-start(f32[112,128]{1,0:T(8,128)S(1)} %get-tuple-element.38), channel_id=1, source_target_pairs={{0,128},{128,0},{256,384},{384,256},{1,129},{129,1},{257,385},{385... | collective-permute-start | bytes 172040 | tf_op jit(solution)/shard_map/ppermute | solution.py:584
  7.3 12.5 %collective-permute-start.1 = (f32[112,128]{1,0:T(8,128)S(1)}, f32[112,128]{1,0:T(8,128)S(1)}, u32[]{:S(2)}, u32[]{:S(2)}) collective-permute-start(f32[112,128]{1,0:T(8,128)S(1)} %get-tuple-element.39), channel_id=1, source_target_pairs={{128,256},{256,128},{129,257},{257,129},{130,258},{258,130},{131,2... | collective-permute-start | bytes 172040 | tf_op jit(solution)/shard_map/ppermute | solution.py:589
  8.0 11.8 %collective-permute-start.2 = (f32[8,128]{1,0:T(8,128)S(1)}, f32[8,128]{1,0:T(8,128)S(1)}, u32[]{:S(2)}, u32[]{:S(2)}) collective-permute-start(f32[8,128]{1,0:T(8,128)S(1)} %get-tuple-element.40), channel_id=1, source_target_pairs={{0,1},{1,0},{2,3},{3,2},{4,5},{5,4},{6,7},{7,6},{8,9},{9,8},{10,11... | collective-permute-start | bytes 12296 | tf_op jit(solution)/shard_map/ppermute | solution.py:584
  14.3 5.5 %collective-permute-start.3 = (f32[8,128]{1,0:T(8,128)S(1)}, f32[8,128]{1,0:T(8,128)S(1)}, u32[]{:S(2)}, u32[]{:S(2)}) collective-permute-start(f32[8,128]{1,0:T(8,128)S(1)} %get-tuple-element.41), channel_id=1, source_target_pairs={{1,2},{3,4},{5,6},{2,1},{4,3},{6,5},{9,10},{11,12},{13,14},{10,9},... | collective-permute-start | bytes 12296 | tf_op jit(solution)/shard_map/ppermute | solution.py:589
  16.3 0.7 copy-start.7
  16.3 0.7 copy-start.6
  17.0 0.8 copy-start.5
  20.2 4.1 %collective-permute-start.4 = (f32[136,128]{1,0:T(8,128)S(1)}, f32[136,128]{1,0:T(8,128)S(1)}, u32[]{:S(2)}, u32[]{:S(2)}) collective-permute-start(f32[136,128]{1,0:T(8,128)S(1)} %get-tuple-element.45), channel_id=1, source_target_pairs={{8,16},{24,32},{40,48},{56,64},{72,80},{88,96},{104,112},{16,8},{3... | collective-permute-start | bytes 208904 | tf_op jit(solution)/shard_map/ppermute | solution.py:589
  20.9 5.1 %collective-permute-start.5 = (f32[136,128]{1,0:T(8,128)S(1)}, f32[136,128]{1,0:T(8,128)S(1)}, u32[]{:S(2)}, u32[]{:S(2)}) collective-permute-start(f32[136,128]{1,0:T(8,128)S(1)} %get-tuple-element.46), channel_id=1, source_target_pairs={{0,8},{8,0},{16,24},{24,16},{32,40},{40,32},{48,56},{56,48},{64,72... | collective-permute-start | bytes 208904 | tf_op jit(solution)/shard_map/ppermute | solution.py:584
  27.1 40.5 %copy-start.1 = (f32[3,8,16,128]{3,2,1,0:T(8,128)S(1)}, f32[3,8,16,128]{3,2,1,0:T(8,128)}, u32[]{:S(2)}) copy-start(f32[3,8,16,128]{3,2,1,0:T(8,128)} %param.6) | copy-start | bytes 589828
  37.9 38.0 %all-to-all-start.1 = ((f32[64,1,128]{2,1,0:T(1,128)}), f32[64,1,128]{2,1,0:T(1,128)S(1)}, u32[]{:S(2)}, u32[]{:S(2)}) async-start(f32[64,1,128]{2,1,0:T(1,128)} %bitcast.11), calls=%async_computation.1 | async-start | bytes 65536 | tf_op jit(solution)/shard_map/all_to_all | solution.py:627
  62.7 5.0 %collective-permute-start.6 = (f32[48,128]{1,0:T(8,128)S(1)}, f32[48,128]{1,0:T(8,128)S(1)}, u32[]{:S(2)}, u32[]{:S(2)}) collective-permute-start(f32[48,128]{1,0:T(8,128)S(1)} %get-tuple-element.53), channel_id=1, source_target_pairs={{0,128},{128,0},{256,384},{384,256},{1,129},{129,1},{257,385},{385... | collective-permute-start | bytes 73736 | tf_op jit(solution)/shard_map/ppermute | solution.py:584
  65.6 2.0 %collective-permute-start.7 = (f32[48,128]{1,0:T(8,128)S(1)}, f32[48,128]{1,0:T(8,128)S(1)}, u32[]{:S(2)}, u32[]{:S(2)}) collective-permute-start(f32[48,128]{1,0:T(8,128)S(1)} %get-tuple-element.54), channel_id=1, source_target_pairs={{128,256},{256,128},{129,257},{257,129},{130,258},{258,130},{131,2... | collective-permute-start | bytes 73736 | tf_op jit(solution)/shard_map/ppermute | solution.py:589

commit v8 on v7

--- a/solution.py
+++ b/solution.py
@@ -172,11 +172,18 @@
     high[...] = jnp.where(index < count - 1, got[pl.ds(above, high.shape[0]), :], 0.0)
 
 
-def pack_kernel(now_hbm, rig_hbm, xa, xb, za, zb, zd, tails, now, rig, rw, xu, xd, zu, sems):
-    copies = [pltpu.make_async_copy(rig_hbm, rig, sems.at[0]), pltpu.make_async_copy(now_hbm, now, sems.at[1])]
+def pack_kernel(
+    now_hbm, prev_hbm, rig_hbm, rho_hbm, nodes_hbm, ids_hbm,
+    xa, xb, za, zb, zd, tails, rw, now, prev, rho, nodes, ids,
+    rig, xu, xd, zu, sems,
+):
+    pairs = (
+        (rig_hbm, rig), (now_hbm, now), (prev_hbm, prev), (rho_hbm, rho), (nodes_hbm, nodes), (ids_hbm, ids),
+    )
+    copies = [pltpu.make_async_copy(src, dst, sems.at[i]) for i, (src, dst) in enumerate(pairs)]
     for copy in copies:
         copy.start()
-    for copy in copies:
+    for copy in copies[:2]:
         copy.wait()
     widen(rig, rw)
     lane = lane_of()
@@ -205,6 +212,8 @@
     index = place()
     paired(index[0], xu, xd, xa, xb)
     paired(index[2], zu, zd, za, zb)
+    for copy in copies[2:]:
+        copy.wait()
 
 
 def advance(now, prev, rw, low, high_v, high_r, scale, ghost_z, ghost_rz, closing_z, index, store, acc, on_first):
@@ -311,10 +320,7 @@
     return jnp.where((pos == 0) & is_first, np.float32(W0), out)
 
 
-def inner_kernel(now, prev, rig, rho, nodes_in, ids_in, base, term, rw, scale, nodes, ids, acc):
-    nodes[...] = nodes_in[...]
-    ids[...] = ids_in[...]
-    widen(rig, rw)
+def inner_kernel(now, prev, rw, rho, base, term, scale, acc):
     step_scale(rho, scale)
 
     def store(c, x, rows, plane, after):
@@ -598,17 +604,17 @@
     nodes, ids = fault_nodes.reshape(1, -1), patch_ids.reshape(1, -1)
     x_up, x_down, y_up, y_down = ((n, NZL) for n in (X_UP, X_DOWN, Y_UP, Y_DOWN))
     faces, strip = (48, NZL), (24, NZL)
-    xa, xb, za, zb, zd_own, tails = call(
-        pack_kernel, "pack", [x_up, x_up, tile, tile, tile, (32, NZL)],
-        [pltpu.VMEM(flat, F32), pltpu.VMEM(block, jnp.bfloat16), block, x_up, x_down, tile,
-         pltpu.SemaphoreType.DMA((2,))],
-        flops=2_000_000, moved=400_000, in_specs=[pl.BlockSpec(memory_space=pltpu.HBM)] * 2,
-    )(now, rig)
+    xa, xb, za, zb, zd_own, tails, rw, now, prev, rho, nodes, ids = call(
+        pack_kernel, "pack",
+        [x_up, x_up, tile, tile, tile, (32, NZL), block, flat, flat, rho, nodes, ids],
+        [pltpu.VMEM(block, jnp.bfloat16), x_up, x_down, tile, pltpu.SemaphoreType.DMA((6,))],
+        flops=2_000_000, moved=900_000, in_specs=[pl.BlockSpec(memory_space=pltpu.HBM)] * 6,
+    )(*(pltpu.with_memory_space_constraint(x, pltpu.HBM) for x in (now, prev, rig, rho, nodes, ids)))
     xa, xb = swap_near(xa, "normal"), swap_far(xb, "normal")
     zb, za = swap_far(zb, "depth"), swap_near(za, "depth")
-    inner, term, rw, scale, nodes, ids = call(
-        inner_kernel, "inner", [flat, faces, block, block, nodes, ids], [flat], flops=10_000_000, moved=900_000,
-    )(now, prev, rig, rho, nodes, ids)
+    inner, term, scale = call(
+        inner_kernel, "inner", [flat, faces, block], [flat], flops=10_000_000, moved=900_000,
+    )(now, prev, rw, rho)
     base, yb, ya, early, mx, mz, xd, zd = call(
         functools.partial(edge_kernel, counts), "edge",
         [flat, y_up, y_up, faces, (16, NZL), tile, x_down, tile],

time: 77 us -> 74.4 us (0.966)
  local copies, waits for them, and re-layouts: 3.11 us -> 0 us
  waiting for transfers between devices: 7.76 us -> 9.55 us
  blocking collectives: 10.1 us -> 9.15 us
  starting transfers between devices: 45.7 us -> 44.9 us
    unnamed x16 -> x0, local copies, waits for them, and re-layouts: 3.11 us -> none
    all_to_all x1, blocking collectives: 10.1 us -> 9.15 us  [local(): got_z = lax.all_to_all(to_depth, 'depth', 0, 0, tiled=True)]
    ppermute x4, waiting for transfers between devices: 0.01 us -> 0.92 us  [swap_far(): lax.ppermute(value, axis, [(i, i + 1) for i in lower] + [(i + 1, i) for i...]
    ppermute x4, starting transfers between devices: 17 us -> 16.1 us  [swap_near(): lax.ppermute(value, axis, [(i, i ^ 1) for i in range(lax.axis_size(axis))])]
    ppermute x4, waiting for transfers between devices: 3.03 us -> 3.9 us  [swap_near(): lax.ppermute(value, axis, [(i, i ^ 1) for i in range(lax.axis_size(axis))])]
  transfers between devices with their start and end apart: 9 -> 9, of which waited for: 3 -> 4; matrix products, arithmetic and copies ran while one was open for 0% -> 0% of each run, Pallas kernels for 7% -> 7%
where the time goes in v8:
time: 74.4 us; the launch traced here: 74 us
  starting transfers between devices  44.9 us (60%)
  Pallas kernels  9.7 us (13%)
  waiting for transfers between devices  9.55 us (13%)
  blocking collectives  9.15 us (12%)
    all_to_all x1, starting transfers between devices, local(): got_face = lax.all_to_all(to_face, ('normal', 'strike'), 0, 0, tiled=True)  24.8 us
    ppermute x4, starting transfers between devices, swap_near(): lax.ppermute(value, axis, [(i, i ^ 1) for i in range(lax.axis_size(axis))])  16.1 us
    all_to_all x1, blocking collectives, local(): got_z = lax.all_to_all(to_depth, 'depth', 0, 0, tiled=True)  9.15 us
    all_to_all x1, waiting for transfers between devices, local(): got_face = lax.all_to_all(to_face, ('normal', 'strike'), 0, 0, tiled=True)  4.73 us
    ppermute x4, starting transfers between devices, swap_far(): lax.ppermute(value, axis, [(i, i + 1) for i in lower] + [(i + 1, i) for i...  3.91 us
    ppermute x4, waiting for transfers between devices, swap_near(): lax.ppermute(value, axis, [(i, i ^ 1) for i in range(lax.axis_size(axis))])  3.9 us
    pallas_call x1, Pallas kernels, local(): call(functools.partial(second_kernel, counts), 'second', [flat], [flat, f...  3.45 us
    pallas_call x1, Pallas kernels, local(): call(inner_kernel, 'inner', [flat, faces, block], [flat], flops=10000000,...  2.07 us
  transfers between devices with their start and end apart: 9, of which 4 were waited for; matrix products, arithmetic and copies ran while one was open for 0% of the time, Pallas kernels for 7%

profile of v8, /device:TPU:1, one launch (start us, length us, event | category | flops | bytes accessed | tf_op | source)
XLA Modules:
  0.0 74.0 jit_solution(9120660665076298249)
XLA Ops:
  0.6 1.3 %pack.1 = (f32[112,128]{1,0:T(8,128)S(1)}, f32[112,128]{1,0:T(8,128)S(1)}, f32[8,128]{1,0:T(8,128)S(1)}, f32[8,128]{1,0:T(8,128)S(1)}, f32[8,128]{1,0:T(8,128)S(...) custom-call(f32[3,128,128]{2,1,0:T(8,128)} %bitcast.18, ...), custom_call_target="tpu_custom_call" | custom-call | flops 2000000 | bytes 900000 | tf_op jit(solution)/shard_map/pack/pallas_call | solution.py:607
  2.0 4.4 %collective-permute-start = (f32[112,128]{1,0:T(8,128)S(1)}, f32[112,128]{1,0:T(8,128)S(1)}, u32[]{:S(2)}, u32[]{:S(2)}) collective-permute-start(f32[112,128]{1,0:T(8,128)S(1)} %get-tuple-element.44), channel_id=1, source_target_pairs={{0,128},{128,0},{256,384},{384,256},{1,129},{129,1},{257,385},{385... | collective-permute-start | bytes 172040 | tf_op jit(solution)/shard_map/ppermute | solution.py:590
  6.3 0.7 collective-permute-start.1
  7.0 6.3 %collective-permute-start.2 = (f32[8,128]{1,0:T(8,128)S(1)}, f32[8,128]{1,0:T(8,128)S(1)}, u32[]{:S(2)}, u32[]{:S(2)}) collective-permute-start(f32[8,128]{1,0:T(8,128)S(1)} %get-tuple-element.46), channel_id=1, source_target_pairs={{0,1},{1,0},{2,3},{3,2},{4,5},{5,4},{6,7},{7,6},{8,9},{9,8},{10,11... | collective-permute-start | bytes 12296 | tf_op jit(solution)/shard_map/ppermute | solution.py:590
  13.4 1.9 %collective-permute-start.3 = (f32[8,128]{1,0:T(8,128)S(1)}, f32[8,128]{1,0:T(8,128)S(1)}, u32[]{:S(2)}, u32[]{:S(2)}) collective-permute-start(f32[8,128]{1,0:T(8,128)S(1)} %get-tuple-element.47), channel_id=1, source_target_pairs={{1,2},{3,4},{5,6},{2,1},{4,3},{6,5},{9,10},{11,12},{13,14},{10,9},... | collective-permute-start | bytes 12296 | tf_op jit(solution)/shard_map/ppermute | solution.py:595
  15.3 2.1 %inner.1 = (f32[3,128,128]{2,1,0:T(8,128)S(1)}, f32[48,128]{1,0:T(8,128)S(1)}, f32[128,128]{1,0:T(8,128)S(1)}) custom-call(f32[3,128,128]{2,1,0:T(8,128)S(1)} %get-tuple-element.36.now.prev, f32[3,128,128]{2,1,0:T(8,128)S(1)} %get-tuple-element.37.prev, f32[128,128]{1,0:T(8,128)S(1)} %get-tuple-element.38.rw, bf16[128,128]{1,0:T(8,128)(2,1)S(1)} %get-tuple-element.39.rho), custom_call_target="tpu_custom_call" | custom-call | flops 10000000 | bytes 900000 | tf_op jit(solution)/shard_map/inner/pallas_call | solution.py:615
  17.4 0.0 collective-permute-done.2.za
  17.4 0.9 %collective-permute-done.3.zb = f32[8,128]{1,0:T(8,128)S(1)} collective-permute-done((f32[8,128]{1,0:T(8,128)S(1)}, f32[8,128]{1,0:T(8,128)S(1)}, u32[]{:S(2)}, u32[]{:S(2)}) %collective-permute-start.3) | collective-permute-done | bytes 4128 | tf_op jit(solution)/shard_map/ppermute | solution.py:595
  18.3 0.0 collective-permute-done.xa
  18.3 0.0 collective-permute-done.1.xb
  18.3 0.4 edge.1
  18.7 0.7 collective-permute-start.4
  19.3 2.5 %collective-permute-start.5 = (f32[136,128]{1,0:T(8,128)S(1)}, f32[136,128]{1,0:T(8,128)S(1)}, u32[]{:S(2)}, u32[]{:S(2)}) collective-permute-start(f32[136,128]{1,0:T(8,128)S(1)} %get-tuple-element.52), channel_id=1, source_target_pairs={{0,8},{8,0},{16,24},{24,16},{32,40},{40,32},{48,56},{56,48},{64,72... | collective-permute-start | bytes 208904 | tf_op jit(solution)/shard_map/ppermute | solution.py:590
  21.9 0.0 collective-permute-done.4.yb
  21.9 2.5 %collective-permute-done.5.ya = f32[136,128]{1,0:T(8,128)S(1)} collective-permute-done((f32[136,128]{1,0:T(8,128)S(1)}, f32[136,128]{1,0:T(8,128)S(1)}, u32[]{:S(2)}, u32[]{:S(2)}) %collective-permute-start.5) | collective-permute-done | bytes 69664 | tf_op jit(solution)/shard_map/ppermute | solution.py:590
  24.4 1.1 %whole.1 = (f32[3,128,128]{2,1,0:T(8,128)}, f32[3,128,128]{2,1,0:T(8,128)S(1)}, f32[64,128]{1,0:T(8,128)S(1)}, f32[48,128]{1,0:T(8,128)S(1)}, f32[48,128]{1,0:T(...) custom-call(f32[3,128,128]{2,1,0:T(8,128)S(1)} %get-tuple-element.49, ...), custom_call_target="tpu_custom_call" | custom-call | flops 2000000 | bytes 900000 | tf_op jit(solution)/shard_map/whole/pallas_call | solution.py:624
  25.5 9.1 %all_to_all.22 = f32[8,8,128]{2,1,0:T(8,128)S(1)} all-to-all(f32[8,8,128]{2,1,0:T(8,128)S(1)} %bitcast.17), channel_id=1, replica_groups=mesh['normal'=4,'strike'=16,'depth'=8] {'depth'}, dimensions={0} | all-to-all | bytes 65536 | tf_op jit(solution)/shard_map/all_to_all | solution.py:629
  34.7 0.7 add.1
  35.4 24.8 %all-to-all-start.1 = ((f32[64,1,128]{2,1,0:T(1,128)}), f32[64,1,128]{2,1,0:T(1,128)S(1)}, u32[]{:S(2)}, u32[]{:S(2)}) async-start(f32[64,1,128]{2,1,0:T(1,128)} %bitcast.11), calls=%async_computation.1 | async-start | bytes 65536 | tf_op jit(solution)/shard_map/all_to_all | solution.py:633
  60.2 2.9 %collective-permute-start.6 = (f32[48,128]{1,0:T(8,128)S(1)}, f32[48,128]{1,0:T(8,128)S(1)}, u32[]{:S(2)}, u32[]{:S(2)}) collective-permute-start(f32[48,128]{1,0:T(8,128)S(1)} %get-tuple-element.59), channel_id=1, source_target_pairs={{0,128},{128,0},{256,384},{384,256},{1,129},{129,1},{257,385},{385... | collective-permute-start | bytes 73736 | tf_op jit(solution)/shard_map/ppermute | solution.py:590
  63.1 0.7 collective-permute-start.7
  63.8 1.3 %collective-permute-done.6.xa2 = f32[48,128]{1,0:T(8,128)S(1)} collective-permute-done((f32[48,128]{1,0:T(8,128)S(1)}, f32[48,128]{1,0:T(8,128)S(1)}, u32[]{:S(2)}, u32[]{:S(2)}) %collective-permute-start.6) | collective-permute-done | bytes 24608 | tf_op jit(solution)/shard_map/ppermute | solution.py:590
  65.2 0.0 collective-permute-done.7.xb2
  65.2 3.4 %second.1 = f32[3,128,128]{2,1,0:T(8,128)} custom-call(f32[3,128,128]{2,1,0:T(8,128)S(1)} %get-tuple-element.58.now, f32[3,128,128]{2,1,0:T(8,128)S(1)} %get-tuple-element.36.now.prev, f32[128,128]{1,0:T(8,128)S(1)} %get-tuple-element.38.rw, f32[128,128]{1,0:T(8,128)S(1)} %get-tuple-element.41.scale, f32[48,128]{1,0:T(8,128)S(1)} %collective-permute-done.6.xa2, ...), custom_call_target="tpu_custom_call" | custom-call | flops 10000000 | bytes 900000 | tf_op jit(solution)/shard_map/second/pallas_call | solution.py:636
  68.6 4.7 %all-to-all-done.1 = f32[64,1,128]{2,1,0:T(1,128)S(1)} async-done(((f32[64,1,128]{2,1,0:T(1,128)}), f32[64,1,128]{2,1,0:T(1,128)S(1)}, u32[]{:S(2)}, u32[]{:S(2)}) %all-to-all-start.1) | async-done | bytes 32800 | tf_op jit(solution)/shard_map/all_to_all | solution.py:633
  73.3 0.7 final.1
Async XLA Ops:
  2.0 16.3 %collective-permute-start = (f32[112,128]{1,0:T(8,128)S(1)}, f32[112,128]{1,0:T(8,128)S(1)}, u32[]{:S(2)}, u32[]{:S(2)}) collective-permute-start(f32[112,128]{1,0:T(8,128)S(1)} %get-tuple-element.44), channel_id=1, source_target_pairs={{0,128},{128,0},{256,384},{384,256},{1,129},{129,1},{257,385},{385... | collective-permute-start | bytes 172040 | tf_op jit(solution)/shard_map/ppermute | solution.py:590
  6.3 11.9 %collective-permute-start.1 = (f32[112,128]{1,0:T(8,128)S(1)}, f32[112,128]{1,0:T(8,128)S(1)}, u32[]{:S(2)}, u32[]{:S(2)}) collective-permute-start(f32[112,128]{1,0:T(8,128)S(1)} %get-tuple-element.45), channel_id=1, source_target_pairs={{128,256},{256,128},{129,257},{257,129},{130,258},{258,130},{131,2... | collective-permute-start | bytes 172040 | tf_op jit(solution)/shard_map/ppermute | solution.py:595
  7.0 10.4 %collective-permute-start.2 = (f32[8,128]{1,0:T(8,128)S(1)}, f32[8,128]{1,0:T(8,128)S(1)}, u32[]{:S(2)}, u32[]{:S(2)}) collective-permute-start(f32[8,128]{1,0:T(8,128)S(1)} %get-tuple-element.46), channel_id=1, source_target_pairs={{0,1},{1,0},{2,3},{3,2},{4,5},{5,4},{6,7},{7,6},{8,9},{9,8},{10,11... | collective-permute-start | bytes 12296 | tf_op jit(solution)/shard_map/ppermute | solution.py:590
  13.4 4.9 %collective-permute-start.3 = (f32[8,128]{1,0:T(8,128)S(1)}, f32[8,128]{1,0:T(8,128)S(1)}, u32[]{:S(2)}, u32[]{:S(2)}) collective-permute-start(f32[8,128]{1,0:T(8,128)S(1)} %get-tuple-element.47), channel_id=1, source_target_pairs={{1,2},{3,4},{5,6},{2,1},{4,3},{6,5},{9,10},{11,12},{13,14},{10,9},... | collective-permute-start | bytes 12296 | tf_op jit(solution)/shard_map/ppermute | solution.py:595
  18.7 3.2 %collective-permute-start.4 = (f32[136,128]{1,0:T(8,128)S(1)}, f32[136,128]{1,0:T(8,128)S(1)}, u32[]{:S(2)}, u32[]{:S(2)}) collective-permute-start(f32[136,128]{1,0:T(8,128)S(1)} %get-tuple-element.51), channel_id=1, source_target_pairs={{8,16},{24,32},{40,48},{56,64},{72,80},{88,96},{104,112},{16,8},{3... | collective-permute-start | bytes 208904 | tf_op jit(solution)/shard_map/ppermute | solution.py:595
  19.3 5.1 %collective-permute-start.5 = (f32[136,128]{1,0:T(8,128)S(1)}, f32[136,128]{1,0:T(8,128)S(1)}, u32[]{:S(2)}, u32[]{:S(2)}) collective-permute-start(f32[136,128]{1,0:T(8,128)S(1)} %get-tuple-element.52), channel_id=1, source_target_pairs={{0,8},{8,0},{16,24},{24,16},{32,40},{40,32},{48,56},{56,48},{64,72... | collective-permute-start | bytes 208904 | tf_op jit(solution)/shard_map/ppermute | solution.py:590
  35.4 38.0 %all-to-all-start.1 = ((f32[64,1,128]{2,1,0:T(1,128)}), f32[64,1,128]{2,1,0:T(1,128)S(1)}, u32[]{:S(2)}, u32[]{:S(2)}) async-start(f32[64,1,128]{2,1,0:T(1,128)} %bitcast.11), calls=%async_computation.1 | async-start | bytes 65536 | tf_op jit(solution)/shard_map/all_to_all | solution.py:633
  60.2 5.0 %collective-permute-start.6 = (f32[48,128]{1,0:T(8,128)S(1)}, f32[48,128]{1,0:T(8,128)S(1)}, u32[]{:S(2)}, u32[]{:S(2)}) collective-permute-start(f32[48,128]{1,0:T(8,128)S(1)} %get-tuple-element.59), channel_id=1, source_target_pairs={{0,128},{128,0},{256,384},{384,256},{1,129},{129,1},{257,385},{385... | collective-permute-start | bytes 73736 | tf_op jit(solution)/shard_map/ppermute | solution.py:590
  63.1 2.0 %collective-permute-start.7 = (f32[48,128]{1,0:T(8,128)S(1)}, f32[48,128]{1,0:T(8,128)S(1)}, u32[]{:S(2)}, u32[]{:S(2)}) collective-permute-start(f32[48,128]{1,0:T(8,128)S(1)} %get-tuple-element.60), channel_id=1, source_target_pairs={{128,256},{256,128},{129,257},{257,129},{130,258},{258,130},{131,2... | collective-permute-start | bytes 73736 | tf_op jit(solution)/shard_map/ppermute | solution.py:595

commit v9 on v8

--- a/solution.py
+++ b/solution.py
@@ -170,6 +170,44 @@
     above = pl.multiple_of((jnp.minimum(index + 1, count - 1)) * 8, 8)
     low[...] = jnp.where(index > 0, got[pl.ds(below, low.shape[0]), :], 0.0)
     high[...] = jnp.where(index < count - 1, got[pl.ds(above, high.shape[0]), :], 0.0)
+
+
+Y_SPLIT, Y_PAIRS = (0, 1, 2, 3, 4, 5, 12), ((6, 7), (8, 9), (10, 11), (13, 14), (15, 16))
+Y_TILES = len(Y_SPLIT) + len(Y_PAIRS)
+
+
+def plane_of(ref, n):
+    return ref[pl.ds(8 * n, 8), :]
+
+
+def in_parts(value):
+    return jnp.concatenate([value, value - value.astype(jnp.bfloat16).astype(F32)], axis=0)
+
+
+def y_pack(index, up, down, near, far):
+    even = (index & 1) == 0
+    ups = [in_parts(plane_of(up, n)) for n in Y_SPLIT]
+    ups += [jnp.concatenate([plane_of(up, a), plane_of(up, b)], axis=0) for a, b in Y_PAIRS]
+    for t, above in enumerate(ups):
+        below = in_parts(plane_of(down, t)) if t < Y_DOWN // 8 else above
+        rows = pl.ds(16 * t, 16)
+        near[rows, :] = jnp.where(even, above, below).astype(jnp.bfloat16)
+        far[rows, :] = jnp.where(even, below, above).astype(jnp.bfloat16)
+
+
+def y_unpack(index, near, far, low, high):
+    even = (index & 1) == 0
+    for t in range(Y_TILES):
+        rows = pl.ds(16 * t, 16)
+        from_near, from_far = near[rows, :].astype(F32), far[rows, :].astype(F32)
+        below, above = jnp.where(even, from_far, from_near), jnp.where(even, from_near, from_far)
+        if t < Y_DOWN // 8:
+            high[pl.ds(8 * t, 8), :] = above[:8, :] + above[8:, :]
+        if t < len(Y_SPLIT):
+            low[pl.ds(8 * Y_SPLIT[t], 8), :] = below[:8, :] + below[8:, :]
+        else:
+            for part, n in enumerate(Y_PAIRS[t - len(Y_SPLIT)]):
+                low[pl.ds(8 * n, 8), :] = below[8 * part : 8 * part + 8, :]
 
 
 def pack_kernel(
@@ -415,7 +453,7 @@
         yd[pl.ds(24 + 8 * c, 8), :] = base[c, y_rows(0), :]
     yd[pl.ds(48, 8), :] = rw[y_rows(0), :]
     yd[pl.ds(56, 8), :] = scale[y_rows(0), :]
-    paired(index[1], yu, yd, ya, yb)
+    y_pack(index[1], yu, yd, ya, yb)
 
 
 def open_response(scale, r):
@@ -434,7 +472,7 @@
     lane = lane_of()
     kappa, diagonal = np.float32(KAPPA), np.float32(KAPPA * D[4, 4])
     d44 = np.float32(D[4, 4])
-    unpaired(index[1], ya, yb, yu, yd)
+    y_unpack(index[1], ya, yb, yu, yd)
     for c in range(3):
         for k in range(16):
             rows = pl.ds(8 * k, 8)
@@ -577,7 +615,7 @@
     specs = {} if in_specs is None else {"in_specs": in_specs}
     return pl.pallas_call(
         kernel,
-        out_shape=[jax.ShapeDtypeStruct(o, F32) if isinstance(o, tuple) else jax.typeof(o) for o in outs],
+        out_shape=[jax.ShapeDtypeStruct(o, F32) if isinstance(o, tuple) else jax.ShapeDtypeStruct(o.shape, o.dtype) for o in outs],
         scratch_shapes=[pltpu.VMEM(shape, F32) if isinstance(shape, tuple) else shape for shape in scratch],
         compiler_params=pltpu.CompilerParams(vmem_limit_bytes=16 * 2**20),
         cost_estimate=pl.CostEstimate(flops=flops, bytes_accessed=moved, transcendentals=0),
@@ -604,6 +642,7 @@
     nodes, ids = fault_nodes.reshape(1, -1), patch_ids.reshape(1, -1)
     x_up, x_down, y_up, y_down = ((n, NZL) for n in (X_UP, X_DOWN, Y_UP, Y_DOWN))
     faces, strip = (48, NZL), (24, NZL)
+    y_sent = jax.ShapeDtypeStruct((16 * Y_TILES, NZL), jnp.bfloat16)
     xa, xb, za, zb, zd_own, tails, rw, now, prev, rho, nodes, ids = call(
         pack_kernel, "pack",
         [x_up, x_up, tile, tile, tile, (32, NZL), block, flat, flat, rho, nodes, ids],
@@ -617,7 +656,7 @@
     )(now, prev, rw, rho)
     base, yb, ya, early, mx, mz, xd, zd = call(
         functools.partial(edge_kernel, counts), "edge",
-        [flat, y_up, y_up, faces, (16, NZL), tile, x_down, tile],
+        [flat, y_sent, y_sent, faces, (16, NZL), tile, x_down, tile],
         [x_up, tile, y_up, y_down], flops=2_000_000, moved=900_000,
     )(inner, now, rw, scale, term, tails, xa, xb, za, zb, zd_own)
     yb, ya = swap_far(yb, "strike"), swap_near(ya, "strike")

time: 74.4 us -> 72.3 us (0.972)
  starting transfers between devices: 44.9 us -> 43.2 us
    all_to_all x1, starting transfers between devices: 24.8 us -> 23.2 us  [local(): got_face = lax.all_to_all(to_face, ('normal', 'strike'), 0, 0, tiled=True)]
  transfers between devices with their start and end apart: 9 -> 9, of which waited for: 4 -> 4; matrix products, arithmetic and copies ran while one was open for 0% -> 0% of each run, Pallas kernels for 7% -> 8%
where the time goes in v9:
time: 72.3 us; the launch traced here: 71.9 us
  starting transfers between devices  43.2 us (60%)
  Pallas kernels  9.69 us (13%)
  waiting for transfers between devices  9.32 us (13%)
  blocking collectives  8.93 us (12%)
  between operations  0.75 us (1%)
    all_to_all x1, starting transfers between devices, local(): got_face = lax.all_to_all(to_face, ('normal', 'strike'), 0, 0, tiled=True)  23.2 us
    ppermute x4, starting transfers between devices, swap_near(): lax.ppermute(value, axis, [(i, i ^ 1) for i in range(lax.axis_size(axis))])  16.1 us
    all_to_all x1, blocking collectives, local(): got_z = lax.all_to_all(to_depth, 'depth', 0, 0, tiled=True)  8.93 us
    all_to_all x1, waiting for transfers between devices, local(): got_face = lax.all_to_all(to_face, ('normal', 'strike'), 0, 0, tiled=True)  4.73 us
    ppermute x4, starting transfers between devices, swap_far(): lax.ppermute(value, axis, [(i, i + 1) for i in lower] + [(i + 1, i) for i...  3.91 us
    ppermute x4, waiting for transfers between devices, swap_near(): lax.ppermute(value, axis, [(i, i ^ 1) for i in range(lax.axis_size(axis))])  3.68 us
    pallas_call x1, Pallas kernels, local(): call(functools.partial(second_kernel, counts), 'second', [flat], [flat, f...  3.45 us
    pallas_call x1, Pallas kernels, local(): call(inner_kernel, 'inner', [flat, faces, block], [flat], flops=10000000,...  2.07 us
  transfers between devices with their start and end apart: 9, of which 4 were waited for; matrix products, arithmetic and copies ran while one was open for 0% of the time, Pallas kernels for 8%

profile of v9, /device:TPU:1, one launch (start us, length us, event | category | flops | bytes accessed | tf_op | source)
XLA Modules:
  0.0 71.9 jit_solution(14074602578351163196)
XLA Ops:
  0.6 1.3 %pack.1 = (f32[112,128]{1,0:T(8,128)S(1)}, f32[112,128]{1,0:T(8,128)S(1)}, f32[8,128]{1,0:T(8,128)S(1)}, f32[8,128]{1,0:T(8,128)S(1)}, f32[8,128]{1,0:T(8,128)S(...) custom-call(f32[3,128,128]{2,1,0:T(8,128)} %bitcast.18, ...), custom_call_target="tpu_custom_call" | custom-call | flops 2000000 | bytes 900000 | tf_op jit(solution)/shard_map/pack/pallas_call | solution.py:646
  2.0 4.4 %collective-permute-start = (f32[112,128]{1,0:T(8,128)S(1)}, f32[112,128]{1,0:T(8,128)S(1)}, u32[]{:S(2)}, u32[]{:S(2)}) collective-permute-start(f32[112,128]{1,0:T(8,128)S(1)} %get-tuple-element.44), channel_id=1, source_target_pairs={{0,128},{128,0},{256,384},{384,256},{1,129},{129,1},{257,385},{385... | collective-permute-start | bytes 172040 | tf_op jit(solution)/shard_map/ppermute | solution.py:628
  6.3 0.7 collective-permute-start.1
  7.0 6.3 %collective-permute-start.2 = (f32[8,128]{1,0:T(8,128)S(1)}, f32[8,128]{1,0:T(8,128)S(1)}, u32[]{:S(2)}, u32[]{:S(2)}) collective-permute-start(f32[8,128]{1,0:T(8,128)S(1)} %get-tuple-element.46), channel_id=1, source_target_pairs={{0,1},{1,0},{2,3},{3,2},{4,5},{5,4},{6,7},{7,6},{8,9},{9,8},{10,11... | collective-permute-start | bytes 12296 | tf_op jit(solution)/shard_map/ppermute | solution.py:628
  13.4 1.9 %collective-permute-start.3 = (f32[8,128]{1,0:T(8,128)S(1)}, f32[8,128]{1,0:T(8,128)S(1)}, u32[]{:S(2)}, u32[]{:S(2)}) collective-permute-start(f32[8,128]{1,0:T(8,128)S(1)} %get-tuple-element.47), channel_id=1, source_target_pairs={{1,2},{3,4},{5,6},{2,1},{4,3},{6,5},{9,10},{11,12},{13,14},{10,9},... | collective-permute-start | bytes 12296 | tf_op jit(solution)/shard_map/ppermute | solution.py:633
  15.3 2.1 %inner.1 = (f32[3,128,128]{2,1,0:T(8,128)S(1)}, f32[48,128]{1,0:T(8,128)S(1)}, f32[128,128]{1,0:T(8,128)S(1)}) custom-call(f32[3,128,128]{2,1,0:T(8,128)S(1)} %get-tuple-element.36.now.prev, f32[3,128,128]{2,1,0:T(8,128)S(1)} %get-tuple-element.37.prev, f32[128,128]{1,0:T(8,128)S(1)} %get-tuple-element.38.rw, bf16[128,128]{1,0:T(8,128)(2,1)S(1)} %get-tuple-element.39.rho), custom_call_target="tpu_custom_call" | custom-call | flops 10000000 | bytes 900000 | tf_op jit(solution)/shard_map/inner/pallas_call | solution.py:654
  17.4 0.0 collective-permute-done.2.za
  17.4 0.9 %collective-permute-done.3.zb = f32[8,128]{1,0:T(8,128)S(1)} collective-permute-done((f32[8,128]{1,0:T(8,128)S(1)}, f32[8,128]{1,0:T(8,128)S(1)}, u32[]{:S(2)}, u32[]{:S(2)}) %collective-permute-start.3) | collective-permute-done | bytes 4128 | tf_op jit(solution)/shard_map/ppermute | solution.py:633
  18.3 0.0 collective-permute-done.xa
  18.3 0.0 collective-permute-done.1.xb
  18.3 0.4 edge.1
  18.7 0.7 collective-permute-start.4
  19.4 2.5 %collective-permute-start.5 = (bf16[192,128]{1,0:T(8,128)(2,1)S(1)}, bf16[192,128]{1,0:T(8,128)(2,1)S(1)}, u32[]{:S(2)}, u32[]{:S(2)}) collective-permute-start(bf16[192,128]{1,0:T(8,128)(2,1)S(1)} %get-tuple-element.52), channel_id=1, source_target_pairs={{0,8},{8,0},{16,24},{24,16},{32,40},{40,32},{48,56},{56,48},{64,72... | collective-permute-start | bytes 147464 | tf_op jit(solution)/shard_map/ppermute | solution.py:628
  21.9 0.0 collective-permute-done.4.yb
  21.9 2.3 %collective-permute-done.5.ya = bf16[192,128]{1,0:T(8,128)(2,1)S(1)} collective-permute-done((bf16[192,128]{1,0:T(8,128)(2,1)S(1)}, bf16[192,128]{1,0:T(8,128)(2,1)S(1)}, u32[]{:S(2)}, u32[]{:S(2)}) %collective-permute-start.5) | collective-permute-done | bytes 49184 | tf_op jit(solution)/shard_map/ppermute | solution.py:628
  24.2 1.1 %whole.1 = (f32[3,128,128]{2,1,0:T(8,128)}, f32[3,128,128]{2,1,0:T(8,128)S(1)}, f32[64,128]{1,0:T(8,128)S(1)}, f32[48,128]{1,0:T(8,128)S(1)}, f32[48,128]{1,0:T(...) custom-call(f32[3,128,128]{2,1,0:T(8,128)S(1)} %get-tuple-element.49, ...), custom_call_target="tpu_custom_call" | custom-call | flops 2000000 | bytes 900000 | tf_op jit(solution)/shard_map/whole/pallas_call | solution.py:663
  25.3 8.9 %all_to_all.22 = f32[8,8,128]{2,1,0:T(8,128)S(1)} all-to-all(f32[8,8,128]{2,1,0:T(8,128)S(1)} %bitcast.17), channel_id=1, replica_groups=mesh['normal'=4,'strike'=16,'depth'=8] {'depth'}, dimensions={0} | all-to-all | bytes 65536 | tf_op jit(solution)/shard_map/all_to_all | solution.py:668
  34.2 0.7 add.1
  34.9 23.2 %all-to-all-start.1 = ((f32[64,1,128]{2,1,0:T(1,128)}), f32[64,1,128]{2,1,0:T(1,128)S(1)}, u32[]{:S(2)}, u32[]{:S(2)}) async-start(f32[64,1,128]{2,1,0:T(1,128)} %bitcast.11), calls=%async_computation.1 | async-start | bytes 65536 | tf_op jit(solution)/shard_map/all_to_all | solution.py:672
  58.1 2.9 %collective-permute-start.6 = (f32[48,128]{1,0:T(8,128)S(1)}, f32[48,128]{1,0:T(8,128)S(1)}, u32[]{:S(2)}, u32[]{:S(2)}) collective-permute-start(f32[48,128]{1,0:T(8,128)S(1)} %get-tuple-element.59), channel_id=1, source_target_pairs={{0,128},{128,0},{256,384},{384,256},{1,129},{129,1},{257,385},{385... | collective-permute-start | bytes 73736 | tf_op jit(solution)/shard_map/ppermute | solution.py:628
  61.1 0.7 collective-permute-start.7
  61.8 1.3 %collective-permute-done.6.xa2 = f32[48,128]{1,0:T(8,128)S(1)} collective-permute-done((f32[48,128]{1,0:T(8,128)S(1)}, f32[48,128]{1,0:T(8,128)S(1)}, u32[]{:S(2)}, u32[]{:S(2)}) %collective-permute-start.6) | collective-permute-done | bytes 24608 | tf_op jit(solution)/shard_map/ppermute | solution.py:628
  63.1 0.0 collective-permute-done.7.xb2
  63.1 3.4 %second.1 = f32[3,128,128]{2,1,0:T(8,128)} custom-call(f32[3,128,128]{2,1,0:T(8,128)S(1)} %get-tuple-element.58.now, f32[3,128,128]{2,1,0:T(8,128)S(1)} %get-tuple-element.36.now.prev, f32[128,128]{1,0:T(8,128)S(1)} %get-tuple-element.38.rw, f32[128,128]{1,0:T(8,128)S(1)} %get-tuple-element.41.scale, f32[48,128]{1,0:T(8,128)S(1)} %collective-permute-done.6.xa2, ...), custom_call_target="tpu_custom_call" | custom-call | flops 10000000 | bytes 900000 | tf_op jit(solution)/shard_map/second/pallas_call | solution.py:675
  66.6 4.7 %all-to-all-done.1 = f32[64,1,128]{2,1,0:T(1,128)S(1)} async-done(((f32[64,1,128]{2,1,0:T(1,128)}), f32[64,1,128]{2,1,0:T(1,128)S(1)}, u32[]{:S(2)}, u32[]{:S(2)}) %all-to-all-start.1) | async-done | bytes 32800 | tf_op jit(solution)/shard_map/all_to_all | solution.py:672
  71.3 0.7 final.1
Async XLA Ops:
  2.0 16.3 %collective-permute-start = (f32[112,128]{1,0:T(8,128)S(1)}, f32[112,128]{1,0:T(8,128)S(1)}, u32[]{:S(2)}, u32[]{:S(2)}) collective-permute-start(f32[112,128]{1,0:T(8,128)S(1)} %get-tuple-element.44), channel_id=1, source_target_pairs={{0,128},{128,0},{256,384},{384,256},{1,129},{129,1},{257,385},{385... | collective-permute-start | bytes 172040 | tf_op jit(solution)/shard_map/ppermute | solution.py:628
  6.3 11.9 %collective-permute-start.1 = (f32[112,128]{1,0:T(8,128)S(1)}, f32[112,128]{1,0:T(8,128)S(1)}, u32[]{:S(2)}, u32[]{:S(2)}) collective-permute-start(f32[112,128]{1,0:T(8,128)S(1)} %get-tuple-element.45), channel_id=1, source_target_pairs={{128,256},{256,128},{129,257},{257,129},{130,258},{258,130},{131,2... | collective-permute-start | bytes 172040 | tf_op jit(solution)/shard_map/ppermute | solution.py:633
  7.0 10.4 %collective-permute-start.2 = (f32[8,128]{1,0:T(8,128)S(1)}, f32[8,128]{1,0:T(8,128)S(1)}, u32[]{:S(2)}, u32[]{:S(2)}) collective-permute-start(f32[8,128]{1,0:T(8,128)S(1)} %get-tuple-element.46), channel_id=1, source_target_pairs={{0,1},{1,0},{2,3},{3,2},{4,5},{5,4},{6,7},{7,6},{8,9},{9,8},{10,11... | collective-permute-start | bytes 12296 | tf_op jit(solution)/shard_map/ppermute | solution.py:628
  13.4 4.9 %collective-permute-start.3 = (f32[8,128]{1,0:T(8,128)S(1)}, f32[8,128]{1,0:T(8,128)S(1)}, u32[]{:S(2)}, u32[]{:S(2)}) collective-permute-start(f32[8,128]{1,0:T(8,128)S(1)} %get-tuple-element.47), channel_id=1, source_target_pairs={{1,2},{3,4},{5,6},{2,1},{4,3},{6,5},{9,10},{11,12},{13,14},{10,9},... | collective-permute-start | bytes 12296 | tf_op jit(solution)/shard_map/ppermute | solution.py:633
  18.7 3.2 %collective-permute-start.4 = (bf16[192,128]{1,0:T(8,128)(2,1)S(1)}, bf16[192,128]{1,0:T(8,128)(2,1)S(1)}, u32[]{:S(2)}, u32[]{:S(2)}) collective-permute-start(bf16[192,128]{1,0:T(8,128)(2,1)S(1)} %get-tuple-element.51), channel_id=1, source_target_pairs={{8,16},{24,32},{40,48},{56,64},{72,80},{88,96},{104,112},{16,8},{3... | collective-permute-start | bytes 147464 | tf_op jit(solution)/shard_map/ppermute | solution.py:633
  19.4 4.8 %collective-permute-start.5 = (bf16[192,128]{1,0:T(8,128)(2,1)S(1)}, bf16[192,128]{1,0:T(8,128)(2,1)S(1)}, u32[]{:S(2)}, u32[]{:S(2)}) collective-permute-start(bf16[192,128]{1,0:T(8,128)(2,1)S(1)} %get-tuple-element.52), channel_id=1, source_target_pairs={{0,8},{8,0},{16,24},{24,16},{32,40},{40,32},{48,56},{56,48},{64,72... | collective-permute-start | bytes 147464 | tf_op jit(solution)/shard_map/ppermute | solution.py:628
  34.9 36.4 %all-to-all-start.1 = ((f32[64,1,128]{2,1,0:T(1,128)}), f32[64,1,128]{2,1,0:T(1,128)S(1)}, u32[]{:S(2)}, u32[]{:S(2)}) async-start(f32[64,1,128]{2,1,0:T(1,128)} %bitcast.11), calls=%async_computation.1 | async-start | bytes 65536 | tf_op jit(solution)/shard_map/all_to_all | solution.py:672
  58.1 5.0 %collective-permute-start.6 = (f32[48,128]{1,0:T(8,128)S(1)}, f32[48,128]{1,0:T(8,128)S(1)}, u32[]{:S(2)}, u32[]{:S(2)}) collective-permute-start(f32[48,128]{1,0:T(8,128)S(1)} %get-tuple-element.59), channel_id=1, source_target_pairs={{0,128},{128,0},{256,384},{384,256},{1,129},{129,1},{257,385},{385... | collective-permute-start | bytes 73736 | tf_op jit(solution)/shard_map/ppermute | solution.py:628
  61.1 2.0 %collective-permute-start.7 = (f32[48,128]{1,0:T(8,128)S(1)}, f32[48,128]{1,0:T(8,128)S(1)}, u32[]{:S(2)}, u32[]{:S(2)}) collective-permute-start(f32[48,128]{1,0:T(8,128)S(1)} %get-tuple-element.60), channel_id=1, source_target_pairs={{128,256},{256,128},{129,257},{257,129},{130,258},{258,130},{131,2... | collective-permute-start | bytes 73736 | tf_op jit(solution)/shard_map/ppermute | solution.py:633

commit v10 on v9

--- a/solution.py
+++ b/solution.py
@@ -254,7 +254,7 @@
         copy.wait()
 
 
-def advance(now, prev, rw, low, high_v, high_r, scale, ghost_z, ghost_rz, closing_z, index, store, acc, on_first):
+def advance(now, prev, rw, low, high_v, high_r, scale, ghost_z, ghost_rz, closing_z, index, store, acc, on_first, on_end=None):
     index_x, index_y, index_z = index
     at_x = jnp.where(index_x == 0, 2.0, 1.0).astype(F32)
     at_y = jnp.where(index_y == 0, 2.0, 1.0).astype(F32)
@@ -339,6 +339,8 @@
                 after = (v[x] + v[x]) - prev[c, rows[x], :] - scale[rows[x], :] * force
                 store(c, x, rows[x], plane, after)
             carried = terms[4]
+        if on_end is not None:
+            on_end(c, half)
         return carry
 
     lax.fori_loop(0, 6, along_xz, 0)
@@ -464,7 +466,7 @@
 
 def whole_kernel(
     counts, base, now, rw, scale, early, yb, ya, mx, xd, zd, nodes, ids,
-    out, kept, to_depth, xa2, xb2, zd2, my, y_low, y_high, r_high,
+    out, to_depth, xa2, xb2, zd2, my, y_low, y_high, r_high,
     slip, yu, yd, xu2, xd2, zu2,
 ):
     middle = counts[0] // 2
@@ -476,9 +478,7 @@
     for c in range(3):
         for k in range(16):
             rows = pl.ds(8 * k, 8)
-            values = base[c, rows, :]
-            out[c, rows, :] = values
-            kept[c, rows, :] = values
+            out[c, rows, :] = base[c, rows, :]
     r = [rw[y_rows(12 + a), :] for a in range(4)]
     by_value, by_flux = open_response([scale[y_rows(12 + a), :] for a in range(4)], r)
     own_scale = open_scale(r)
@@ -494,7 +494,6 @@
         v0 = now[c, y_rows(0), :]
         after = base[c, y_rows(0), :] - s0 * (part + kappa * r0 * grad + gain * v0)
         out[c, y_rows(0), :] = after
-        kept[c, y_rows(0), :] = after
         flux = r0 * (grad + d44 * v0)
         y_low[plane, :] = (part2 - value_part * v0 - flux_part * flux) + kappa * r0 * (
             grad2 - value_grad * v0 - flux_grad * flux
@@ -506,7 +505,6 @@
         for a in range(4):
             after = base[c, y_rows(12 + a), :] - by_value[a] * above - by_flux[a] * flux
             out[c, y_rows(12 + a), :] = after
-            kept[c, y_rows(12 + a), :] = after
 
     on_one, on_two = index[0] == middle - 1, index[0] == middle
     for half in range(2):
@@ -558,9 +556,12 @@
 
 def second_kernel(
     counts, now, prev, rw, scale, xa2, xb2, got_z, zd2_own, mx, my, mz, xd, zd, y_low, y_high, r_high,
-    out, acc, xu2, xd2, zu2, zd2,
+    out_hbm, mid_hbm, out, acc, xu2, xd2, zu2, zd2, sems,
 ):
     index = place()
+    copies = [pltpu.make_async_copy(out.at[c], out_hbm.at[c], sems.at[c]) for c in range(3)]
+    copies.append(pltpu.make_async_copy(now, mid_hbm, sems.at[3]))
+    copies[3].start()
     unpaired(index[0], xa2, xb2, xu2, xd2)
     beside(index[2], counts[2], got_z, zu2, zd2)
     closing_z = zu2[...] + mz[...] * zd2_own[...]
@@ -574,10 +575,17 @@
     def store(c, x, rows, plane, after):
         out[c, rows, :] = after
 
+    def sent(c, half):
+        @pl.when(half == 1)
+        def _():
+            pltpu.make_async_copy(out.at[c], out_hbm.at[c], sems.at[c]).start()
+
     advance(
         now, prev, rw, (low_x, low_y), (xd2, y_high), (xd.at[pl.ds(48, 16)], r_high), scale,
-        zd2[...], rolled(zd[...], -3), closing_z, index, store, acc, lambda *args: None,
+        zd2[...], rolled(zd[...], -3), closing_z, index, store, acc, lambda *args: None, sent,
     )
+    for copy in copies:
+        copy.wait()
 
 
 def patch_tile(count_d, slip, node, patch):
@@ -611,8 +619,7 @@
         out[:, pl.ds(c, 1)] = jnp.sum(jnp.where(hit, summed, 0.0), axis=1, keepdims=True)
 
 
-def call(kernel, name, outs, scratch=(), flops=0, moved=0, in_specs=None):
-    specs = {} if in_specs is None else {"in_specs": in_specs}
+def call(kernel, name, outs, scratch=(), flops=0, moved=0, **specs):
     return pl.pallas_call(
         kernel,
         out_shape=[jax.ShapeDtypeStruct(o, F32) if isinstance(o, tuple) else jax.ShapeDtypeStruct(o.shape, o.dtype) for o in outs],
@@ -660,9 +667,9 @@
         [x_up, tile, y_up, y_down], flops=2_000_000, moved=900_000,
     )(inner, now, rw, scale, term, tails, xa, xb, za, zb, zd_own)
     yb, ya = swap_far(yb, "strike"), swap_near(ya, "strike")
-    mid, kept, to_depth, xa2, xb2, zd2, my, y_low, y_high, r_high = call(
+    kept, to_depth, xa2, xb2, zd2, my, y_low, y_high, r_high = call(
         functools.partial(whole_kernel, counts), "whole",
-        [flat, flat, (8 * counts[2], NZL), faces, faces, tile, tile, strip, strip, tile],
+        [flat, (8 * counts[2], NZL), faces, faces, tile, tile, strip, strip, tile],
         [faces, y_up, y_down, faces, faces, tile], flops=2_000_000, moved=900_000,
     )(base, now, rw, scale, early, yb, ya, mx, xd, zd, nodes, ids)
     got_z = lax.all_to_all(to_depth, "depth", 0, 0, tiled=True)
@@ -672,9 +679,10 @@
     got_face = lax.all_to_all(to_face, ("normal", "strike"), 0, 0, tiled=True)
     xa2, xb2 = swap_near(xa2, "normal"), swap_far(xb2, "normal")
     (share,) = call(final_kernel, "final", [(2, 3)], flops=10_000, moved=10_000)(got_face)
-    (following,) = call(
-        functools.partial(second_kernel, counts), "second", [flat], [flat, faces, faces, tile, tile],
-        flops=10_000_000, moved=900_000,
+    following, mid = call(
+        functools.partial(second_kernel, counts), "second", [flat, flat],
+        [flat, flat, faces, faces, tile, tile, pltpu.SemaphoreType.DMA((4,))],
+        flops=10_000_000, moved=900_000, out_specs=[pl.BlockSpec(memory_space=pltpu.HBM)] * 2,
     )(kept, now, rw, scale, xa2, xb2, got_z, zd2, mx, my, mz, xd, zd, y_low, y_high, r_high)
     return following.reshape(field_now.shape), mid.reshape(field_now.shape), share
 

time: 72.3 us -> 72 us (level)
  no operation moved by 1% of the time
where the time goes in v10:
time: 72 us; the launch traced here: 71.6 us
  starting transfers between devices  43.2 us (60%)
  waiting for transfers between devices  9.32 us (13%)
  Pallas kernels  9.27 us (13%)
  blocking collectives  8.98 us (12%)
  between operations  0.75 us (1%)
    all_to_all x1, starting transfers between devices, local(): got_face = lax.all_to_all(to_face, ('normal', 'strike'), 0, 0, tiled=True)  23.2 us
    ppermute x4, starting transfers between devices, swap_near(): lax.ppermute(value, axis, [(i, i ^ 1) for i in range(lax.axis_size(axis))])  16.1 us
    all_to_all x1, blocking collectives, local(): got_z = lax.all_to_all(to_depth, 'depth', 0, 0, tiled=True)  8.98 us
    all_to_all x1, waiting for transfers between devices, local(): got_face = lax.all_to_all(to_face, ('normal', 'strike'), 0, 0, tiled=True)  4.72 us
    ppermute x4, starting transfers between devices, swap_far(): lax.ppermute(value, axis, [(i, i + 1) for i in lower] + [(i + 1, i) for i...  3.91 us
    ppermute x4, waiting for transfers between devices, swap_near(): lax.ppermute(value, axis, [(i, i ^ 1) for i in range(lax.axis_size(axis))])  3.69 us
    pallas_call x1, Pallas kernels, local(): call(functools.partial(second_kernel, counts), 'second', [flat, flat], [f...  3.44 us
    pallas_call x1, Pallas kernels, local(): call(inner_kernel, 'inner', [flat, faces, block], [flat], flops=10000000,...  2.07 us
  transfers between devices with their start and end apart: 9, of which 4 were waited for; matrix products, arithmetic and copies ran while one was open for 0% of the time, Pallas kernels for 8%

profile of v10, /device:TPU:1, one launch (start us, length us, event | category | flops | bytes accessed | tf_op | source)
XLA Modules:
  0.0 71.6 jit_solution(6558964747480730341)
XLA Ops:
  0.6 1.3 %pack.1 = (f32[112,128]{1,0:T(8,128)S(1)}, f32[112,128]{1,0:T(8,128)S(1)}, f32[8,128]{1,0:T(8,128)S(1)}, f32[8,128]{1,0:T(8,128)S(1)}, f32[8,128]{1,0:T(8,128)S(...) custom-call(f32[3,128,128]{2,1,0:T(8,128)} %bitcast.18, ...), custom_call_target="tpu_custom_call" | custom-call | flops 2000000 | bytes 900000 | tf_op jit(solution)/shard_map/pack/pallas_call | solution.py:653
  2.0 4.4 %collective-permute-start = (f32[112,128]{1,0:T(8,128)S(1)}, f32[112,128]{1,0:T(8,128)S(1)}, u32[]{:S(2)}, u32[]{:S(2)}) collective-permute-start(f32[112,128]{1,0:T(8,128)S(1)} %get-tuple-element.45), channel_id=1, source_target_pairs={{0,128},{128,0},{256,384},{384,256},{1,129},{129,1},{257,385},{385... | collective-permute-start | bytes 172040 | tf_op jit(solution)/shard_map/ppermute | solution.py:635
  6.3 0.7 collective-permute-start.1
  7.0 6.3 %collective-permute-start.2 = (f32[8,128]{1,0:T(8,128)S(1)}, f32[8,128]{1,0:T(8,128)S(1)}, u32[]{:S(2)}, u32[]{:S(2)}) collective-permute-start(f32[8,128]{1,0:T(8,128)S(1)} %get-tuple-element.47), channel_id=1, source_target_pairs={{0,1},{1,0},{2,3},{3,2},{4,5},{5,4},{6,7},{7,6},{8,9},{9,8},{10,11... | collective-permute-start | bytes 12296 | tf_op jit(solution)/shard_map/ppermute | solution.py:635
  13.4 1.9 %collective-permute-start.3 = (f32[8,128]{1,0:T(8,128)S(1)}, f32[8,128]{1,0:T(8,128)S(1)}, u32[]{:S(2)}, u32[]{:S(2)}) collective-permute-start(f32[8,128]{1,0:T(8,128)S(1)} %get-tuple-element.48), channel_id=1, source_target_pairs={{1,2},{3,4},{5,6},{2,1},{4,3},{6,5},{9,10},{11,12},{13,14},{10,9},... | collective-permute-start | bytes 12296 | tf_op jit(solution)/shard_map/ppermute | solution.py:640
  15.3 2.1 %inner.1 = (f32[3,128,128]{2,1,0:T(8,128)S(1)}, f32[48,128]{1,0:T(8,128)S(1)}, f32[128,128]{1,0:T(8,128)S(1)}) custom-call(f32[3,128,128]{2,1,0:T(8,128)S(1)} %get-tuple-element.37.now.prev, f32[3,128,128]{2,1,0:T(8,128)S(1)} %get-tuple-element.38.prev, f32[128,128]{1,0:T(8,128)S(1)} %get-tuple-element.39.rw, bf16[128,128]{1,0:T(8,128)(2,1)S(1)} %get-tuple-element.40.rho), custom_call_target="tpu_custom_call" | custom-call | flops 10000000 | bytes 900000 | tf_op jit(solution)/shard_map/inner/pallas_call | solution.py:661
  17.4 0.0 collective-permute-done.2.za
  17.4 0.9 %collective-permute-done.3.zb = f32[8,128]{1,0:T(8,128)S(1)} collective-permute-done((f32[8,128]{1,0:T(8,128)S(1)}, f32[8,128]{1,0:T(8,128)S(1)}, u32[]{:S(2)}, u32[]{:S(2)}) %collective-permute-start.3) | collective-permute-done | bytes 4128 | tf_op jit(solution)/shard_map/ppermute | solution.py:640
  18.3 0.0 collective-permute-done.xa
  18.3 0.0 collective-permute-done.1.xb
  18.3 0.4 edge.1
  18.7 0.7 collective-permute-start.4
  19.4 2.5 %collective-permute-start.5 = (bf16[192,128]{1,0:T(8,128)(2,1)S(1)}, bf16[192,128]{1,0:T(8,128)(2,1)S(1)}, u32[]{:S(2)}, u32[]{:S(2)}) collective-permute-start(bf16[192,128]{1,0:T(8,128)(2,1)S(1)} %get-tuple-element.53), channel_id=1, source_target_pairs={{0,8},{8,0},{16,24},{24,16},{32,40},{40,32},{48,56},{56,48},{64,72... | collective-permute-start | bytes 147464 | tf_op jit(solution)/shard_map/ppermute | solution.py:635
  21.9 0.0 collective-permute-done.4.yb
  21.9 2.3 %collective-permute-done.5.ya = bf16[192,128]{1,0:T(8,128)(2,1)S(1)} collective-permute-done((bf16[192,128]{1,0:T(8,128)(2,1)S(1)}, bf16[192,128]{1,0:T(8,128)(2,1)S(1)}, u32[]{:S(2)}, u32[]{:S(2)}) %collective-permute-start.5) | collective-permute-done | bytes 49184 | tf_op jit(solution)/shard_map/ppermute | solution.py:635
  24.2 0.7 whole.1
  24.9 9.0 %all_to_all.22 = f32[8,8,128]{2,1,0:T(8,128)S(1)} all-to-all(f32[8,8,128]{2,1,0:T(8,128)S(1)} %bitcast.17), channel_id=1, replica_groups=mesh['normal'=4,'strike'=16,'depth'=8] {'depth'}, dimensions={0} | all-to-all | bytes 65536 | tf_op jit(solution)/shard_map/all_to_all | solution.py:675
  33.9 0.7 add.1
  34.6 23.2 %all-to-all-start.1 = ((f32[64,1,128]{2,1,0:T(1,128)}), f32[64,1,128]{2,1,0:T(1,128)S(1)}, u32[]{:S(2)}, u32[]{:S(2)}) async-start(f32[64,1,128]{2,1,0:T(1,128)} %bitcast.11), calls=%async_computation.1 | async-start | bytes 65536 | tf_op jit(solution)/shard_map/all_to_all | solution.py:679
  57.8 2.9 %collective-permute-start.6 = (f32[48,128]{1,0:T(8,128)S(1)}, f32[48,128]{1,0:T(8,128)S(1)}, u32[]{:S(2)}, u32[]{:S(2)}) collective-permute-start(f32[48,128]{1,0:T(8,128)S(1)} %get-tuple-element.60), channel_id=1, source_target_pairs={{0,128},{128,0},{256,384},{384,256},{1,129},{129,1},{257,385},{385... | collective-permute-start | bytes 73736 | tf_op jit(solution)/shard_map/ppermute | solution.py:635
  60.7 0.7 collective-permute-start.7
  61.4 1.4 %collective-permute-done.6.xa2 = f32[48,128]{1,0:T(8,128)S(1)} collective-permute-done((f32[48,128]{1,0:T(8,128)S(1)}, f32[48,128]{1,0:T(8,128)S(1)}, u32[]{:S(2)}, u32[]{:S(2)}) %collective-permute-start.6) | collective-permute-done | bytes 24608 | tf_op jit(solution)/shard_map/ppermute | solution.py:635
  62.7 0.0 collective-permute-done.7.xb2
  62.8 3.4 %second.1 = (f32[3,128,128]{2,1,0:T(8,128)}, f32[3,128,128]{2,1,0:T(8,128)}) custom-call(f32[3,128,128]{2,1,0:T(8,128)S(1)} %get-tuple-element.59.now, f32[3,128,128]{2,1,0:T(8,128)S(1)} %get-tuple-element.37.now.prev, f32[128,128]{1,0:T(8,128)S(1)} %get-tuple-element.39.rw, f32[128,128]{1,0:T(8,128)S(1)} %get-tuple-element.42.scale, ...), custom_call_target="tpu_custom_call" | custom-call | flops 10000000 | bytes 900000 | tf_op jit(solution)/shard_map/second/pallas_call | solution.py:682
  66.2 4.7 %all-to-all-done.1 = f32[64,1,128]{2,1,0:T(1,128)S(1)} async-done(((f32[64,1,128]{2,1,0:T(1,128)}), f32[64,1,128]{2,1,0:T(1,128)S(1)}, u32[]{:S(2)}, u32[]{:S(2)}) %all-to-all-start.1) | async-done | bytes 32800 | tf_op jit(solution)/shard_map/all_to_all | solution.py:679
  70.9 0.7 final.1
Async XLA Ops:
  2.0 16.3 %collective-permute-start = (f32[112,128]{1,0:T(8,128)S(1)}, f32[112,128]{1,0:T(8,128)S(1)}, u32[]{:S(2)}, u32[]{:S(2)}) collective-permute-start(f32[112,128]{1,0:T(8,128)S(1)} %get-tuple-element.45), channel_id=1, source_target_pairs={{0,128},{128,0},{256,384},{384,256},{1,129},{129,1},{257,385},{385... | collective-permute-start | bytes 172040 | tf_op jit(solution)/shard_map/ppermute | solution.py:635
  6.3 11.9 %collective-permute-start.1 = (f32[112,128]{1,0:T(8,128)S(1)}, f32[112,128]{1,0:T(8,128)S(1)}, u32[]{:S(2)}, u32[]{:S(2)}) collective-permute-start(f32[112,128]{1,0:T(8,128)S(1)} %get-tuple-element.46), channel_id=1, source_target_pairs={{128,256},{256,128},{129,257},{257,129},{130,258},{258,130},{131,2... | collective-permute-start | bytes 172040 | tf_op jit(solution)/shard_map/ppermute | solution.py:640
  7.0 10.4 %collective-permute-start.2 = (f32[8,128]{1,0:T(8,128)S(1)}, f32[8,128]{1,0:T(8,128)S(1)}, u32[]{:S(2)}, u32[]{:S(2)}) collective-permute-start(f32[8,128]{1,0:T(8,128)S(1)} %get-tuple-element.47), channel_id=1, source_target_pairs={{0,1},{1,0},{2,3},{3,2},{4,5},{5,4},{6,7},{7,6},{8,9},{9,8},{10,11... | collective-permute-start | bytes 12296 | tf_op jit(solution)/shard_map/ppermute | solution.py:635
  13.4 4.9 %collective-permute-start.3 = (f32[8,128]{1,0:T(8,128)S(1)}, f32[8,128]{1,0:T(8,128)S(1)}, u32[]{:S(2)}, u32[]{:S(2)}) collective-permute-start(f32[8,128]{1,0:T(8,128)S(1)} %get-tuple-element.48), channel_id=1, source_target_pairs={{1,2},{3,4},{5,6},{2,1},{4,3},{6,5},{9,10},{11,12},{13,14},{10,9},... | collective-permute-start | bytes 12296 | tf_op jit(solution)/shard_map/ppermute | solution.py:640
  18.7 3.2 %collective-permute-start.4 = (bf16[192,128]{1,0:T(8,128)(2,1)S(1)}, bf16[192,128]{1,0:T(8,128)(2,1)S(1)}, u32[]{:S(2)}, u32[]{:S(2)}) collective-permute-start(bf16[192,128]{1,0:T(8,128)(2,1)S(1)} %get-tuple-element.52), channel_id=1, source_target_pairs={{8,16},{24,32},{40,48},{56,64},{72,80},{88,96},{104,112},{16,8},{3... | collective-permute-start | bytes 147464 | tf_op jit(solution)/shard_map/ppermute | solution.py:640
  19.4 4.8 %collective-permute-start.5 = (bf16[192,128]{1,0:T(8,128)(2,1)S(1)}, bf16[192,128]{1,0:T(8,128)(2,1)S(1)}, u32[]{:S(2)}, u32[]{:S(2)}) collective-permute-start(bf16[192,128]{1,0:T(8,128)(2,1)S(1)} %get-tuple-element.53), channel_id=1, source_target_pairs={{0,8},{8,0},{16,24},{24,16},{32,40},{40,32},{48,56},{56,48},{64,72... | collective-permute-start | bytes 147464 | tf_op jit(solution)/shard_map/ppermute | solution.py:635
  34.6 36.4 %all-to-all-start.1 = ((f32[64,1,128]{2,1,0:T(1,128)}), f32[64,1,128]{2,1,0:T(1,128)S(1)}, u32[]{:S(2)}, u32[]{:S(2)}) async-start(f32[64,1,128]{2,1,0:T(1,128)} %bitcast.11), calls=%async_computation.1 | async-start | bytes 65536 | tf_op jit(solution)/shard_map/all_to_all | solution.py:679
  57.8 5.0 %collective-permute-start.6 = (f32[48,128]{1,0:T(8,128)S(1)}, f32[48,128]{1,0:T(8,128)S(1)}, u32[]{:S(2)}, u32[]{:S(2)}) collective-permute-start(f32[48,128]{1,0:T(8,128)S(1)} %get-tuple-element.60), channel_id=1, source_target_pairs={{0,128},{128,0},{256,384},{384,256},{1,129},{129,1},{257,385},{385... | collective-permute-start | bytes 73736 | tf_op jit(solution)/shard_map/ppermute | solution.py:635
  60.7 2.0 %collective-permute-start.7 = (f32[48,128]{1,0:T(8,128)S(1)}, f32[48,128]{1,0:T(8,128)S(1)}, u32[]{:S(2)}, u32[]{:S(2)}) collective-permute-start(f32[48,128]{1,0:T(8,128)S(1)} %get-tuple-element.61), channel_id=1, source_target_pairs={{128,256},{256,128},{129,257},{257,129},{130,258},{258,130},{131,2... | collective-permute-start | bytes 73736 | tf_op jit(solution)/shard_map/ppermute | solution.py:640

commit v11 on v10

--- a/solution.py
+++ b/solution.py
@@ -676,7 +676,7 @@
     (to_face,) = call(
         functools.partial(sum_kernel, counts), "add", [(counts[0] * counts[1], NZL)], flops=10_000, moved=80_000,
     )(got_z)
-    got_face = lax.all_to_all(to_face, ("normal", "strike"), 0, 0, tiled=True)
+    got_face = lax.all_to_all(to_face, ("strike", "normal"), 0, 0, tiled=True)
     xa2, xb2 = swap_near(xa2, "normal"), swap_far(xb2, "normal")
     (share,) = call(final_kernel, "final", [(2, 3)], flops=10_000, moved=10_000)(got_face)
     following, mid = call(

time: 72 us -> 72.1 us (level)
  no operation moved by 1% of the time
where the time goes in v11:
time: 72.1 us; the launch traced here: 71.8 us
  starting transfers between devices  43.2 us (60%)
  waiting for transfers between devices  9.51 us (13%)
  Pallas kernels  9.27 us (13%)
  blocking collectives  8.98 us (12%)
  between operations  0.75 us (1%)
    all_to_all x1, starting transfers between devices, local(): got_face = lax.all_to_all(to_face, ('strike', 'normal'), 0, 0, tiled=True)  23.2 us
    ppermute x4, starting transfers between devices, swap_near(): lax.ppermute(value, axis, [(i, i ^ 1) for i in range(lax.axis_size(axis))])  16.1 us
    all_to_all x1, blocking collectives, local(): got_z = lax.all_to_all(to_depth, 'depth', 0, 0, tiled=True)  8.98 us
    all_to_all x1, waiting for transfers between devices, local(): got_face = lax.all_to_all(to_face, ('strike', 'normal'), 0, 0, tiled=True)  4.95 us
    ppermute x4, starting transfers between devices, swap_far(): lax.ppermute(value, axis, [(i, i + 1) for i in lower] + [(i + 1, i) for i...  3.91 us
    ppermute x4, waiting for transfers between devices, swap_near(): lax.ppermute(value, axis, [(i, i ^ 1) for i in range(lax.axis_size(axis))])  3.64 us
    pallas_call x1, Pallas kernels, local(): call(functools.partial(second_kernel, counts), 'second', [flat, flat], [f...  3.44 us
    pallas_call x1, Pallas kernels, local(): call(inner_kernel, 'inner', [flat, faces, block], [flat], flops=10000000,...  2.07 us
  transfers between devices with their start and end apart: 9, of which 4 were waited for; matrix products, arithmetic and copies ran while one was open for 0% of the time, Pallas kernels for 8%

profile of v11, /device:TPU:1, one launch (start us, length us, event | category | flops | bytes accessed | tf_op | source)
XLA Modules:
  0.0 71.8 jit_solution(10731727217637537785)
XLA Ops:
  0.6 1.3 %pack.1 = (f32[112,128]{1,0:T(8,128)S(1)}, f32[112,128]{1,0:T(8,128)S(1)}, f32[8,128]{1,0:T(8,128)S(1)}, f32[8,128]{1,0:T(8,128)S(1)}, f32[8,128]{1,0:T(8,128)S(...) custom-call(f32[3,128,128]{2,1,0:T(8,128)} %bitcast.18, ...), custom_call_target="tpu_custom_call" | custom-call | flops 2000000 | bytes 900000 | tf_op jit(solution)/shard_map/pack/pallas_call | solution.py:653
  2.0 4.4 %collective-permute-start = (f32[112,128]{1,0:T(8,128)S(1)}, f32[112,128]{1,0:T(8,128)S(1)}, u32[]{:S(2)}, u32[]{:S(2)}) collective-permute-start(f32[112,128]{1,0:T(8,128)S(1)} %get-tuple-element.45), channel_id=1, source_target_pairs={{0,128},{128,0},{256,384},{384,256},{1,129},{129,1},{257,385},{385... | collective-permute-start | bytes 172040 | tf_op jit(solution)/shard_map/ppermute | solution.py:635
  6.3 0.7 collective-permute-start.1
  7.0 6.3 %collective-permute-start.2 = (f32[8,128]{1,0:T(8,128)S(1)}, f32[8,128]{1,0:T(8,128)S(1)}, u32[]{:S(2)}, u32[]{:S(2)}) collective-permute-start(f32[8,128]{1,0:T(8,128)S(1)} %get-tuple-element.47), channel_id=1, source_target_pairs={{0,1},{1,0},{2,3},{3,2},{4,5},{5,4},{6,7},{7,6},{8,9},{9,8},{10,11... | collective-permute-start | bytes 12296 | tf_op jit(solution)/shard_map/ppermute | solution.py:635
  13.4 1.9 %collective-permute-start.3 = (f32[8,128]{1,0:T(8,128)S(1)}, f32[8,128]{1,0:T(8,128)S(1)}, u32[]{:S(2)}, u32[]{:S(2)}) collective-permute-start(f32[8,128]{1,0:T(8,128)S(1)} %get-tuple-element.48), channel_id=1, source_target_pairs={{1,2},{3,4},{5,6},{2,1},{4,3},{6,5},{9,10},{11,12},{13,14},{10,9},... | collective-permute-start | bytes 12296 | tf_op jit(solution)/shard_map/ppermute | solution.py:640
  15.3 2.1 %inner.1 = (f32[3,128,128]{2,1,0:T(8,128)S(1)}, f32[48,128]{1,0:T(8,128)S(1)}, f32[128,128]{1,0:T(8,128)S(1)}) custom-call(f32[3,128,128]{2,1,0:T(8,128)S(1)} %get-tuple-element.37.now.prev, f32[3,128,128]{2,1,0:T(8,128)S(1)} %get-tuple-element.38.prev, f32[128,128]{1,0:T(8,128)S(1)} %get-tuple-element.39.rw, bf16[128,128]{1,0:T(8,128)(2,1)S(1)} %get-tuple-element.40.rho), custom_call_target="tpu_custom_call" | custom-call | flops 10000000 | bytes 900000 | tf_op jit(solution)/shard_map/inner/pallas_call | solution.py:661
  17.4 0.0 collective-permute-done.2.za
  17.4 0.9 %collective-permute-done.3.zb = f32[8,128]{1,0:T(8,128)S(1)} collective-permute-done((f32[8,128]{1,0:T(8,128)S(1)}, f32[8,128]{1,0:T(8,128)S(1)}, u32[]{:S(2)}, u32[]{:S(2)}) %collective-permute-start.3) | collective-permute-done | bytes 4128 | tf_op jit(solution)/shard_map/ppermute | solution.py:640
  18.3 0.0 collective-permute-done.xa
  18.3 0.0 collective-permute-done.1.xb
  18.3 0.4 edge.1
  18.7 0.7 collective-permute-start.4
  19.4 2.5 %collective-permute-start.5 = (bf16[192,128]{1,0:T(8,128)(2,1)S(1)}, bf16[192,128]{1,0:T(8,128)(2,1)S(1)}, u32[]{:S(2)}, u32[]{:S(2)}) collective-permute-start(bf16[192,128]{1,0:T(8,128)(2,1)S(1)} %get-tuple-element.53), channel_id=1, source_target_pairs={{0,8},{8,0},{16,24},{24,16},{32,40},{40,32},{48,56},{56,48},{64,72... | collective-permute-start | bytes 147464 | tf_op jit(solution)/shard_map/ppermute | solution.py:635
  21.9 0.0 collective-permute-done.4.yb
  21.9 2.3 %collective-permute-done.5.ya = bf16[192,128]{1,0:T(8,128)(2,1)S(1)} collective-permute-done((bf16[192,128]{1,0:T(8,128)(2,1)S(1)}, bf16[192,128]{1,0:T(8,128)(2,1)S(1)}, u32[]{:S(2)}, u32[]{:S(2)}) %collective-permute-start.5) | collective-permute-done | bytes 49184 | tf_op jit(solution)/shard_map/ppermute | solution.py:635
  24.2 0.7 whole.1
  24.9 9.0 %all_to_all.22 = f32[8,8,128]{2,1,0:T(8,128)S(1)} all-to-all(f32[8,8,128]{2,1,0:T(8,128)S(1)} %bitcast.17), channel_id=1, replica_groups=mesh['normal'=4,'strike'=16,'depth'=8] {'depth'}, dimensions={0} | all-to-all | bytes 65536 | tf_op jit(solution)/shard_map/all_to_all | solution.py:675
  33.9 0.7 add.1
  34.6 23.2 %all-to-all-start.1 = ((f32[64,1,128]{2,1,0:T(1,128)}), f32[64,1,128]{2,1,0:T(1,128)S(1)}, u32[]{:S(2)}, u32[]{:S(2)}) async-start(f32[64,1,128]{2,1,0:T(1,128)} %bitcast.11), calls=%async_computation.1 | async-start | bytes 65536 | tf_op jit(solution)/shard_map/all_to_all | solution.py:679
  57.8 2.9 %collective-permute-start.6 = (f32[48,128]{1,0:T(8,128)S(1)}, f32[48,128]{1,0:T(8,128)S(1)}, u32[]{:S(2)}, u32[]{:S(2)}) collective-permute-start(f32[48,128]{1,0:T(8,128)S(1)} %get-tuple-element.60), channel_id=1, source_target_pairs={{0,128},{128,0},{256,384},{384,256},{1,129},{129,1},{257,385},{385... | collective-permute-start | bytes 73736 | tf_op jit(solution)/shard_map/ppermute | solution.py:635
  60.7 0.7 collective-permute-start.7
  61.4 1.3 %collective-permute-done.6.xa2 = f32[48,128]{1,0:T(8,128)S(1)} collective-permute-done((f32[48,128]{1,0:T(8,128)S(1)}, f32[48,128]{1,0:T(8,128)S(1)}, u32[]{:S(2)}, u32[]{:S(2)}) %collective-permute-start.6) | collective-permute-done | bytes 24608 | tf_op jit(solution)/shard_map/ppermute | solution.py:635
  62.7 0.0 collective-permute-done.7.xb2
  62.7 3.4 %second.1 = (f32[3,128,128]{2,1,0:T(8,128)}, f32[3,128,128]{2,1,0:T(8,128)}) custom-call(f32[3,128,128]{2,1,0:T(8,128)S(1)} %get-tuple-element.59.now, f32[3,128,128]{2,1,0:T(8,128)S(1)} %get-tuple-element.37.now.prev, f32[128,128]{1,0:T(8,128)S(1)} %get-tuple-element.39.rw, f32[128,128]{1,0:T(8,128)S(1)} %get-tuple-element.42.scale, ...), custom_call_target="tpu_custom_call" | custom-call | flops 10000000 | bytes 900000 | tf_op jit(solution)/shard_map/second/pallas_call | solution.py:682
  66.1 5.0 %all-to-all-done.1 = f32[64,1,128]{2,1,0:T(1,128)S(1)} async-done(((f32[64,1,128]{2,1,0:T(1,128)}), f32[64,1,128]{2,1,0:T(1,128)S(1)}, u32[]{:S(2)}, u32[]{:S(2)}) %all-to-all-start.1) | async-done | bytes 32800 | tf_op jit(solution)/shard_map/all_to_all | solution.py:679
  71.1 0.7 final.1
Async XLA Ops:
  2.0 16.3 %collective-permute-start = (f32[112,128]{1,0:T(8,128)S(1)}, f32[112,128]{1,0:T(8,128)S(1)}, u32[]{:S(2)}, u32[]{:S(2)}) collective-permute-start(f32[112,128]{1,0:T(8,128)S(1)} %get-tuple-element.45), channel_id=1, source_target_pairs={{0,128},{128,0},{256,384},{384,256},{1,129},{129,1},{257,385},{385... | collective-permute-start | bytes 172040 | tf_op jit(solution)/shard_map/ppermute | solution.py:635
  6.3 11.9 %collective-permute-start.1 = (f32[112,128]{1,0:T(8,128)S(1)}, f32[112,128]{1,0:T(8,128)S(1)}, u32[]{:S(2)}, u32[]{:S(2)}) collective-permute-start(f32[112,128]{1,0:T(8,128)S(1)} %get-tuple-element.46), channel_id=1, source_target_pairs={{128,256},{256,128},{129,257},{257,129},{130,258},{258,130},{131,2... | collective-permute-start | bytes 172040 | tf_op jit(solution)/shard_map/ppermute | solution.py:640
  7.0 10.4 %collective-permute-start.2 = (f32[8,128]{1,0:T(8,128)S(1)}, f32[8,128]{1,0:T(8,128)S(1)}, u32[]{:S(2)}, u32[]{:S(2)}) collective-permute-start(f32[8,128]{1,0:T(8,128)S(1)} %get-tuple-element.47), channel_id=1, source_target_pairs={{0,1},{1,0},{2,3},{3,2},{4,5},{5,4},{6,7},{7,6},{8,9},{9,8},{10,11... | collective-permute-start | bytes 12296 | tf_op jit(solution)/shard_map/ppermute | solution.py:635
  13.4 4.9 %collective-permute-start.3 = (f32[8,128]{1,0:T(8,128)S(1)}, f32[8,128]{1,0:T(8,128)S(1)}, u32[]{:S(2)}, u32[]{:S(2)}) collective-permute-start(f32[8,128]{1,0:T(8,128)S(1)} %get-tuple-element.48), channel_id=1, source_target_pairs={{1,2},{3,4},{5,6},{2,1},{4,3},{6,5},{9,10},{11,12},{13,14},{10,9},... | collective-permute-start | bytes 12296 | tf_op jit(solution)/shard_map/ppermute | solution.py:640
  18.7 3.2 %collective-permute-start.4 = (bf16[192,128]{1,0:T(8,128)(2,1)S(1)}, bf16[192,128]{1,0:T(8,128)(2,1)S(1)}, u32[]{:S(2)}, u32[]{:S(2)}) collective-permute-start(bf16[192,128]{1,0:T(8,128)(2,1)S(1)} %get-tuple-element.52), channel_id=1, source_target_pairs={{8,16},{24,32},{40,48},{56,64},{72,80},{88,96},{104,112},{16,8},{3... | collective-permute-start | bytes 147464 | tf_op jit(solution)/shard_map/ppermute | solution.py:640
  19.4 4.8 %collective-permute-start.5 = (bf16[192,128]{1,0:T(8,128)(2,1)S(1)}, bf16[192,128]{1,0:T(8,128)(2,1)S(1)}, u32[]{:S(2)}, u32[]{:S(2)}) collective-permute-start(bf16[192,128]{1,0:T(8,128)(2,1)S(1)} %get-tuple-element.53), channel_id=1, source_target_pairs={{0,8},{8,0},{16,24},{24,16},{32,40},{40,32},{48,56},{56,48},{64,72... | collective-permute-start | bytes 147464 | tf_op jit(solution)/shard_map/ppermute | solution.py:635
  34.6 36.5 %all-to-all-start.1 = ((f32[64,1,128]{2,1,0:T(1,128)}), f32[64,1,128]{2,1,0:T(1,128)S(1)}, u32[]{:S(2)}, u32[]{:S(2)}) async-start(f32[64,1,128]{2,1,0:T(1,128)} %bitcast.11), calls=%async_computation.1 | async-start | bytes 65536 | tf_op jit(solution)/shard_map/all_to_all | solution.py:679
  57.8 4.9 %collective-permute-start.6 = (f32[48,128]{1,0:T(8,128)S(1)}, f32[48,128]{1,0:T(8,128)S(1)}, u32[]{:S(2)}, u32[]{:S(2)}) collective-permute-start(f32[48,128]{1,0:T(8,128)S(1)} %get-tuple-element.60), channel_id=1, source_target_pairs={{0,128},{128,0},{256,384},{384,256},{1,129},{129,1},{257,385},{385... | collective-permute-start | bytes 73736 | tf_op jit(solution)/shard_map/ppermute | solution.py:635
  60.7 2.0 %collective-permute-start.7 = (f32[48,128]{1,0:T(8,128)S(1)}, f32[48,128]{1,0:T(8,128)S(1)}, u32[]{:S(2)}, u32[]{:S(2)}) collective-permute-start(f32[48,128]{1,0:T(8,128)S(1)} %get-tuple-element.61), channel_id=1, source_target_pairs={{128,256},{256,128},{129,257},{257,129},{130,258},{258,130},{131,2... | collective-permute-start | bytes 73736 | tf_op jit(solution)/shard_map/ppermute | solution.py:640
